TPU v7x, 256 devices: a whole 4x4x8 slice. The times are simulated.
256 devices in a mesh: inst: 16 (over z, x_hi), tp: 16 (over x_lo, y, core).
Axes of the slice: x: 4 (x_hi: 2, x_lo: 2; x = x_hi * 2 + x_lo), y: 4, z: 8, core: 2. Of those that a mesh axis runs over, the one named last changes fastest.
Arguments:
- query: bfloat16 [2, 768, 4096], P(None, 'inst', 'tp'), may hold values from -200 to 200
- new_kv: bfloat16 [2, 768, 2, 1024], P(None, 'inst'), may hold values from -7 to 7
- residual: bfloat16 [2, 768, 8192], P(None, 'inst', 'tp'), may hold values from -60 to 60
- kv_pages: bfloat16 [2304, 2, 16, 128, 128], P('inst', None, 'tp'), may hold values from -6 to 6, as said below
- block_table: int32 [768, 3], P('inst'), may hold values from 0 to 143, as said below
- blocks: int32 [768], P('inst'), may hold values from 1 to 3
- moves: int32 [16, 16], P('inst'), may hold values from 0 to 47, as said below
- out_weight: bfloat16 [4096, 8192], P('tp'), may hold values from -0.5 to 0.5
- norm_gain: bfloat16 [8192], replicated, may hold values from 0.5 to 1.5
Outputs:
- hidden_out: bfloat16 [2, 768, 8192], P(None, 'inst', 'tp')
- normed: bfloat16 [2, 768, 8192], P(None, 'inst')
- arrived_pages: bfloat16 [256, 3, 2, 16, 128, 128], P('inst', None, None, 'tp')
- arrived_tail: bfloat16 [256, 2, 2, 16, 128], P('inst', None, None, 'tp')
Inputs may be any that keep to these rules, and one draw needn't show every extreme that they name: `kv_pages`: stored heads a and a2 hold the same numbers whenever a // 2 equals a2 // 2. `block_table`: the 48 x 3 entries of one instance's rows are different pages of its pool. `moves`: the 16 slots in each row are different.
All inputs are finite; a program needn't handle non-finite values.
Results may differ from a plain program's by a relative error of at most 0.0054.
Values may be sent and summed in bfloat16 or wider, within the bound.
No kernel may reach another device: no remote copies, remote signals or barrier semaphores. Data moves between devices by JAX's collectives and lax.ppermute only.
A program may use at most 128 MiB of HBM per device.

v0:
```python
import jax
import jax.numpy as jnp
from jax import lax
from jax.sharding import PartitionSpec as P

KVH = 8


epsilon = 1e-05
masked_score = -1e30


def local(query, new_kv, residual, kv_pages, block_table, blocks, moves, out_weight, norm_gain):
    tp_count = lax.axis_size("tp")
    tp_index = lax.axis_index("tp")
    step_count, slot_count, columns = query.shape
    stored = kv_pages.shape[2]
    page_len = kv_pages.shape[3]
    head_width = kv_pages.shape[4]
    block_count = block_table.shape[1]
    group_size = columns // (stored * head_width)
    copies = max(1, tp_count // KVH)
    kv_first = tp_index * stored // copies
    fresh_all = new_kv.reshape(step_count, slot_count, 2, KVH, head_width)
    fresh_rows = lax.dynamic_slice_in_dim(fresh_all, kv_first, stored, 3)
    cached = jnp.take(kv_pages, block_table.reshape(-1), axis=0)
    cached = cached.reshape(slot_count, block_count, 2, stored, page_len, head_width)
    queries = query.reshape(step_count, slot_count, stored, group_size, head_width)
    scaling = head_width ** (-0.5)
    cache_scores = (
        jnp.einsum(
            "tsagd,sbapd->tsagbp", queries, cached[:, :, 0], preferred_element_type=jnp.float32
        )
        * scaling
    )
    cache_scores = cache_scores.reshape(
        step_count, slot_count, stored, group_size, block_count * page_len
    )
    valid = (jnp.arange(block_count * page_len) // page_len)[None, :] < blocks[:, None]
    cache_scores = jnp.where(valid[None, :, None, None, :], cache_scores, masked_score)
    fresh_scores = (
        jnp.einsum(
            "tsagd,usad->tsagu", queries, fresh_rows[:, :, 0], preferred_element_type=jnp.float32
        )
        * scaling
    )
    causal = jnp.arange(step_count)[None, :] <= jnp.arange(step_count)[:, None]
    fresh_scores = jnp.where(causal[:, None, None, None, :], fresh_scores, masked_score)
    scores = jnp.concatenate([cache_scores, fresh_scores], axis=-1)
    highest = jnp.max(scores, axis=-1, keepdims=True)
    expanded = jnp.exp(scores - highest)
    weights = (expanded / jnp.sum(expanded, axis=-1, keepdims=True)).astype(jnp.bfloat16)
    cache_weights = weights[..., : block_count * page_len].reshape(
        step_count, slot_count, stored, group_size, block_count, page_len
    )
    mixed = jnp.einsum(
        "tsagbp,sbapd->tsagd", cache_weights, cached[:, :, 1], preferred_element_type=jnp.float32
    )
    mixed = mixed + jnp.einsum(
        "tsagu,usad->tsagd",
        weights[..., block_count * page_len :],
        fresh_rows[:, :, 1],
        preferred_element_type=jnp.float32,
    )
    heads = mixed.astype(jnp.bfloat16).reshape(step_count * slot_count, columns)
    model_width = out_weight.shape[1]
    share = model_width // tp_count
    partial_sums = jnp.dot(heads, out_weight, preferred_element_type=jnp.float32)
    total = lax.psum(partial_sums, "tp")
    full_residual = lax.all_gather(residual, "tp", axis=2, tiled=True)
    hidden_full = (
        full_residual.astype(jnp.float32) + total.reshape(step_count, slot_count, model_width)
    ).astype(jnp.bfloat16)
    hidden_wide = lax.optimization_barrier(hidden_full).astype(jnp.float32)
    mean_square = jnp.mean(hidden_wide * hidden_wide, axis=-1, keepdims=True)
    normed = (
        hidden_wide * lax.rsqrt(mean_square + epsilon) * norm_gain.astype(jnp.float32)
    ).astype(jnp.bfloat16)
    hidden_out = lax.dynamic_slice_in_dim(hidden_full, tp_index * share, share, 2)
    chosen = moves[0]
    page_ids = jnp.take(block_table, chosen, axis=0)
    keep = jnp.arange(block_count)[None, :] < jnp.take(blocks, chosen)[:, None]
    outgoing = jnp.take(kv_pages, page_ids.reshape(-1), axis=0)
    outgoing = outgoing.reshape(chosen.shape[0], block_count, 2, stored, page_len, head_width)
    outgoing = jnp.where(
        keep[:, :, None, None, None, None], outgoing, jnp.zeros((), outgoing.dtype)
    )
    tail_rows = jnp.take(fresh_rows, chosen, axis=1).transpose(1, 0, 2, 3, 4)
    arrived, tail_in = (
        lax.all_to_all(outgoing, "inst", split_axis=0, concat_axis=0, tiled=True),
        lax.all_to_all(tail_rows, "inst", split_axis=0, concat_axis=0, tiled=True),
    )
    return (hidden_out, normed, arrived, tail_in)


def solution(mesh):
    in_specs = (
        P(None, "inst", "tp"),
        P(None, "inst", None, None),
        P(None, "inst", "tp"),
        P("inst", None, "tp", None, None),
        P("inst", None),
        P("inst"),
        P("inst", None),
        P("tp", None),
        P(),
    )
    out_specs = (
        P(None, "inst", "tp"),
        P(None, "inst", None),
        P("inst", None, None, "tp", None, None),
        P("inst", None, None, "tp", None),
    )
    return jax.shard_map(local, mesh=mesh, in_specs=in_specs, out_specs=out_specs, check_vma=False)
```

profile of v0, /device:TPU:1, one launch (start us, length us, event | category | flops | bytes accessed | tf_op | source)
XLA Modules:
  0.0 222.6 jit_solution(5446171204302299595)
XLA Ops:
  7.2 0.7 all-gather.2.cloned.1.call-update
  7.9 0.8 copy.45
  8.7 0.7 compare_and_fusion.2
  9.6 10.9 %gather_fusion = bf16[144,2,128,128]{3,2,1,0:T(8,128)(2,1)} fusion(bf16[144,2,128,128]{3,2,1,0:T(8,128)(2,1)} %bitcast.106, s32[1024]{0:T(1024)S(1)} %pad_clamp_fusion.2), kind=kCustom, calls=%fused_computation | custom fusion | bytes 18874944 | tf_op jit(solution)/shard_map/jit(_take)/gather | solution.py:26
  20.5 11.6 %copy.46 = bf16[144,2,128,128]{3,2,0,1:T(8,128)(2,1)} copy(bf16[144,2,128,128]{3,2,1,0:T(8,128)(2,1)} %gather_fusion) | data formatting | bytes 18874368 | tf_op jit(solution)/shard_map/jit(_take)/gather | solution.py:26
  32.3 0.3 reshape.466
  32.5 8.3 %broadcast_select_fusion = bf16[48,3,2,1,128,128]{5,4,1,0,3,2:T(8,128)(2,1)} fusion(bf16[48,3,2,1,128,128]{5,4,1,0,3,2:T(8,128)(2,1)} %bitcast.105, pred[48,3]{1,0:T(8,128)(4,1)S(1)} %copy.44), kind=kLoop, calls=%fused_computation.5 | loop fusion | flops 4718592 | bytes 18874512 | tf_op jit(solution)/shard_map/jit(_take)/select_n | solution.py:26
  41.0 4.2 %select_reduce_fusion = (f32[2,48,2]{2,0,1:T(2,128)S(1)}, f32[2,48,1,2,3,128]{5,3,0,4,1,2:T(2,128)S(1)}) fusion(pred[48,3,128]{2,1,0:T(4,128)(4,1)S(1)} %broadcast_compare_fusion, bf16[48,3,2,1,128,128]{5,4,1,0,3,2:T(8,128)(2,1)} %broadcast_select_fusion, bf16[2,48,2,128]{3,2,1,0:T(2,128)(2,1)S(1)} %reshape.402), kind=kOutput, calls=%fused_computation.29 | convolution fusion | flops 19095360 | bytes 5081856 | tf_op jit(solution)/shard_map/tsagd,sbapd->tsagbp/dot_general | solution.py:31
  45.4 0.3 reshape.465
  45.8 0.4 fusion.26
  46.2 0.2 select_bitcast_fusion
  46.5 0.5 fusion.25
  47.0 0.4 divide_convert_fusion
  47.4 3.4 %fusion.7 = f32[48,128,2,2]{1,3,2,0:T(2,128)S(1)} fusion(bf16[48,3,2,1,128,128]{5,4,1,0,3,2:T(8,128)(2,1)} %broadcast_select_fusion, bf16[2,48,1,2,386]{4,3,0,1,2:T(2,128)(2,1)S(1)} %divide_convert_fusion), kind=kOutput, calls=%fused_computation.19 | convolution fusion | flops 18874368 | bytes 4964352 | tf_op jit(solution)/shard_map/tsagbp,sbapd->tsagd/dot_general | solution.py:56
  51.1 2.5 %fusion.13 = f32[96,8192]{1,0:T(8,128)} fusion(bf16[256,8192]{1,0:T(8,128)(2,1)S(1)} %copy-done.1, bf16[12,8,2,128]{3,2,1,0:T(2,128)(2,1)S(1)} %bitcast.110), kind=kOutput, calls=%fused_computation.32 | convolution fusion | flops 402653184 | bytes 7389184 | tf_op jit(solution)/shard_map/dot_general | solution.py:68
  53.6 0.6 copy-done.5
  54.3 0.7 gather_fusion.1
  55.1 0.6 gather_fusion.4
  55.7 0.7 fusion.18
  56.4 11.6 %all-to-all-start.1 = ((bf16[16,2,2,1,128]{4,2,1,3,0:T(2,128)(2,1)}), bf16[16,2,2,1,128]{4,2,1,3,0:T(2,128)(2,1)S(1)}, u32[]{:S(2)}, u32[]{:S(2)}) async-start(bf16[16,2,2,1,128]{4,2,1,3,0:T(2,128)(2,1)} %fusion.18), calls=%async_computation.1 | async-start | bytes 32768 | tf_op jit(solution)/shard_map/all_to_all | solution.py:91
  68.0 0.6 gather_fusion.2
  68.8 4.9 %gather_fusion.3 = bf16[48,2,128,128]{3,2,1,0:T(8,128)(2,1)S(1)} fusion(bf16[144,2,128,128]{3,2,1,0:T(8,128)(2,1)} %bitcast.107, s32[1024]{0:T(1024)S(1)} %pad_clamp_fusion), kind=kCustom, calls=%fused_computation.3 | custom fusion | bytes 6291648 | tf_op jit(solution)/shard_map/jit(_take)/gather | solution.py:83
  73.7 2.1 select_select_fusion
  75.8 1.1 all-to-all-done.1
  76.9 8.1 %all-to-all-start = ((bf16[16,3,2,1,128,128]{5,4,3,2,1,0:T(8,128)(2,1)}), bf16[16,3,2,1,128,128]{5,4,3,2,1,0:T(8,128)(2,1)S(1)}, u32[]{:S(2)}, u32[]{:S(2)}) async-start(bf16[16,3,2,1,128,128]{5,4,3,2,1,0:T(8,128)(2,1)} %select_select_fusion), calls=%async_computation | async-start | bytes 6291456 | tf_op jit(solution)/shard_map/all_to_all | solution.py:90
  85.1 123.0 %all-reduce.2.cloned.1.call-done = f32[2,48,8192]{2,1,0:T(8,128)} async-done(((f32[2,48,8192]{2,1,0:T(8,128)}), f32[2,48,8192]{2,1,0:T(8,128)}) %all-reduce.2.cloned.1.call-update) | async-done | bytes 3145744 | tf_op jit(solution)/shard_map/psum | solution.py:69
  208.1 2.7 %add_convert_fusion = bf16[2,48,8192]{2,1,0:T(8,128)(2,1)S(1)} fusion(f32[2,48,8192]{2,1,0:T(8,128)} %all-reduce.2.cloned.1.call-done, bf16[2,48,8192]{2,1,0:T(8,128)(2,1)} %all-gather.2.cloned.1.call-done), kind=kLoop, calls=%fused_computation.16 | loop fusion | flops 2359296 | bytes 6291456 | tf_op jit(solution)/shard_map/convert_element_type | solution.py:73
  210.8 0.7 constant_dynamic-slice_fusion.2
  211.5 0.4 fusion.2
  211.9 1.6 fusion.4
  213.5 1.7 copy.101
  215.2 0.6 copy.102
  (42 shorter events, 1.4 us)
Async XLA Ops:
  7.2 77.9 %all-gather.2.cloned.1.call-start = ((), (), s32[]{:S(2)}) async-start(), calls=%async_computation.2 | async-start | bytes 1671168 | tf_op jit(solution)/shard_map/all_gather | solution.py:70
  7.9 200.2 %all-reduce.2.cloned.1.call-start = ((), (), s32[]{:S(2)}) async-start(), calls=%async_computation.3 | async-start | bytes 6291456 | tf_op jit(solution)/shard_map/psum | solution.py:69
  20.5 11.7 %copy-start.3 = (bf16[2,48,256]{2,1,0:T(8,128)(2,1)S(1)}, bf16[2,48,256]{2,1,0:T(8,128)(2,1)}, u32[]{:S(2)}) copy-start(bf16[2,48,256]{2,1,0:T(8,128)(2,1)} %param.9) | copy-start | bytes 147460
  20.5 11.8 %copy-start.2 = (bf16[2,48,2,1024]{3,2,1,0:T(2,128)(2,1)S(1)}, bf16[2,48,2,1024]{3,2,1,0:T(2,128)(2,1)}, u32[]{:S(2)}) copy-start(bf16[2,48,2,1024]{3,2,1,0:T(2,128)(2,1)} %param.10) | copy-start | bytes 1179652
  32.5 8.3 %copy-start = (s32[48]{0:T(128)S(1)}, s32[48]{0:T(128)}, u32[]{:S(2)}) copy-start(s32[48]{0:T(128)} %param.14) | copy-start | bytes 580
  47.4 3.7 %copy-start.1 = (bf16[256,8192]{1,0:T(8,128)(2,1)S(1)}, bf16[256,8192]{1,0:T(8,128)(2,1)}, u32[]{:S(2)}) copy-start(bf16[256,8192]{1,0:T(8,128)(2,1)} %param.16) | copy-start | bytes 12582916
  53.6 0.7 copy-start.5
  56.4 20.5 %all-to-all-start.1 = ((bf16[16,2,2,1,128]{4,2,1,3,0:T(2,128)(2,1)}), bf16[16,2,2,1,128]{4,2,1,3,0:T(2,128)(2,1)S(1)}, u32[]{:S(2)}, u32[]{:S(2)}) async-start(bf16[16,2,2,1,128]{4,2,1,3,0:T(2,128)(2,1)} %fusion.18), calls=%async_computation.1 | async-start | bytes 32768 | tf_op jit(solution)/shard_map/all_to_all | solution.py:91
  75.8 9.3 %copy-start.4 = (bf16[8192]{0:T(1024)(128)(2,1)S(1)}, bf16[8192]{0:T(1024)(128)(2,1)}, u32[]{:S(2)}) copy-start(bf16[8192]{0:T(1024)(128)(2,1)} %param.17) | copy-start | bytes 49156
  76.9 136.6 %all-to-all-start = ((bf16[16,3,2,1,128,128]{5,4,3,2,1,0:T(8,128)(2,1)}), bf16[16,3,2,1,128,128]{5,4,3,2,1,0:T(8,128)(2,1)S(1)}, u32[]{:S(2)}, u32[]{:S(2)}) async-start(bf16[16,3,2,1,128,128]{5,4,3,2,1,0:T(8,128)(2,1)} %select_select_fusion), calls=%async_computation | async-start | bytes 6291456 | tf_op jit(solution)/shard_map/all_to_all | solution.py:90
Sparse Core Ops, SparseCore 0:
  9.8 39.8 all-gather.1
  53.7 154.3 all-reduce.1
where the time goes:
time: 224 us; the launch traced here: 223 us
  waiting for transfers between devices  125 us (56%)
  local copies, waits for them, and re-layouts  34.8 us (16%)
  starting transfers between devices  19.8 us (9%)
  other arithmetic  18.1 us (8%)
  between operations  14.3 us (6%)
  matrix products  10.7 us (5%)
    psum x1, waiting for transfers between devices, local(): total = lax.psum(partial_sums, 'tp')  123 us
    gather x2, local copies, waits for them, and re-layouts, local(): cached = jnp.take(kv_pages, block_table.reshape(-1), axis=0)  22.5 us
    all_to_all x1, starting transfers between devices, local(): lax.all_to_all(tail_rows, 'inst', split_axis=0, concat_axis=0, tiled=True)  11.6 us
    select_n x2, other arithmetic, local(): cached = jnp.take(kv_pages, block_table.reshape(-1), axis=0)  8.32 us
    all_to_all x1, starting transfers between devices, local(): lax.all_to_all(outgoing, 'inst', split_axis=0, concat_axis=0, tiled=True)  8.13 us
    gather x1, local copies, waits for them, and re-layouts, local(): outgoing = jnp.take(kv_pages, page_ids.reshape(-1), axis=0)  4.87 us
  transfers between devices with their start and end apart: 4, of which 2 were waited for; matrix products, arithmetic and copies ran while one was open for 27% of the time, Pallas kernels for 0%

commit v1 on v0

v1 whole, which is shorter than its diff:
```python
import functools

import jax
import jax.numpy as jnp
from jax import lax
from jax.experimental import pallas as pl
from jax.experimental.pallas import tpu as pltpu
from jax.sharding import PartitionSpec as P

F32 = jnp.float32
BF16 = jnp.bfloat16
EPSILON = 1e-05
MASKED = -1e30

SLOTS = 48
MAXB = 3
PAGE = 128
HD = 128
STEPS = 2
INST = 16
CHIPS = 8
ROWS = STEPS * SLOTS
D = 8192
SHARE = 512
PAGES = SLOTS * MAXB
TOK = MAXB * PAGE
MSG = TOK + 16
SHIFTS = [(dx, dy) for dx in range(2) for dy in range(4)]


def any_spec():
    return pl.BlockSpec(memory_space=pl.ANY)


def smem_spec():
    return pl.BlockSpec(memory_space=pltpu.SMEM)


def vmem_spec():
    return pl.BlockSpec(memory_space=pltpu.VMEM)


def pack_kernel(tbl, blk, mv, nkv, kv, out, zeros, fresh, stage32, stage, sems, fsem, ssem):
    tp = lax.axis_index("tp")
    core = lax.rem(tp, 2)
    head = lax.div(tp, 2)
    fcopy = pltpu.make_async_copy(
        nkv.at[:, :, :, pl.ds(pl.multiple_of(head * HD, HD), HD)], fresh, fsem
    )
    fcopy.start()
    zeros[...] = jnp.zeros_like(zeros)
    for j in range(INST):
        m = mv[0, j]
        for b in range(MAXB):
            dst = out.at[j, pl.ds(b * PAGE, PAGE)]
            sem = sems.at[j * MAXB + b]
            valid = b < blk[m]

            @pl.when(valid)
            def _():
                pltpu.make_async_copy(kv.at[tbl[m, b], core, 0], dst, sem).start()

            @pl.when(jnp.logical_not(valid))
            def _():
                pltpu.make_async_copy(zeros, dst, sem).start()

    stage32[...] = jnp.zeros_like(stage32)
    fcopy.wait()
    for j in range(INST):
        m = mv[0, j]
        stage32[j, 0:2] = fresh[0, m].astype(F32)
        stage32[j, 2:4] = fresh[1, m].astype(F32)
    stage[...] = stage32[...].astype(BF16)
    scopy = pltpu.make_async_copy(stage, out.at[:, pl.ds(TOK, 16)], ssem)
    scopy.start()
    for j in range(INST):
        for b in range(MAXB):
            pltpu.make_async_copy(
                zeros, out.at[j, pl.ds(b * PAGE, PAGE)], sems.at[j * MAXB + b]
            ).wait()
    scopy.wait()


def pack(block_table, blocks, moves, new_kv, kv_pages):
    return pl.pallas_call(
        pack_kernel,
        out_shape=jax.ShapeDtypeStruct((INST, MSG, HD), BF16),
        in_specs=[smem_spec()] * 3 + [any_spec()] * 2,
        out_specs=any_spec(),
        scratch_shapes=[
            pltpu.VMEM((PAGE, HD), BF16),
            pltpu.VMEM((STEPS, SLOTS, 2, HD), BF16),
            pltpu.VMEM((INST, 16, HD), F32),
            pltpu.VMEM((INST, 16, HD), BF16),
            pltpu.SemaphoreType.DMA((INST * MAXB,)),
            pltpu.SemaphoreType.DMA,
            pltpu.SemaphoreType.DMA,
        ],
        compiler_params=pltpu.CompilerParams(vmem_limit_bytes=8 << 20),
        cost_estimate=pl.CostEstimate(flops=0, bytes_accessed=4 << 20, transcendentals=0),
        name="pack",
    )(block_table, blocks, moves, new_kv, kv_pages)


def attend_kernel(tbl, blk, q, nkv, kv, w, send, keep, kvb, wb, fresh, qs, ks, sc, ob, sbuf, kbuf,
                  kvsem, wsem, fsem, osem):
    tp = lax.axis_index("tp")
    core = lax.rem(tp, 2)
    chip = lax.div(tp, 2)
    x = lax.div(chip, 4)
    y = lax.rem(chip, 4)
    fcopy = pltpu.make_async_copy(
        nkv.at[:, :, :, pl.ds(pl.multiple_of(chip * HD, HD), HD)], fresh, fsem
    )
    fcopy.start()

    def page_copy(s, b):
        return pltpu.make_async_copy(kv.at[tbl[s, b], :, 0], kvb.at[s * MAXB + b], kvsem.at[s * MAXB + b])

    def start_slot(s, carry):
        for b in range(MAXB):
            valid = b < blk[s]

            @pl.when(valid)
            def _():
                page_copy(s, b).start()

            @pl.when(jnp.logical_not(valid))
            def _():
                kvb[s * MAXB + b, 1] = jnp.zeros((PAGE, HD), BF16)
        return carry

    lax.fori_loop(0, SLOTS, start_slot, 0)

    def owner(k):
        dx, dy = SHIFTS[k % CHIPS]
        other = lax.rem(x + dx, 2) * 4 + lax.rem(y + dy, 4)
        return other * 2 + (1 - core if k < CHIPS else core)

    def w_copy(k):
        return pltpu.make_async_copy(
            w.at[:, pl.ds(pl.multiple_of(owner(k) * SHARE, SHARE), SHARE)], wb.at[k], wsem.at[k]
        )

    for k in range(2 * CHIPS):
        w_copy(k).start()

    for t in range(STEPS):
        for g in range(2):
            qs[pl.ds(t * 2 + g, SLOTS, stride=4), :] = q[t, :, g * HD:(g + 1) * HD].astype(F32)
    fcopy.wait()
    fr = fresh[...].astype(F32)
    for u in range(STEPS):
        for c in range(2):
            val = fr[u, :, c, :]
            for j in range(4):
                ks[u * 2 + c, pl.ds(j, SLOTS, stride=4), :] = val

    scaling = HD ** (-0.5)
    row_a = lax.broadcasted_iota(jnp.int32, (8, TOK), 0) < 4
    block_of = lax.div(lax.broadcasted_iota(jnp.int32, (8, TOK), 1), PAGE)

    def wait_slot(s):
        for b in range(MAXB):
            @pl.when(b < blk[s])
            def _():
                page_copy(s, b).wait()

    def score_pair(p, carry):
        wait_slot(2 * p)
        wait_slot(2 * p + 1)
        rows = pl.ds(pl.multiple_of(p * 8, 8), 8)
        q8 = qs[rows, :].astype(BF16)
        parts = []
        for h in range(2):
            keys = kvb[pl.ds((2 * p + h) * MAXB, MAXB), 0].reshape(TOK, HD)
            parts.append(lax.dot_general(q8, keys, (((1,), (1,)), ((), ())), preferred_element_type=F32))
        s8 = jnp.where(row_a, parts[0], parts[1]) * scaling
        count = jnp.where(row_a, blk[2 * p], blk[2 * p + 1])
        sc[rows, :] = jnp.where(block_of < count, s8, MASKED)
        return carry

    lax.fori_loop(0, SLOTS // 2, score_pair, 0)

    qa = qs[...]
    f0 = jnp.sum(qa * ks[0], axis=-1, keepdims=True) * scaling
    f1 = jnp.sum(qa * ks[2], axis=-1, keepdims=True) * scaling
    late = lax.rem(lax.broadcasted_iota(jnp.int32, (SLOTS * 4, 1), 0), 4) >= 2
    f1 = jnp.where(late, f1, MASKED)
    s = sc[...]
    top = jnp.maximum(jnp.max(s, axis=-1, keepdims=True), jnp.maximum(f0, f1))
    e = jnp.exp(s - top)
    e0 = jnp.exp(f0 - top)
    e1 = jnp.exp(f1 - top)
    total = jnp.sum(e, axis=-1, keepdims=True) + e0 + e1
    sc[...] = e / total
    w0 = (e0 / total).astype(BF16).astype(F32)
    w1 = (e1 / total).astype(BF16).astype(F32)
    ob[...] = w0 * ks[1] + w1 * ks[3]
    row_o = lax.broadcasted_iota(jnp.int32, (8, HD), 0) < 4

    def mix_pair(p, carry):
        rows = pl.ds(pl.multiple_of(p * 8, 8), 8)
        w8 = sc[rows, :].astype(BF16)
        parts = []
        for h in range(2):
            vals = kvb[pl.ds((2 * p + h) * MAXB, MAXB), 1].reshape(TOK, HD)
            parts.append(jnp.dot(w8, vals, preferred_element_type=F32))
        ob[rows, :] += jnp.where(row_o, parts[0], parts[1])
        return carry

    lax.fori_loop(0, SLOTS // 2, mix_pair, 0)

    heads = jnp.concatenate(
        [
            jnp.concatenate([ob[pl.ds(t * 2 + g, SLOTS, stride=4), :] for g in range(2)], axis=1)
            for t in range(STEPS)
        ],
        axis=0,
    ).astype(BF16)

    outs = []
    for k in range(2 * CHIPS):
        w_copy(k).wait()
        part = jnp.dot(heads, wb[k], preferred_element_type=F32)
        i = k % CHIPS
        if k < CHIPS:
            sbuf[i] = part.astype(BF16)
            copy = pltpu.make_async_copy(sbuf.at[i], send.at[i], osem.at[k])
        else:
            kbuf[i] = part
            copy = pltpu.make_async_copy(kbuf.at[i], keep.at[i], osem.at[k])
        copy.start()
        outs.append(copy)
    for copy in outs:
        copy.wait()


def attend(block_table, blocks, query, new_kv, kv_pages, out_weight):
    return pl.pallas_call(
        attend_kernel,
        out_shape=(
            jax.ShapeDtypeStruct((CHIPS, ROWS, SHARE), BF16),
            jax.ShapeDtypeStruct((CHIPS, ROWS, SHARE), F32),
        ),
        in_specs=[smem_spec()] * 2 + [vmem_spec()] + [any_spec()] * 3,
        out_specs=(any_spec(), any_spec()),
        scratch_shapes=[
            pltpu.VMEM((PAGES, 2, PAGE, HD), BF16),
            pltpu.VMEM((2 * CHIPS, 2 * HD, SHARE), BF16),
            pltpu.VMEM((STEPS, SLOTS, 2, HD), BF16),
            pltpu.VMEM((SLOTS * 4, HD), F32),
            pltpu.VMEM((4, SLOTS * 4, HD), F32),
            pltpu.VMEM((SLOTS * 4, TOK), F32),
            pltpu.VMEM((SLOTS * 4, HD), F32),
            pltpu.VMEM((CHIPS, ROWS, SHARE), BF16),
            pltpu.VMEM((CHIPS, ROWS, SHARE), F32),
            pltpu.SemaphoreType.DMA((PAGES,)),
            pltpu.SemaphoreType.DMA((2 * CHIPS,)),
            pltpu.SemaphoreType.DMA,
            pltpu.SemaphoreType.DMA((2 * CHIPS,)),
        ],
        compiler_params=pltpu.CompilerParams(vmem_limit_bytes=32 << 20),
        cost_estimate=pl.CostEstimate(flops=10**9, bytes_accessed=16 << 20, transcendentals=10**5),
        name="attend",
    )(block_table, blocks, query, new_kv, kv_pages, out_weight)


def norm_kernel(gain, *refs):
    mine, other, out = refs[:CHIPS], refs[CHIPS], refs[CHIPS + 1]
    tp = lax.axis_index("tp")
    core = lax.rem(tp, 2)
    chip = lax.div(tp, 2)
    x = lax.div(chip, 4)
    y = lax.rem(chip, 4)
    total = jnp.zeros((ROWS, 1), F32)
    for k in range(CHIPS):
        for h in (mine[k][...], other[k]):
            v = h.astype(F32)
            total = total + jnp.sum(v * v, axis=-1, keepdims=True)
    scale = lax.rsqrt(total / D + EPSILON)
    for k, (dx, dy) in enumerate(SHIFTS):
        chunk = lax.rem(x + dx, 2) * 4 + lax.rem(y + dy, 4)
        for part in range(2):
            v = (mine[k][...] if part == 0 else other[k]).astype(F32)
            place = (2 * chunk + (core if part == 0 else 1 - core)) * SHARE
            at = pl.ds(pl.multiple_of(place, SHARE), SHARE)
            out[:, at] = (v * scale * gain[:, at].astype(F32)).astype(BF16)


def norm(gain, mine, other):
    return pl.pallas_call(
        norm_kernel,
        out_shape=jax.ShapeDtypeStruct((ROWS, D), BF16),
        in_specs=[vmem_spec()] * (CHIPS + 2),
        out_specs=vmem_spec(),
        compiler_params=pltpu.CompilerParams(vmem_limit_bytes=16 << 20),
        cost_estimate=pl.CostEstimate(flops=4 * ROWS * D, bytes_accessed=4 * ROWS * D, transcendentals=0),
        name="norm",
    )(gain.reshape(1, D), *mine, other)


def place_kernel(mine, other, out, sems):
    core = lax.rem(lax.axis_index("tp"), 2)
    copies = []
    for b in range(MAXB):
        at = pl.ds(b * PAGE, PAGE)
        for k, ref in enumerate((mine, other)):
            kv = core if k == 0 else 1 - core
            copies.append(pltpu.make_async_copy(ref.at[:, at], out.at[:, b, kv, 0], sems.at[2 * b + k]))
            copies[-1].start()
    for copy in copies:
        copy.wait()


def place(mine, other):
    return pl.pallas_call(
        place_kernel,
        out_shape=jax.ShapeDtypeStruct((INST, MAXB, 2, 1, PAGE, HD), BF16),
        in_specs=[any_spec()] * 2,
        out_specs=any_spec(),
        scratch_shapes=[pltpu.SemaphoreType.DMA((2 * MAXB,))],
        cost_estimate=pl.CostEstimate(flops=0, bytes_accessed=6 << 20, transcendentals=0),
        name="place",
    )(mine, other)


def tp_perm(dx, dy, dc):
    return [
        (k, ((k // 8) ^ dx) * 8 + ((k // 2 % 4 + dy) % 4) * 2 + ((k % 2) ^ dc)) for k in range(16)
    ]


SWAP = tp_perm(0, 0, 1)


def local(query, new_kv, residual, kv_pages, block_table, blocks, moves, out_weight, norm_gain):
    packed = pack(block_table, blocks, moves, new_kv, kv_pages)
    half = lax.all_to_all(packed, "inst", split_axis=0, concat_axis=0, tiled=True)

    send, keep = attend(block_table, blocks, query, new_kv, kv_pages, out_weight)
    got = lax.ppermute(send, "tp", SWAP)
    sums = [keep[k] + got[k].astype(F32) for k in range(CHIPS)]
    order = [k for k in range(CHIPS - 1, 0, -1)]
    terms = {k: lax.ppermute(sums[k].astype(BF16), "tp", tp_perm(*SHIFTS[k], 0)) for k in order}
    attn = sums[0]
    for k in order:
        attn = attn + terms[k].astype(F32)
    hidden = (residual.astype(F32) + attn.reshape(STEPS, SLOTS, SHARE)).astype(BF16)
    flat = hidden.reshape(ROWS, SHARE)
    mine = [flat] + [
        lax.ppermute(flat, "tp", tp_perm(dx, (4 - dy) % 4, 0)) for dx, dy in SHIFTS[1:]
    ]
    other = lax.ppermute(jnp.stack(mine), "tp", SWAP)
    normed = norm(norm_gain, mine, other).reshape(STEPS, SLOTS, D)

    rest = lax.ppermute(half, "tp", SWAP)
    arrived = place(half, rest)
    tail = half[:, TOK:TOK + 4].reshape(INST, STEPS, 2, 1, HD)
    return (hidden, normed, arrived, tail)


def solution(mesh):
    in_specs = (
        P(None, "inst", "tp"),
        P(None, "inst", None, None),
        P(None, "inst", "tp"),
        P("inst", None, "tp", None, None),
        P("inst", None),
        P("inst"),
        P("inst", None),
        P("tp", None),
        P(),
    )
    out_specs = (
        P(None, "inst", "tp"),
        P(None, "inst", None),
        P("inst", None, None, "tp", None, None),
        P("inst", None, None, "tp", None),
    )
    return jax.shard_map(local, mesh=mesh, in_specs=in_specs, out_specs=out_specs, check_vma=False)
```

time: 224 us -> 205 us (0.915)
  Pallas kernels: 0 us -> 129 us
  waiting for transfers between devices: 125 us -> 26.1 us
  local copies, waits for them, and re-layouts: 34.8 us -> 13.3 us
  other arithmetic: 18.1 us -> 0.39 us
  starting transfers between devices: 19.8 us -> 34.2 us
  between operations: 14.3 us -> 1.02 us
  matrix products: 10.7 us -> 0 us
    pallas_call x0 -> x4, Pallas kernels: none -> 129 us  [the longest x1 96.4 us: place(): pl.pallas_call(place_kernel, out_shape=jax.ShapeDtypeStruct((INST, MAXB,...]
    psum x1 -> x0, waiting for transfers between devices: 123 us -> none  [local(): total = lax.psum(partial_sums, 'tp')]
    gather x6 -> x0, local copies, waits for them, and re-layouts: 29.2 us -> none  [the longest x2 22.5 us: local(): cached = jnp.take(kv_pages, block_table.reshape(-1), axis=0)]
    ppermute x0 -> x17, waiting for transfers between devices: none -> 26.1 us  [the longest x7 12.2 us: local(): lax.ppermute(flat, 'tp', tp_perm(dx, (4 - dy) % 4, 0))]
    ppermute x0 -> x17, starting transfers between devices: none -> 22.5 us  [the longest x7 8.26 us: local(): lax.ppermute(sums[k].astype(BF16), 'tp', tp_perm(*SHIFTS[k], 0))]
    dot_general x5 -> x0, matrix products: 10.7 us -> none  [the longest x1 4.24 us: local(): jnp.einsum('tsagd,sbapd->tsagbp', queries, cached[:, :, 0], preferred_ele...]
    select_n x8 -> x0, other arithmetic: 10.5 us -> none  [the longest x2 8.32 us: local(): cached = jnp.take(kv_pages, block_table.reshape(-1), axis=0)]
    unnamed x15 -> x34, local copies, waits for them, and re-layouts: 3.69 us -> 12.7 us
  transfers between devices with their start and end apart: 4 -> 18, of which waited for: 2 -> 8; matrix products, arithmetic and copies ran while one was open for 27% -> 1% of each run, Pallas kernels for 0% -> 15%
where the time goes in v1:
time: 205 us; the launch traced here: 204 us
  Pallas kernels  129 us (63%)
  starting transfers between devices  34.2 us (17%)
  waiting for transfers between devices  26.1 us (13%)
  local copies, waits for them, and re-layouts  13.3 us (6%)
    pallas_call x1, Pallas kernels, place(): pl.pallas_call(place_kernel, out_shape=jax.ShapeDtypeStruct((INST, MAXB,...  96.4 us
    pallas_call x1, Pallas kernels, attend(): pl.pallas_call(attend_kernel, out_shape=(jax.ShapeDtypeStruct((CHIPS, ROW...  27.7 us
    unnamed x34, local copies, waits for them, and re-layouts  12.7 us
    ppermute x7, waiting for transfers between devices, local(): lax.ppermute(flat, 'tp', tp_perm(dx, (4 - dy) % 4, 0))  12.2 us
    all_to_all x1, starting transfers between devices, local(): lax.all_to_all(packed, 'inst', split_axis=0, concat_axis=0, tiled=True)  11.7 us
    ppermute x7, starting transfers between devices, local(): lax.ppermute(sums[k].astype(BF16), 'tp', tp_perm(*SHIFTS[k], 0))  8.26 us
    ppermute x7, waiting for transfers between devices, local(): lax.ppermute(sums[k].astype(BF16), 'tp', tp_perm(*SHIFTS[k], 0))  7.91 us
    ppermute x7, starting transfers between devices, local(): lax.ppermute(flat, 'tp', tp_perm(dx, (4 - dy) % 4, 0))  7.46 us
  transfers between devices with their start and end apart: 18, of which 8 were waited for; matrix products, arithmetic and copies ran while one was open for 1% of the time, Pallas kernels for 15%

profile of v1, /device:TPU:1, one launch (start us, length us, event | category | flops | bytes accessed | tf_op | source)
XLA Modules:
  0.0 204.0 jit_solution(4698594087506628058)
XLA Ops:
  0.6 0.8 copy.13.tbl
  1.4 3.7 %copy-done = bf16[144,2,1,128,128]{4,3,2,1,0:T(8,128)(2,1)S(1)} copy-done((bf16[144,2,1,128,128]{4,3,2,1,0:T(8,128)(2,1)S(1)}, bf16[144,2,1,128,128]{4,3,2,1,0:T(8,128)(2,1)}, u32[]{:S(2)}) %copy-start) | copy-done | bytes 9437208
  5.1 1.0 copy-done.3
  6.1 0.7 copy-done.7
  6.7 0.7 copy-done.9
  7.4 2.6 %pack.1 = bf16[16,400,128]{2,1,0:T(8,128)(2,1)} custom-call(s32[48,3]{1,0:T(8,128)S(1)} %copy.13.tbl, s32[48]{0:T(128)S(1)} %copy-done.7, s32[1,16]{1,0:T(1,128)S(1)} %copy-done.9, bf16[2,48,2,1024]{3,2,1,0:T(2,128)(2,1)S(1)} %copy-done.3, bf16[144,2,1,128,128]{4,3,2,1,0:T(8,128)(2,1)S(1)} %copy-done), custom_call_target="tpu_custom_call" | custom-call | bytes 4194304 | tf_op jit(solution)/shard_map/pack/pallas_call | solution.py:85
  10.0 11.7 %all-to-all-start = ((bf16[16,400,128]{2,1,0:T(8,128)(2,1)}), bf16[16,400,128]{2,1,0:T(8,128)(2,1)S(1)}, u32[]{:S(2)}, u32[]{:S(2)}) async-start(bf16[16,400,128]{2,1,0:T(8,128)(2,1)} %pack.1), calls=%async_computation | async-start | bytes 3276800 | tf_op jit(solution)/shard_map/all_to_all | solution.py:339
  21.8 3.7 %copy-done.1 = bf16[144,2,1,128,128]{4,3,2,1,0:T(8,128)(2,1)S(1)} copy-done((bf16[144,2,1,128,128]{4,3,2,1,0:T(8,128)(2,1)S(1)}, bf16[144,2,1,128,128]{4,3,2,1,0:T(8,128)(2,1)}, u32[]{:S(2)}) %copy-start.1) | copy-done | bytes 9437208
  25.5 2.2 %copy-done.2 = bf16[256,8192]{1,0:T(8,128)(2,1)S(1)} copy-done((bf16[256,8192]{1,0:T(8,128)(2,1)S(1)}, bf16[256,8192]{1,0:T(8,128)(2,1)}, u32[]{:S(2)}) %copy-start.2) | copy-done | bytes 4194328
  27.6 27.7 %attend.1 = (bf16[8,96,512]{2,1,0:T(8,128)(2,1)S(1)}, f32[8,96,512]{2,1,0:T(8,128)S(1)}) custom-call(s32[48,3]{1,0:T(8,128)S(1)} %copy.13.tbl, s32[48]{0:T(128)S(1)} %copy-done.8, bf16[2,48,256]{2,1,0:T(8,128)(2,1)S(1)} %copy-done.6, bf16[2,48,2,1024]{3,2,1,0:T(2,128)(2,1)S(1)} %copy-done.4, bf16[144,2,1,128,128]{4,3,2,1,0:T(8,128)(2,1)S(1)} %copy-done.1, ...), custom_call_target="tpu_custom_call" | custom-call | flops 1000000000 | bytes 16777216 | tf_op jit(solution)/shard_map/attend/pallas_call | solution.py:240
  55.4 1.0 collective-permute-start
  56.4 1.9 collective-permute-done
  58.6 2.8 %collective-permute-start.1 = (bf16[96,512]{1,0:T(8,128)(2,1)S(1)}, bf16[96,512]{1,0:T(8,128)(2,1)S(1)}, u32[]{:S(2)}, u32[]{:S(2)}) collective-permute-start(bf16[96,512]{1,0:T(8,128)(2,1)S(1)} %get-tuple-element.12), channel_id=1, source_target_pairs={{0,14},{1,15},{2,8},{3,9},{4,10},{5,11},{6,12},{7,13},{8,6},{9,7},... | collective-permute-start | bytes 294920 | tf_op jit(solution)/shard_map/ppermute | solution.py:345
  61.4 1.6 collective-permute-start.6
  63.1 1.0 collective-permute-start.5
  64.1 1.2 collective-permute-start.4
  65.3 0.8 collective-permute-start.3
  66.1 2.8 %collective-permute-done.7 = bf16[96,512]{1,0:T(8,128)(2,1)S(1)} collective-permute-done((bf16[96,512]{1,0:T(8,128)(2,1)S(1)}, bf16[96,512]{1,0:T(8,128)(2,1)S(1)}, u32[]{:S(2)}, u32[]{:S(2)}) %collective-permute-start.7) | collective-permute-done | bytes 98336 | tf_op jit(solution)/shard_map/ppermute | solution.py:345
  68.8 0.8 collective-permute-start.2
  69.6 1.2 collective-permute-done.3
  70.8 3.9 %collective-permute-done.2 = bf16[96,512]{1,0:T(8,128)(2,1)S(1)} collective-permute-done((bf16[96,512]{1,0:T(8,128)(2,1)S(1)}, bf16[96,512]{1,0:T(8,128)(2,1)S(1)}, u32[]{:S(2)}, u32[]{:S(2)}) %collective-permute-start.2) | collective-permute-done | bytes 98336 | tf_op jit(solution)/shard_map/ppermute | solution.py:345
  75.0 1.8 collective-permute-start.13
  76.8 2.3 %collective-permute-start.12 = (bf16[96,512]{1,0:T(8,128)(2,1)S(1)}, bf16[96,512]{1,0:T(8,128)(2,1)S(1)}, u32[]{:S(2)}, u32[]{:S(2)}) collective-permute-start(bf16[96,512]{1,0:T(8,128)(2,1)S(1)} %bitcast.53), channel_id=1, source_target_pairs={{0,14},{1,15},{2,8},{3,9},{4,10},{5,11},{6,12},{7,13},{8,6},{9,7},... | collective-permute-start | bytes 294920 | tf_op jit(solution)/shard_map/ppermute | solution.py:352
  79.1 0.8 collective-permute-start.11
  80.4 4.0 %collective-permute-done.8.refs_1_ = bf16[96,512]{1,0:T(8,128)(2,1)S(1)} collective-permute-done((bf16[96,512]{1,0:T(8,128)(2,1)S(1)}, bf16[96,512]{1,0:T(8,128)(2,1)S(1)}, u32[]{:S(2)}, u32[]{:S(2)}) %collective-permute-start.8) | collective-permute-done | bytes 98336 | tf_op jit(solution)/shard_map/ppermute | solution.py:352
  84.4 1.5 collective-permute-start.9
  86.0 3.4 %collective-permute-done.9.refs_2_ = bf16[96,512]{1,0:T(8,128)(2,1)S(1)} collective-permute-done((bf16[96,512]{1,0:T(8,128)(2,1)S(1)}, bf16[96,512]{1,0:T(8,128)(2,1)S(1)}, u32[]{:S(2)}, u32[]{:S(2)}) %collective-permute-start.9) | collective-permute-done | bytes 98336 | tf_op jit(solution)/shard_map/ppermute | solution.py:352
  89.9 4.8 %collective-permute-done.10.refs_3_ = bf16[96,512]{1,0:T(8,128)(2,1)S(1)} collective-permute-done((bf16[96,512]{1,0:T(8,128)(2,1)S(1)}, bf16[96,512]{1,0:T(8,128)(2,1)S(1)}, u32[]{:S(2)}, u32[]{:S(2)}) %collective-permute-start.10) | collective-permute-done | bytes 98336 | tf_op jit(solution)/shard_map/ppermute | solution.py:352
  94.7 5.6 %collective-permute-start.16 = (bf16[16,400,128]{2,1,0:T(8,128)(2,1)S(1)}, bf16[16,400,128]{2,1,0:T(8,128)(2,1)}, u32[]{:S(2)}, u32[]{:S(2)}) collective-permute-start(bf16[16,400,128]{2,1,0:T(8,128)(2,1)S(1)} %all-to-all-done.mine), channel_id=1, source_target_pairs={{0,1},{1,0},{2,3},{3,2},{4,5},{5,4},{6,7},{7,6},{8,9},{9,8},{10,11... | collective-permute-start | bytes 4915208 | tf_op jit(solution)/shard_map/ppermute | solution.py:357
  100.6 4.0 %collective-permute-done.15.refs_8_ = bf16[8,96,512]{2,1,0:T(8,128)(2,1)S(1)} collective-permute-done((bf16[8,96,512]{2,1,0:T(8,128)(2,1)S(1)}, bf16[8,96,512]{2,1,0:T(8,128)(2,1)S(1)}, u32[]{:S(2)}, u32[]{:S(2)}) %collective-permute-start.15) | collective-permute-done | bytes 786464 | tf_op jit(solution)/shard_map/ppermute | solution.py:354
  104.6 2.2 %norm.1 = bf16[96,8192]{1,0:T(8,128)(2,1)} custom-call(bf16[1,8192]{1,0:T(2,128)(2,1)S(1)} %reshape.47.gain, bf16[96,512]{1,0:T(8,128)(2,1)S(1)} %bitcast.59, bf16[96,512]{1,0:T(8,128)(2,1)S(1)} %collective-permute-done.8.refs_1_, bf16[96,512]{1,0:T(8,128)(2,1)S(1)} %collective-permute-done.9.refs_2_, bf16[96,512]{1,0:T(8,128)(2,1)S(1)} %collective-permute-done.10.refs_3_, ...), custom_call_target="tpu_custom_call" | custom-call | flops 3145728 | bytes 3145728 | tf_op jit(solution)/shard_map/norm/pallas_call | solution.py:292
  107.4 96.4 %place.1 = bf16[16,3,2,1,128,128]{5,4,3,2,1,0:T(8,128)(2,1)} custom-call(bf16[16,400,128]{2,1,0:T(8,128)(2,1)} %copy-done.10, bf16[16,400,128]{2,1,0:T(8,128)(2,1)} %collective-permute-done.16.other), custom_call_target="tpu_custom_call" | custom-call | bytes 6291456 | tf_op jit(solution)/shard_map/place/pallas_call | solution.py:317
  (48 shorter events, 2.2 us)
Async XLA Ops:
  1.4 3.7 %copy-start = (bf16[144,2,1,128,128]{4,3,2,1,0:T(8,128)(2,1)S(1)}, bf16[144,2,1,128,128]{4,3,2,1,0:T(8,128)(2,1)}, u32[]{:S(2)}) copy-start(bf16[144,2,1,128,128]{4,3,2,1,0:T(8,128)(2,1)} %kv.3) | copy-start | bytes 28311556
  5.1 1.0 copy-start.3
  6.1 0.7 copy-start.7
  6.7 0.7 copy-start.9
  10.0 11.8 %copy-start.4 = (bf16[2,48,2,1024]{3,2,1,0:T(2,128)(2,1)S(1)}, bf16[2,48,2,1024]{3,2,1,0:T(2,128)(2,1)}, u32[]{:S(2)}) copy-start(bf16[2,48,2,1024]{3,2,1,0:T(2,128)(2,1)} %nkv.3) | copy-start | bytes 1179652
  10.0 11.8 %copy-start.6 = (bf16[2,48,256]{2,1,0:T(8,128)(2,1)S(1)}, bf16[2,48,256]{2,1,0:T(8,128)(2,1)}, u32[]{:S(2)}) copy-start(bf16[2,48,256]{2,1,0:T(8,128)(2,1)} %q.1) | copy-start | bytes 147460
  10.0 11.8 %copy-start.8 = (s32[48]{0:T(128)S(1)}, s32[48]{0:T(128)}, u32[]{:S(2)}) copy-start(s32[48]{0:T(128)} %blk.3) | copy-start | bytes 580
  10.0 84.7 %all-to-all-start = ((bf16[16,400,128]{2,1,0:T(8,128)(2,1)}), bf16[16,400,128]{2,1,0:T(8,128)(2,1)S(1)}, u32[]{:S(2)}, u32[]{:S(2)}) async-start(bf16[16,400,128]{2,1,0:T(8,128)(2,1)} %pack.1), calls=%async_computation | async-start | bytes 3276800 | tf_op jit(solution)/shard_map/all_to_all | solution.py:339
  21.8 3.7 %copy-start.1 = (bf16[144,2,1,128,128]{4,3,2,1,0:T(8,128)(2,1)S(1)}, bf16[144,2,1,128,128]{4,3,2,1,0:T(8,128)(2,1)}, u32[]{:S(2)}) copy-start(bf16[144,2,1,128,128]{4,3,2,1,0:T(8,128)(2,1)} %kv.3) | copy-start | bytes 28311556
  25.5 2.2 %copy-start.2 = (bf16[256,8192]{1,0:T(8,128)(2,1)S(1)}, bf16[256,8192]{1,0:T(8,128)(2,1)}, u32[]{:S(2)}) copy-start(bf16[256,8192]{1,0:T(8,128)(2,1)} %w.1) | copy-start | bytes 12582916
  55.4 3.0 %collective-permute-start = (bf16[8,96,512]{2,1,0:T(8,128)(2,1)S(1)}, bf16[8,96,512]{2,1,0:T(8,128)(2,1)S(1)}, u32[]{:S(2)}, u32[]{:S(2)}) collective-permute-start(bf16[8,96,512]{2,1,0:T(8,128)(2,1)S(1)} %get-tuple-element.7), channel_id=1, source_target_pairs={{0,1},{1,0},{2,3},{3,2},{4,5},{5,4},{6,7},{7,6},{8,9},{9,8},{10,11... | collective-permute-start | bytes 2359304 | tf_op jit(solution)/shard_map/ppermute | solution.py:342
  58.3 16.6 %copy-start.11 = (bf16[2,48,512]{2,1,0:T(8,128)(2,1)S(1)}, bf16[2,48,512]{2,1,0:T(8,128)(2,1)}, u32[]{:S(2)}) copy-start(bf16[2,48,512]{2,1,0:T(8,128)(2,1)} %param.11) | copy-start | bytes 294916
  58.6 42.0 %copy-start.12 = (bf16[8192]{0:T(1024)(128)(2,1)S(1)}, bf16[8192]{0:T(1024)(128)(2,1)}, u32[]{:S(2)}) copy-start(bf16[8192]{0:T(1024)(128)(2,1)} %param.17) | copy-start | bytes 49156
  58.6 6.7 %collective-permute-start.1 = (bf16[96,512]{1,0:T(8,128)(2,1)S(1)}, bf16[96,512]{1,0:T(8,128)(2,1)S(1)}, u32[]{:S(2)}, u32[]{:S(2)}) collective-permute-start(bf16[96,512]{1,0:T(8,128)(2,1)S(1)} %get-tuple-element.12), channel_id=1, source_target_pairs={{0,14},{1,15},{2,8},{3,9},{4,10},{5,11},{6,12},{7,13},{8,6},{9,7},... | collective-permute-start | bytes 294920 | tf_op jit(solution)/shard_map/ppermute | solution.py:345
  61.4 7.4 %collective-permute-start.7 = (bf16[96,512]{1,0:T(8,128)(2,1)S(1)}, bf16[96,512]{1,0:T(8,128)(2,1)S(1)}, u32[]{:S(2)}, u32[]{:S(2)}) collective-permute-start(bf16[96,512]{1,0:T(8,128)(2,1)S(1)} %get-tuple-element.13), channel_id=1, source_target_pairs={{0,2},{1,3},{2,4},{3,5},{4,6},{5,7},{6,0},{7,1},{8,10},{9,11},{10,... | collective-permute-start | bytes 294920 | tf_op jit(solution)/shard_map/ppermute | solution.py:345
  61.4 8.2 %collective-permute-start.6 = (bf16[96,512]{1,0:T(8,128)(2,1)S(1)}, bf16[96,512]{1,0:T(8,128)(2,1)S(1)}, u32[]{:S(2)}, u32[]{:S(2)}) collective-permute-start(bf16[96,512]{1,0:T(8,128)(2,1)S(1)} %get-tuple-element.14), channel_id=1, source_target_pairs={{0,4},{1,5},{2,6},{3,7},{4,0},{5,1},{6,2},{7,3},{8,12},{9,13},{10,... | collective-permute-start | bytes 294920 | tf_op jit(solution)/shard_map/ppermute | solution.py:345
  63.1 6.5 %collective-permute-start.5 = (bf16[96,512]{1,0:T(8,128)(2,1)S(1)}, bf16[96,512]{1,0:T(8,128)(2,1)S(1)}, u32[]{:S(2)}, u32[]{:S(2)}) collective-permute-start(bf16[96,512]{1,0:T(8,128)(2,1)S(1)} %get-tuple-element.15), channel_id=1, source_target_pairs={{0,6},{1,7},{2,0},{3,1},{4,2},{5,3},{6,4},{7,5},{8,14},{9,15},{10,... | collective-permute-start | bytes 294920 | tf_op jit(solution)/shard_map/ppermute | solution.py:345
  64.1 5.5 %collective-permute-start.4 = (bf16[96,512]{1,0:T(8,128)(2,1)S(1)}, bf16[96,512]{1,0:T(8,128)(2,1)S(1)}, u32[]{:S(2)}, u32[]{:S(2)}) collective-permute-start(bf16[96,512]{1,0:T(8,128)(2,1)S(1)} %get-tuple-element.16), channel_id=1, source_target_pairs={{0,8},{1,9},{2,10},{3,11},{4,12},{5,13},{6,14},{7,15},{8,0},{9,1},... | collective-permute-start | bytes 294920 | tf_op jit(solution)/shard_map/ppermute | solution.py:345
  65.3 5.6 %collective-permute-start.3 = (bf16[96,512]{1,0:T(8,128)(2,1)S(1)}, bf16[96,512]{1,0:T(8,128)(2,1)S(1)}, u32[]{:S(2)}, u32[]{:S(2)}) collective-permute-start(bf16[96,512]{1,0:T(8,128)(2,1)S(1)} %get-tuple-element.17), channel_id=1, source_target_pairs={{0,10},{1,11},{2,12},{3,13},{4,14},{5,15},{6,8},{7,9},{8,2},{9,3},... | collective-permute-start | bytes 294920 | tf_op jit(solution)/shard_map/ppermute | solution.py:345
  68.8 5.9 %collective-permute-start.2 = (bf16[96,512]{1,0:T(8,128)(2,1)S(1)}, bf16[96,512]{1,0:T(8,128)(2,1)S(1)}, u32[]{:S(2)}, u32[]{:S(2)}) collective-permute-start(bf16[96,512]{1,0:T(8,128)(2,1)S(1)} %get-tuple-element.18), channel_id=1, source_target_pairs={{0,12},{1,13},{2,14},{3,15},{4,8},{5,9},{6,10},{7,11},{8,4},{9,5},... | collective-permute-start | bytes 294920 | tf_op jit(solution)/shard_map/ppermute | solution.py:345
  74.9 31.9 %copy-start.5 = (bf16[2,48,512]{2,1,0:T(8,128)(2,1)}, bf16[2,48,512]{2,1,0:T(8,128)(2,1)S(1)}, u32[]{:S(2)}) copy-start(bf16[2,48,512]{2,1,0:T(8,128)(2,1)S(1)} %add_convert_fusion) | copy-start | bytes 294916
  74.9 25.5 %collective-permute-start.14 = (bf16[96,512]{1,0:T(8,128)(2,1)S(1)}, bf16[96,512]{1,0:T(8,128)(2,1)S(1)}, u32[]{:S(2)}, u32[]{:S(2)}) collective-permute-start(bf16[96,512]{1,0:T(8,128)(2,1)S(1)} %bitcast.51), channel_id=1, source_target_pairs={{0,10},{1,11},{2,12},{3,13},{4,14},{5,15},{6,8},{7,9},{8,2},{9,3},... | collective-permute-start | bytes 294920 | tf_op jit(solution)/shard_map/ppermute | solution.py:352
  75.0 25.3 %collective-permute-start.13 = (bf16[96,512]{1,0:T(8,128)(2,1)S(1)}, bf16[96,512]{1,0:T(8,128)(2,1)S(1)}, u32[]{:S(2)}, u32[]{:S(2)}) collective-permute-start(bf16[96,512]{1,0:T(8,128)(2,1)S(1)} %bitcast.52), channel_id=1, source_target_pairs={{0,12},{1,13},{2,14},{3,15},{4,8},{5,9},{6,10},{7,11},{8,4},{9,5},... | collective-permute-start | bytes 294920 | tf_op jit(solution)/shard_map/ppermute | solution.py:352
  76.8 23.5 %collective-permute-start.12 = (bf16[96,512]{1,0:T(8,128)(2,1)S(1)}, bf16[96,512]{1,0:T(8,128)(2,1)S(1)}, u32[]{:S(2)}, u32[]{:S(2)}) collective-permute-start(bf16[96,512]{1,0:T(8,128)(2,1)S(1)} %bitcast.53), channel_id=1, source_target_pairs={{0,14},{1,15},{2,8},{3,9},{4,10},{5,11},{6,12},{7,13},{8,6},{9,7},... | collective-permute-start | bytes 294920 | tf_op jit(solution)/shard_map/ppermute | solution.py:352
  79.1 21.2 %collective-permute-start.11 = (bf16[96,512]{1,0:T(8,128)(2,1)S(1)}, bf16[96,512]{1,0:T(8,128)(2,1)S(1)}, u32[]{:S(2)}, u32[]{:S(2)}) collective-permute-start(bf16[96,512]{1,0:T(8,128)(2,1)S(1)} %bitcast.54), channel_id=1, source_target_pairs={{0,8},{1,9},{2,10},{3,11},{4,12},{5,13},{6,14},{7,15},{8,0},{9,1},... | collective-permute-start | bytes 294920 | tf_op jit(solution)/shard_map/ppermute | solution.py:352
  80.0 4.4 %collective-permute-start.8 = (bf16[96,512]{1,0:T(8,128)(2,1)S(1)}, bf16[96,512]{1,0:T(8,128)(2,1)S(1)}, u32[]{:S(2)}, u32[]{:S(2)}) collective-permute-start(bf16[96,512]{1,0:T(8,128)(2,1)S(1)} %bitcast.55), channel_id=1, source_target_pairs={{0,6},{1,7},{2,0},{3,1},{4,2},{5,3},{6,4},{7,5},{8,14},{9,15},{10,... | collective-permute-start | bytes 294920 | tf_op jit(solution)/shard_map/ppermute | solution.py:352
  84.4 5.0 %collective-permute-start.9 = (bf16[96,512]{1,0:T(8,128)(2,1)S(1)}, bf16[96,512]{1,0:T(8,128)(2,1)S(1)}, u32[]{:S(2)}, u32[]{:S(2)}) collective-permute-start(bf16[96,512]{1,0:T(8,128)(2,1)S(1)} %bitcast.57), channel_id=1, source_target_pairs={{0,4},{1,5},{2,6},{3,7},{4,0},{5,1},{6,2},{7,3},{8,12},{9,13},{10,... | collective-permute-start | bytes 294920 | tf_op jit(solution)/shard_map/ppermute | solution.py:352
  89.4 5.3 %collective-permute-start.10 = (bf16[96,512]{1,0:T(8,128)(2,1)S(1)}, bf16[96,512]{1,0:T(8,128)(2,1)S(1)}, u32[]{:S(2)}, u32[]{:S(2)}) collective-permute-start(bf16[96,512]{1,0:T(8,128)(2,1)S(1)} %bitcast.58), channel_id=1, source_target_pairs={{0,2},{1,3},{2,4},{3,5},{4,6},{5,7},{6,0},{7,1},{8,10},{9,11},{10,... | collective-permute-start | bytes 294920 | tf_op jit(solution)/shard_map/ppermute | solution.py:352
  94.7 12.1 %copy-start.10 = (bf16[16,400,128]{2,1,0:T(8,128)(2,1)}, bf16[16,400,128]{2,1,0:T(8,128)(2,1)S(1)}, u32[]{:S(2)}) copy-start(bf16[16,400,128]{2,1,0:T(8,128)(2,1)S(1)} %all-to-all-done.mine) | copy-start | bytes 4915204
  94.7 12.7 %collective-permute-start.16 = (bf16[16,400,128]{2,1,0:T(8,128)(2,1)S(1)}, bf16[16,400,128]{2,1,0:T(8,128)(2,1)}, u32[]{:S(2)}, u32[]{:S(2)}) collective-permute-start(bf16[16,400,128]{2,1,0:T(8,128)(2,1)S(1)} %all-to-all-done.mine), channel_id=1, source_target_pairs={{0,1},{1,0},{2,3},{3,2},{4,5},{5,4},{6,7},{7,6},{8,9},{9,8},{10,11... | collective-permute-start | bytes 4915208 | tf_op jit(solution)/shard_map/ppermute | solution.py:357
  100.4 4.2 %collective-permute-start.15 = (bf16[8,96,512]{2,1,0:T(8,128)(2,1)S(1)}, bf16[8,96,512]{2,1,0:T(8,128)(2,1)S(1)}, u32[]{:S(2)}, u32[]{:S(2)}) collective-permute-start(bf16[8,96,512]{2,1,0:T(8,128)(2,1)S(1)} %bitcast_dynamic-update-slice_fusion), channel_id=1, source_target_pairs={{0,1},{1,0},{2,3},{3,2},{4,5},{5,4},{6,7},{7,6},{8,9},{9,8},{10,11... | collective-permute-start | bytes 2359304 | tf_op jit(solution)/shard_map/ppermute | solution.py:354

commit v2 on v1

v2 whole, which is shorter than its diff:
```python
import functools

import jax
import jax.numpy as jnp
from jax import lax
from jax.experimental import pallas as pl
from jax.experimental.pallas import tpu as pltpu
from jax.sharding import PartitionSpec as P

F32 = jnp.float32
BF16 = jnp.bfloat16
EPSILON = 1e-05
MASKED = -1e30

SLOTS = 48
MAXB = 3
PAGE = 128
HD = 128
STEPS = 2
INST = 16
CHIPS = 8
ROWS = STEPS * SLOTS
D = 8192
SHARE = 512
PAGES = SLOTS * MAXB
TOK = MAXB * PAGE
MSG = TOK + 16
SHIFTS = [(dx, dy) for dy in range(4) for dx in range(2)]


def any_spec():
    return pl.BlockSpec(memory_space=pl.ANY)


def smem_spec():
    return pl.BlockSpec(memory_space=pltpu.SMEM)


def vmem_spec():
    return pl.BlockSpec(memory_space=pltpu.VMEM)


def pack_kernel(tbl, blk, mv, nkv, kv, out, buf, fresh, stage, sems, fsem, osem):
    tp = lax.axis_index("tp")
    core = lax.rem(tp, 2)
    head = lax.div(tp, 2)
    fcopy = pltpu.make_async_copy(
        nkv.at[:, :, :, pl.ds(pl.multiple_of(head * HD, HD), HD)], fresh, fsem
    )
    fcopy.start()

    def page_copy(j, b, page):
        return pltpu.make_async_copy(
            kv.at[page, core, 0], buf.at[j, pl.ds(b * PAGE, PAGE)], sems.at[j * MAXB + b]
        )

    for j in range(INST):
        for b in range(MAXB):
            page_copy(j, b, tbl[b, mv[0, j]]).start()
    stage[...] = jnp.zeros_like(stage)
    fcopy.wait()
    for j in range(INST):
        m = mv[0, j]
        stage[j, 0:2] = fresh[0, m].astype(F32)
        stage[j, 2:4] = fresh[1, m].astype(F32)
    buf[:, TOK:MSG] = stage[...].astype(BF16)
    for j in range(INST):
        count = blk[mv[0, j]]
        for b in range(MAXB):
            page_copy(j, b, 0).wait()
            if b > 0:
                @pl.when(b >= count)
                def _():
                    buf[j, b * PAGE:(b + 1) * PAGE] = jnp.zeros((PAGE, HD), BF16)
    ocopy = pltpu.make_async_copy(buf, out, osem)
    ocopy.start()
    ocopy.wait()


def pack(table, blocks, moves, new_kv, kv_pages):
    return pl.pallas_call(
        pack_kernel,
        out_shape=jax.ShapeDtypeStruct((INST, MSG, HD), BF16),
        in_specs=[smem_spec()] * 3 + [any_spec()] * 2,
        out_specs=any_spec(),
        scratch_shapes=[
            pltpu.VMEM((INST, MSG, HD), BF16),
            pltpu.VMEM((STEPS, SLOTS, 2, HD), BF16),
            pltpu.VMEM((INST, 16, HD), F32),
            pltpu.SemaphoreType.DMA((INST * MAXB,)),
            pltpu.SemaphoreType.DMA,
            pltpu.SemaphoreType.DMA,
        ],
        compiler_params=pltpu.CompilerParams(vmem_limit_bytes=60 << 20),
        cost_estimate=pl.CostEstimate(flops=0, bytes_accessed=4 << 20, transcendentals=0),
        name="pack",
    )(table, blocks, moves, new_kv, kv_pages)


def attend_kernel(tbl, blk, q_hbm, nkv, kv, w, send, keep, kvb, wb, fresh, qs, ks, sc, ob, sbuf, kbuf,
                  kvsem, wsem, fsem, osem, q, qsem):
    qcopy = pltpu.make_async_copy(q_hbm, q, qsem)
    qcopy.start()
    tp = lax.axis_index("tp")
    core = lax.rem(tp, 2)
    chip = lax.div(tp, 2)
    x = lax.div(chip, 4)
    y = lax.rem(chip, 4)
    fcopy = pltpu.make_async_copy(
        nkv.at[:, :, :, pl.ds(pl.multiple_of(chip * HD, HD), HD)], fresh, fsem
    )
    fcopy.start()

    kcopy = pltpu.make_async_copy(kv.at[:, 0, 0], kvb.at[0], kvsem.at[0])
    vcopy = pltpu.make_async_copy(kv.at[:, 1, 0], kvb.at[1], kvsem.at[1])
    kcopy.start()
    vcopy.start()

    def owner(k):
        dx, dy = SHIFTS[k % CHIPS]
        other = lax.rem(x + dx, 2) * 4 + lax.rem(y + dy, 4)
        return other * 2 + (1 - core if k < CHIPS else core)

    wcopy = pltpu.make_async_copy(w, wb, wsem.at[0])
    wcopy.start()

    qcopy.wait()
    for t in range(STEPS):
        for g in range(2):
            qs[pl.ds(t * 2 + g, SLOTS, stride=4), :] = q[t, :, g * HD:(g + 1) * HD].astype(F32)
    fcopy.wait()
    fr = fresh[...].astype(F32)
    for u in range(STEPS):
        for c in range(2):
            val = fr[u, :, c, :]
            for j in range(4):
                ks[u * 2 + c, pl.ds(j, SLOTS, stride=4), :] = val

    scaling = HD ** (-0.5)
    row_a = lax.broadcasted_iota(jnp.int32, (8, TOK), 0) < 4
    block_of = lax.div(lax.broadcasted_iota(jnp.int32, (8, TOK), 1), PAGE)

    def score_pair(p, carry):
        rows = pl.ds(pl.multiple_of(p * 8, 8), 8)
        q8 = qs[rows, :].astype(BF16)
        parts = []
        for h in range(2):
            keys = jnp.concatenate([kvb[0, tbl[b, 2 * p + h]] for b in range(MAXB)], axis=0)
            parts.append(lax.dot_general(q8, keys, (((1,), (1,)), ((), ())), preferred_element_type=F32))
        s8 = jnp.where(row_a, parts[0], parts[1]) * scaling
        count = jnp.where(row_a, blk[2 * p], blk[2 * p + 1])
        sc[rows, :] = jnp.where(block_of < count, s8, MASKED)
        return carry

    kcopy.wait()
    lax.fori_loop(0, SLOTS // 2, score_pair, 0, unroll=True)

    qa = qs[...]
    f0 = jnp.sum(qa * ks[0], axis=-1, keepdims=True) * scaling
    f1 = jnp.sum(qa * ks[2], axis=-1, keepdims=True) * scaling
    late = lax.rem(lax.broadcasted_iota(jnp.int32, (SLOTS * 4, 1), 0), 4) >= 2
    f1 = jnp.where(late, f1, MASKED)
    s = sc[...]
    top = jnp.maximum(jnp.max(s, axis=-1, keepdims=True), jnp.maximum(f0, f1))
    e = jnp.exp(s - top)
    e0 = jnp.exp(f0 - top)
    e1 = jnp.exp(f1 - top)
    total = jnp.sum(e, axis=-1, keepdims=True) + e0 + e1
    sc[...] = e / total
    w0 = (e0 / total).astype(BF16).astype(F32)
    w1 = (e1 / total).astype(BF16).astype(F32)
    ob[...] = w0 * ks[1] + w1 * ks[3]
    row_o = lax.broadcasted_iota(jnp.int32, (8, HD), 0) < 4

    def mix_pair(p, carry):
        rows = pl.ds(pl.multiple_of(p * 8, 8), 8)
        w8 = sc[rows, :].astype(BF16)
        parts = []
        for h in range(2):
            vals = jnp.concatenate([kvb[1, tbl[b, 2 * p + h]] for b in range(MAXB)], axis=0)
            parts.append(jnp.dot(w8, vals, preferred_element_type=F32))
        ob[rows, :] += jnp.where(row_o, parts[0], parts[1])
        return carry

    vcopy.wait()
    lax.fori_loop(0, SLOTS // 2, mix_pair, 0, unroll=True)

    heads = jnp.concatenate(
        [
            jnp.concatenate([ob[pl.ds(t * 2 + g, SLOTS, stride=4), :] for g in range(2)], axis=1)
            for t in range(STEPS)
        ],
        axis=0,
    ).astype(BF16)

    outs = []
    wcopy.wait()
    for k in range(2 * CHIPS):
        cols = pl.ds(pl.multiple_of(owner(k) * SHARE, SHARE), SHARE)
        part = jnp.dot(heads, wb[:, cols], preferred_element_type=F32)
        i = k % CHIPS
        if k < CHIPS:
            sbuf[i] = part.astype(BF16)
            copy = pltpu.make_async_copy(sbuf.at[i], send.at[i], osem.at[k])
        else:
            kbuf[i] = part
            copy = pltpu.make_async_copy(kbuf.at[i], keep.at[i], osem.at[k])
        copy.start()
        outs.append(copy)
    for copy in outs:
        copy.wait()


def attend(table, blocks, query, new_kv, kv_pages, out_weight):
    return pl.pallas_call(
        attend_kernel,
        out_shape=(
            jax.ShapeDtypeStruct((CHIPS, ROWS, SHARE), BF16),
            jax.ShapeDtypeStruct((CHIPS, ROWS, SHARE), F32),
        ),
        in_specs=[smem_spec()] * 2 + [any_spec()] * 4,
        out_specs=(any_spec(), any_spec()),
        scratch_shapes=[
            pltpu.VMEM((2, PAGES, PAGE, HD), BF16),
            pltpu.VMEM((2 * HD, D), BF16),
            pltpu.VMEM((STEPS, SLOTS, 2, HD), BF16),
            pltpu.VMEM((SLOTS * 4, HD), F32),
            pltpu.VMEM((4, SLOTS * 4, HD), F32),
            pltpu.VMEM((SLOTS * 4, TOK), F32),
            pltpu.VMEM((SLOTS * 4, HD), F32),
            pltpu.VMEM((CHIPS, ROWS, SHARE), BF16),
            pltpu.VMEM((CHIPS, ROWS, SHARE), F32),
            pltpu.SemaphoreType.DMA((2,)),
            pltpu.SemaphoreType.DMA((2 * CHIPS,)),
            pltpu.SemaphoreType.DMA,
            pltpu.SemaphoreType.DMA((2 * CHIPS,)),
            pltpu.VMEM((STEPS, SLOTS, 2 * HD), BF16),
            pltpu.SemaphoreType.DMA,
        ],
        compiler_params=pltpu.CompilerParams(vmem_limit_bytes=60 << 20),
        cost_estimate=pl.CostEstimate(flops=10**9, bytes_accessed=16 << 20, transcendentals=10**5),
        name="attend",
    )(table, blocks, query, new_kv, kv_pages, out_weight)


def norm_kernel(gain, *refs):
    mine, other, out = refs[:4], refs[4:8], refs[8]
    tp = lax.axis_index("tp")
    core = lax.rem(tp, 2)
    chip = lax.div(tp, 2)
    x = lax.div(chip, 4)
    y = lax.rem(chip, 4)
    squares = jnp.zeros((ROWS, SHARE), F32)
    for ref in refs[:8]:
        for dx in range(2):
            v = ref[dx].astype(F32)
            squares = squares + v * v
    scale = lax.rsqrt(jnp.sum(squares, axis=-1, keepdims=True) / D + EPSILON)
    for dy in range(4):
        for dx in range(2):
            chunk = lax.rem(x + dx, 2) * 4 + lax.rem(y + dy, 4)
            for ref, parity in ((mine[dy], core), (other[dy], 1 - core)):
                v = ref[dx].astype(F32)
                at = pl.ds(pl.multiple_of((2 * chunk + parity) * SHARE, SHARE), SHARE)
                out[:, at] = (v * scale * gain[:, at].astype(F32)).astype(BF16)


def norm(gain, mine, other):
    return pl.pallas_call(
        norm_kernel,
        out_shape=jax.ShapeDtypeStruct((ROWS, D), BF16),
        in_specs=[vmem_spec()] * 9,
        out_specs=vmem_spec(),
        compiler_params=pltpu.CompilerParams(vmem_limit_bytes=16 << 20),
        cost_estimate=pl.CostEstimate(flops=4 * ROWS * D, bytes_accessed=4 * ROWS * D, transcendentals=0),
        name="norm",
    )(gain.reshape(1, D), *mine, *other)


def place_kernel(other, *refs):
    src, out, sem = refs[0], refs[-2], refs[-1]
    core = lax.rem(lax.axis_index("tp"), 2)
    half = 1 - core if other else core
    copies = [
        pltpu.make_async_copy(src.at[:, pl.ds(b * PAGE, PAGE)], out.at[:, b, half, 0], sem.at[b])
        for b in range(MAXB)
    ]
    for copy in copies:
        copy.start()
    for copy in copies:
        copy.wait()


def place(src, into=None):
    extra = () if into is None else (into,)
    return pl.pallas_call(
        functools.partial(place_kernel, into is not None),
        out_shape=jax.ShapeDtypeStruct((INST, MAXB, 2, 1, PAGE, HD), BF16),
        in_specs=[vmem_spec()] + [any_spec()] * len(extra),
        out_specs=any_spec(),
        scratch_shapes=[pltpu.SemaphoreType.DMA((MAXB,))],
        input_output_aliases={1: 0} if extra else {},
        compiler_params=pltpu.CompilerParams(vmem_limit_bytes=60 << 20),
        cost_estimate=pl.CostEstimate(flops=0, bytes_accessed=3 << 20, transcendentals=0),
        name="place",
    )(src, *extra)


def tp_perm(dx, dy, dc):
    return [
        (k, ((k // 8) ^ dx) * 8 + ((k // 2 % 4 + dy) % 4) * 2 + ((k % 2) ^ dc)) for k in range(16)
    ]


SWAP = tp_perm(0, 0, 1)
CROSS = tp_perm(1, 0, 0)
AROUND = (2, 1, 3)


def local(query, new_kv, residual, kv_pages, block_table, blocks, moves, out_weight, norm_gain):
    table = block_table.T
    packed = pack(table, blocks, moves, new_kv, kv_pages)
    half = lax.all_to_all(packed, "inst", split_axis=0, concat_axis=0, tiled=True)

    send, keep = attend(table, blocks, query, new_kv, kv_pages, out_weight)
    got = lax.ppermute(send, "tp", SWAP)
    sums = [
        keep[2 * dy:2 * dy + 2] + got[2 * dy:2 * dy + 2].astype(F32) for dy in range(4)
    ]
    terms = [lax.ppermute(sums[dy].astype(BF16), "tp", tp_perm(0, dy, 0)) for dy in AROUND]
    total = sums[0]
    for term in terms:
        total = total + term.astype(F32)
    crossed = lax.ppermute(total[1].astype(BF16), "tp", CROSS)
    attn = total[0] + crossed.astype(F32)
    hidden = (residual.astype(F32) + attn.reshape(STEPS, SLOTS, SHARE)).astype(BF16)
    flat = hidden.reshape(ROWS, SHARE)
    pair = jnp.stack([flat, lax.ppermute(flat, "tp", CROSS)])
    mine = {0: pair}
    for dy in AROUND:
        mine[dy] = lax.ppermute(pair, "tp", tp_perm(0, 4 - dy, 0))
    mine = [mine[dy] for dy in range(4)]
    other = [lax.ppermute(block, "tp", SWAP) for block in mine]
    normed = norm(norm_gain, mine, other).reshape(STEPS, SLOTS, D)

    rest = lax.ppermute(half, "tp", SWAP)
    arrived = place(rest, place(half))
    tail = half[:, TOK:TOK + 4].reshape(INST, STEPS, 2, 1, HD)
    return (hidden, normed, arrived, tail)


def solution(mesh):
    in_specs = (
        P(None, "inst", "tp"),
        P(None, "inst", None, None),
        P(None, "inst", "tp"),
        P("inst", None, "tp", None, None),
        P("inst", None),
        P("inst"),
        P("inst", None),
        P("tp", None),
        P(),
    )
    out_specs = (
        P(None, "inst", "tp"),
        P(None, "inst", None),
        P("inst", None, None, "tp", None, None),
        P("inst", None, None, "tp", None),
    )
    return jax.shard_map(local, mesh=mesh, in_specs=in_specs, out_specs=out_specs, check_vma=False)
```

time: 205 us -> 94 us (0.46)
  Pallas kernels: 129 us -> 21.5 us
  local copies, waits for them, and re-layouts: 13.3 us -> 1.86 us
  other arithmetic: 0.39 us -> 4.75 us
  waiting for transfers between devices: 26.1 us -> 28.3 us
  starting transfers between devices: 34.2 us -> 36.4 us
    pallas_call x1 -> x2, Pallas kernels: 96.4 us -> 5.18 us  [place(): pl.pallas_call(functools.partial(place_kernel, into is not None), out_sha...]
    all_to_all x1, waiting for transfers between devices: 0.01 us -> 18.4 us  [local(): lax.all_to_all(packed, 'inst', split_axis=0, concat_axis=0, tiled=True)]
    pallas_call x1, Pallas kernels: 27.7 us -> 10.4 us  [attend(): pl.pallas_call(attend_kernel, out_shape=(jax.ShapeDtypeStruct((CHIPS, ROW...]
    ppermute x15 -> x12, waiting for transfers between devices: 24.2 us -> 7.72 us  [the longest x1 3.15 us: local(): crossed = lax.ppermute(total[1].astype(BF16), 'tp', CROSS)]
    unnamed x34 -> x10, local copies, waits for them, and re-layouts: 12.7 us -> 1.21 us
    ppermute x15 -> x12, starting transfers between devices: 15.8 us -> 19.2 us  [the longest x4 8.99 us: local(): other = [lax.ppermute(block, 'tp', SWAP) for block in mine]]
    convert_element_type x1, other arithmetic: 0.23 us -> 2.42 us  [local(): sums[dy].astype(BF16)]
  transfers between devices with their start and end apart: 18 -> 15, of which waited for: 8 -> 6; matrix products, arithmetic and copies ran while one was open for 1% -> 6% of each run, Pallas kernels for 15% -> 16%
where the time goes in v2:
time: 94 us; the launch traced here: 93.6 us
  starting transfers between devices  36.4 us (39%)
  waiting for transfers between devices  28.3 us (30%)
  Pallas kernels  21.5 us (23%)
  other arithmetic  4.75 us (5%)
  local copies, waits for them, and re-layouts  1.86 us (2%)
    all_to_all x1, waiting for transfers between devices, local(): lax.all_to_all(packed, 'inst', split_axis=0, concat_axis=0, tiled=True)  18.4 us
    all_to_all x1, starting transfers between devices, local(): lax.all_to_all(packed, 'inst', split_axis=0, concat_axis=0, tiled=True)  11.6 us
    pallas_call x1, Pallas kernels, attend(): pl.pallas_call(attend_kernel, out_shape=(jax.ShapeDtypeStruct((CHIPS, ROW...  10.4 us
    ppermute x4, starting transfers between devices, local(): other = [lax.ppermute(block, 'tp', SWAP) for block in mine]  8.99 us
    pallas_call x2, Pallas kernels, place(): pl.pallas_call(functools.partial(place_kernel, into is not None), out_sha...  5.18 us
    ppermute x3, starting transfers between devices, local(): mine[dy] = lax.ppermute(pair, 'tp', tp_perm(0, 4 - dy, 0))  5.06 us
    ppermute x1, starting transfers between devices, local(): rest = lax.ppermute(half, 'tp', SWAP)  4.57 us
    ppermute x3, starting transfers between devices, local(): lax.ppermute(sums[dy].astype(BF16), 'tp', tp_perm(0, dy, 0))  4.37 us
  transfers between devices with their start and end apart: 15, of which 6 were waited for; matrix products, arithmetic and copies ran while one was open for 6% of the time, Pallas kernels for 16%

profile of v2, /device:TPU:1, one launch (start us, length us, event | category | flops | bytes accessed | tf_op | source)
XLA Modules:
  0.0 93.6 jit_solution(5309053207819304332)
XLA Ops:
  0.6 4.0 %pack.1 = bf16[16,400,128]{2,1,0:T(8,128)(2,1)} custom-call(s32[3,48]{1,0:T(4,128)} %bitcast.21, s32[48]{0:T(128)} %blk.3, s32[1,16]{1,0:T(1,128)} %mv.1, bf16[2,48,2,1024]{3,2,1,0:T(2,128)(2,1)} %nkv.3, bf16[144,2,1,128,128]{4,3,2,1,0:T(8,128)(2,1)} %kv.3), custom_call_target="tpu_custom_call" | custom-call | bytes 4194304 | tf_op jit(solution)/shard_map/pack/pallas_call | solution.py:81
  4.6 11.6 %all-to-all-start = ((bf16[16,400,128]{2,1,0:T(8,128)(2,1)}), bf16[16,400,128]{2,1,0:T(8,128)(2,1)S(1)}, u32[]{:S(2)}, u32[]{:S(2)}) async-start(bf16[16,400,128]{2,1,0:T(8,128)(2,1)} %pack.1), calls=%async_computation | async-start | bytes 3276800 | tf_op jit(solution)/shard_map/all_to_all | solution.py:323
  16.2 10.4 %attend.1 = (bf16[8,96,512]{2,1,0:T(8,128)(2,1)}, f32[8,96,512]{2,1,0:T(8,128)}) custom-call(s32[3,48]{1,0:T(4,128)} %bitcast.22, s32[48]{0:T(128)} %blk.3, bf16[2,48,256]{2,1,0:T(8,128)(2,1)} %q_hbm.1, bf16[2,48,2,1024]{3,2,1,0:T(2,128)(2,1)} %nkv.3, bf16[144,2,1,128,128]{4,3,2,1,0:T(8,128)(2,1)} %kv.3, bf16[256,8192]{1,0:T(8,128)(2,1)} %w.1), custom_call_target="tpu_custom_call" | custom-call | flops 1000000000 | bytes 16777216 | tf_op jit(solution)/shard_map/attend/pallas_call | solution.py:215
  26.7 1.0 %collective-permute-start = (bf16[8,96,512]{2,1,0:T(8,128)(2,1)}, bf16[8,96,512]{2,1,0:T(8,128)(2,1)S(1)}, u32[]{:S(2)}, u32[]{:S(2)}) collective-permute-start(bf16[8,96,512]{2,1,0:T(8,128)(2,1)} %get-tuple-element.7), channel_id=1, source_target_pairs={{0,1},{1,0},{2,3},{3,2},{4,5},{5,4},{6,7},{7,6},{8,9},{9,8},{10,11... | collective-permute-start | bytes 2359304 | tf_op jit(solution)/shard_map/ppermute | solution.py:326
  27.7 2.1 %collective-permute-done = bf16[8,96,512]{2,1,0:T(8,128)(2,1)S(1)} collective-permute-done((bf16[8,96,512]{2,1,0:T(8,128)(2,1)}, bf16[8,96,512]{2,1,0:T(8,128)(2,1)S(1)}, u32[]{:S(2)}, u32[]{:S(2)}) %collective-permute-start) | collective-permute-done | bytes 786464 | tf_op jit(solution)/shard_map/ppermute | solution.py:326
  29.9 2.4 %add_convert_fusion.2 = (bf16[2,96,512]{2,1,0:T(8,128)(2,1)}, bf16[2,96,512]{2,1,0:T(8,128)(2,1)}, bf16[2,96,512]{2,1,0:T(8,128)(2,1)}) fusion(f32[8,96,512]{2,1,0:T(8,128)} %get-tuple-element.6, bf16[8,96,512]{2,1,0:T(8,128)(2,1)S(1)} %collective-permute-done), kind=kLoop, calls=%fused_computation.3 | loop fusion | flops 884736 | bytes 2359296 | tf_op jit(solution)/shard_map/convert_element_type | solution.py:330
  32.3 2.9 %collective-permute-start.1 = (bf16[2,96,512]{2,1,0:T(8,128)(2,1)}, bf16[2,96,512]{2,1,0:T(8,128)(2,1)S(1)}, u32[]{:S(2)}, u32[]{:S(2)}) collective-permute-start(bf16[2,96,512]{2,1,0:T(8,128)(2,1)} %get-tuple-element.12), channel_id=1, source_target_pairs={{0,4},{1,5},{2,6},{3,7},{4,0},{5,1},{6,2},{7,3},{8,12},{9,13},{10,... | collective-permute-start | bytes 589832 | tf_op jit(solution)/shard_map/ppermute | solution.py:330
  35.2 0.8 collective-permute-start.3
  36.0 0.7 collective-permute-start.2
  36.7 18.4 %all-to-all-done.refs_0_ = bf16[16,400,128]{2,1,0:T(8,128)(2,1)S(1)} async-done(((bf16[16,400,128]{2,1,0:T(8,128)(2,1)}), bf16[16,400,128]{2,1,0:T(8,128)(2,1)S(1)}, u32[]{:S(2)}, u32[]{:S(2)}) %all-to-all-start) | async-done | bytes 1638432 | tf_op jit(solution)/shard_map/all_to_all | solution.py:323
  55.1 4.6 %collective-permute-start.13 = (bf16[16,400,128]{2,1,0:T(8,128)(2,1)S(1)}, bf16[16,400,128]{2,1,0:T(8,128)(2,1)S(1)}, u32[]{:S(2)}, u32[]{:S(2)}) collective-permute-start(bf16[16,400,128]{2,1,0:T(8,128)(2,1)S(1)} %all-to-all-done.refs_0_), channel_id=1, source_target_pairs={{0,1},{1,0},{2,3},{3,2},{4,5},{5,4},{6,7},{7,6},{8,9},{9,8},{10,11... | collective-permute-start | bytes 4915208 | tf_op jit(solution)/shard_map/ppermute | solution.py:346
  59.7 1.4 %convert_add_fusion = f32[2,96,512]{2,1,0:T(8,128)S(1)} fusion(bf16[2,96,512]{2,1,0:T(8,128)(2,1)} %collective-permute-done.3, bf16[2,96,512]{2,1,0:T(8,128)(2,1)} %collective-permute-done.2, bf16[2,96,512]{2,1,0:T(8,128)(2,1)S(1)} %collective-permute-done.1, f32[8,96,512]{2,1,0:T(8,128)} %get-tuple-element.6, bf16[8,96,512]{2,1,0:T(8,128)(2,1)} %copy-done.2), kind=kLoop, calls=%fused_computation | loop fusion | flops 786432 | bytes 1572864 | tf_op jit(solution)/shard_map/add | solution.py:333
  61.1 0.4 collective-permute-start.4
  61.5 3.2 %collective-permute-done.4 = bf16[96,512]{1,0:T(8,128)(2,1)S(1)} collective-permute-done((bf16[96,512]{1,0:T(8,128)(2,1)S(1)}, bf16[96,512]{1,0:T(8,128)(2,1)S(1)}, u32[]{:S(2)}, u32[]{:S(2)}) %collective-permute-start.4) | collective-permute-done | bytes 98336 | tf_op jit(solution)/shard_map/ppermute | solution.py:334
  64.6 0.9 add_convert_fusion.3
  65.6 0.0 copy-start.3
  65.6 0.4 collective-permute-start.5
  66.0 3.2 %collective-permute-done.5 = bf16[96,512]{1,0:T(8,128)(2,1)S(1)} collective-permute-done((bf16[96,512]{1,0:T(8,128)(2,1)S(1)}, bf16[96,512]{1,0:T(8,128)(2,1)S(1)}, u32[]{:S(2)}, u32[]{:S(2)}) %collective-permute-start.5) | collective-permute-done | bytes 98336 | tf_op jit(solution)/shard_map/ppermute | solution.py:338
  69.2 1.4 %collective-permute-start.8 = (bf16[2,96,512]{2,1,0:T(8,128)(2,1)S(1)}, bf16[2,96,512]{2,1,0:T(8,128)(2,1)S(1)}, u32[]{:S(2)}, u32[]{:S(2)}) collective-permute-start(bf16[2,96,512]{2,1,0:T(8,128)(2,1)S(1)} %pad_maximum_fusion.refs_0_), channel_id=1, source_target_pairs={{0,2},{1,3},{2,4},{3,5},{4,6},{5,7},{6,0},{7,1},{8,10},{9,11},{10,... | collective-permute-start | bytes 589832 | tf_op jit(solution)/shard_map/ppermute | solution.py:341
  70.5 2.6 %collective-permute-start.7 = (bf16[2,96,512]{2,1,0:T(8,128)(2,1)S(1)}, bf16[2,96,512]{2,1,0:T(8,128)(2,1)S(1)}, u32[]{:S(2)}, u32[]{:S(2)}) collective-permute-start(bf16[2,96,512]{2,1,0:T(8,128)(2,1)S(1)} %pad_maximum_fusion.refs_0_), channel_id=1, source_target_pairs={{0,4},{1,5},{2,6},{3,7},{4,0},{5,1},{6,2},{7,3},{8,12},{9,13},{10,... | collective-permute-start | bytes 589832 | tf_op jit(solution)/shard_map/ppermute | solution.py:341
  73.2 1.1 %collective-permute-start.6 = (bf16[2,96,512]{2,1,0:T(8,128)(2,1)S(1)}, bf16[2,96,512]{2,1,0:T(8,128)(2,1)S(1)}, u32[]{:S(2)}, u32[]{:S(2)}) collective-permute-start(bf16[2,96,512]{2,1,0:T(8,128)(2,1)S(1)} %pad_maximum_fusion.refs_0_), channel_id=1, source_target_pairs={{0,6},{1,7},{2,0},{3,1},{4,2},{5,3},{6,4},{7,5},{8,14},{9,15},{10,... | collective-permute-start | bytes 589832 | tf_op jit(solution)/shard_map/ppermute | solution.py:341
  74.2 3.7 %collective-permute-start.9 = (bf16[2,96,512]{2,1,0:T(8,128)(2,1)S(1)}, bf16[2,96,512]{2,1,0:T(8,128)(2,1)S(1)}, u32[]{:S(2)}, u32[]{:S(2)}) collective-permute-start(bf16[2,96,512]{2,1,0:T(8,128)(2,1)S(1)} %pad_maximum_fusion.refs_0_), channel_id=1, source_target_pairs={{0,1},{1,0},{2,3},{3,2},{4,5},{5,4},{6,7},{7,6},{8,9},{9,8},{10,11... | collective-permute-start | bytes 589832 | tf_op jit(solution)/shard_map/ppermute | solution.py:343
  78.0 3.2 %collective-permute-start.12 = (bf16[2,96,512]{2,1,0:T(8,128)(2,1)S(1)}, bf16[2,96,512]{2,1,0:T(8,128)(2,1)S(1)}, u32[]{:S(2)}, u32[]{:S(2)}) collective-permute-start(bf16[2,96,512]{2,1,0:T(8,128)(2,1)S(1)} %collective-permute-done.8.refs_3_), channel_id=1, source_target_pairs={{0,1},{1,0},{2,3},{3,2},{4,5},{5,4},{6,7},{7,6},{8,9},{9,8},{10,11... | collective-permute-start | bytes 589832 | tf_op jit(solution)/shard_map/ppermute | solution.py:343
  81.1 2.1 %collective-permute-start.11 = (bf16[2,96,512]{2,1,0:T(8,128)(2,1)S(1)}, bf16[2,96,512]{2,1,0:T(8,128)(2,1)S(1)}, u32[]{:S(2)}, u32[]{:S(2)}) collective-permute-start(bf16[2,96,512]{2,1,0:T(8,128)(2,1)S(1)} %collective-permute-done.7.refs_2_), channel_id=1, source_target_pairs={{0,1},{1,0},{2,3},{3,2},{4,5},{5,4},{6,7},{7,6},{8,9},{9,8},{10,11... | collective-permute-start | bytes 589832 | tf_op jit(solution)/shard_map/ppermute | solution.py:343
  83.2 0.0 collective-permute-start.10
  83.3 1.0 %collective-permute-done.11.refs_6_ = bf16[2,96,512]{2,1,0:T(8,128)(2,1)S(1)} collective-permute-done((bf16[2,96,512]{2,1,0:T(8,128)(2,1)S(1)}, bf16[2,96,512]{2,1,0:T(8,128)(2,1)S(1)}, u32[]{:S(2)}, u32[]{:S(2)}) %collective-permute-start.11) | collective-permute-done | bytes 196640 | tf_op jit(solution)/shard_map/ppermute | solution.py:343
  84.3 0.4 collective-permute-done.10.refs_5_
  84.7 1.9 %norm.1 = bf16[96,8192]{1,0:T(8,128)(2,1)} custom-call(bf16[1,8192]{1,0:T(2,128)(2,1)S(1)} %reshape.25.gain, bf16[2,96,512]{2,1,0:T(8,128)(2,1)S(1)} %pad_maximum_fusion.refs_0_, bf16[2,96,512]{2,1,0:T(8,128)(2,1)S(1)} %collective-permute-done.6.refs_1_, bf16[2,96,512]{2,1,0:T(8,128)(2,1)S(1)} %collective-permute-done.7.refs_2_, ...), custom_call_target="tpu_custom_call" | custom-call | flops 3145728 | bytes 3145728 | tf_op jit(solution)/shard_map/norm/pallas_call | solution.py:269
  86.5 0.6 slice.51
  87.2 2.6 %place.2.refs_1_ = bf16[16,3,2,1,128,128]{5,4,3,2,1,0:T(8,128)(2,1)} custom-call(bf16[16,400,128]{2,1,0:T(8,128)(2,1)} %copy-done), custom_call_target="tpu_custom_call" | custom-call | bytes 3145728 | tf_op jit(solution)/shard_map/place/pallas_call | solution.py:296
  89.8 1.2 %copy-done.1 = bf16[16,400,128]{2,1,0:T(8,128)(2,1)} copy-done((bf16[16,400,128]{2,1,0:T(8,128)(2,1)}, bf16[16,400,128]{2,1,0:T(8,128)(2,1)S(1)}, u32[]{:S(2)}) %copy-start.1) | copy-done | bytes 1638424
  91.0 2.6 %place.3 = bf16[16,3,2,1,128,128]{5,4,3,2,1,0:T(8,128)(2,1)} custom-call(bf16[16,400,128]{2,1,0:T(8,128)(2,1)} %copy-done.1, bf16[16,3,2,1,128,128]{5,4,3,2,1,0:T(8,128)(2,1)} %place.2.refs_1_), custom_call_target="tpu_custom_call", output_to_operand_aliasing={{}: (1, {})} | custom-call | bytes 3145728 | tf_op jit(solution)/shard_map/place/pallas_call | solution.py:296
  (21 shorter events, 0.1 us)
Async XLA Ops:
  4.6 50.5 %all-to-all-start = ((bf16[16,400,128]{2,1,0:T(8,128)(2,1)}), bf16[16,400,128]{2,1,0:T(8,128)(2,1)S(1)}, u32[]{:S(2)}, u32[]{:S(2)}) async-start(bf16[16,400,128]{2,1,0:T(8,128)(2,1)} %pack.1), calls=%async_computation | async-start | bytes 3276800 | tf_op jit(solution)/shard_map/all_to_all | solution.py:323
  26.7 3.2 %collective-permute-start = (bf16[8,96,512]{2,1,0:T(8,128)(2,1)}, bf16[8,96,512]{2,1,0:T(8,128)(2,1)S(1)}, u32[]{:S(2)}, u32[]{:S(2)}) collective-permute-start(bf16[8,96,512]{2,1,0:T(8,128)(2,1)} %get-tuple-element.7), channel_id=1, source_target_pairs={{0,1},{1,0},{2,3},{3,2},{4,5},{5,4},{6,7},{7,6},{8,9},{9,8},{10,11... | collective-permute-start | bytes 2359304 | tf_op jit(solution)/shard_map/ppermute | solution.py:326
  29.9 6.8 %copy-start.2 = (bf16[8,96,512]{2,1,0:T(8,128)(2,1)}, bf16[8,96,512]{2,1,0:T(8,128)(2,1)S(1)}, u32[]{:S(2)}) copy-start(bf16[8,96,512]{2,1,0:T(8,128)(2,1)S(1)} %collective-permute-done) | copy-start | bytes 2359300
  32.3 50.9 %copy-start.4 = (bf16[8192]{0:T(1024)(128)(2,1)S(1)}, bf16[8192]{0:T(1024)(128)(2,1)}, u32[]{:S(2)}) copy-start(bf16[8192]{0:T(1024)(128)(2,1)} %param.17) | copy-start | bytes 49156
  32.3 27.4 %collective-permute-start.1 = (bf16[2,96,512]{2,1,0:T(8,128)(2,1)}, bf16[2,96,512]{2,1,0:T(8,128)(2,1)S(1)}, u32[]{:S(2)}, u32[]{:S(2)}) collective-permute-start(bf16[2,96,512]{2,1,0:T(8,128)(2,1)} %get-tuple-element.12), channel_id=1, source_target_pairs={{0,4},{1,5},{2,6},{3,7},{4,0},{5,1},{6,2},{7,3},{8,12},{9,13},{10,... | collective-permute-start | bytes 589832 | tf_op jit(solution)/shard_map/ppermute | solution.py:330
  35.2 24.5 %collective-permute-start.3 = (bf16[2,96,512]{2,1,0:T(8,128)(2,1)}, bf16[2,96,512]{2,1,0:T(8,128)(2,1)}, u32[]{:S(2)}, u32[]{:S(2)}) collective-permute-start(bf16[2,96,512]{2,1,0:T(8,128)(2,1)} %get-tuple-element.13), channel_id=1, source_target_pairs={{0,6},{1,7},{2,0},{3,1},{4,2},{5,3},{6,4},{7,5},{8,14},{9,15},{10,... | collective-permute-start | bytes 589832 | tf_op jit(solution)/shard_map/ppermute | solution.py:330
  36.0 23.7 %collective-permute-start.2 = (bf16[2,96,512]{2,1,0:T(8,128)(2,1)}, bf16[2,96,512]{2,1,0:T(8,128)(2,1)}, u32[]{:S(2)}, u32[]{:S(2)}) collective-permute-start(bf16[2,96,512]{2,1,0:T(8,128)(2,1)} %get-tuple-element.14), channel_id=1, source_target_pairs={{0,2},{1,3},{2,4},{3,5},{4,6},{5,7},{6,0},{7,1},{8,10},{9,11},{10,... | collective-permute-start | bytes 589832 | tf_op jit(solution)/shard_map/ppermute | solution.py:330
  55.1 31.5 %copy-start = (bf16[16,400,128]{2,1,0:T(8,128)(2,1)}, bf16[16,400,128]{2,1,0:T(8,128)(2,1)S(1)}, u32[]{:S(2)}) copy-start(bf16[16,400,128]{2,1,0:T(8,128)(2,1)S(1)} %all-to-all-done.refs_0_) | copy-start | bytes 4915204
  55.1 34.7 %collective-permute-start.13 = (bf16[16,400,128]{2,1,0:T(8,128)(2,1)S(1)}, bf16[16,400,128]{2,1,0:T(8,128)(2,1)S(1)}, u32[]{:S(2)}, u32[]{:S(2)}) collective-permute-start(bf16[16,400,128]{2,1,0:T(8,128)(2,1)S(1)} %all-to-all-done.refs_0_), channel_id=1, source_target_pairs={{0,1},{1,0},{2,3},{3,2},{4,5},{5,4},{6,7},{7,6},{8,9},{9,8},{10,11... | collective-permute-start | bytes 4915208 | tf_op jit(solution)/shard_map/ppermute | solution.py:346
  61.1 3.6 %collective-permute-start.4 = (bf16[96,512]{1,0:T(8,128)(2,1)S(1)}, bf16[96,512]{1,0:T(8,128)(2,1)S(1)}, u32[]{:S(2)}, u32[]{:S(2)}) collective-permute-start(bf16[96,512]{1,0:T(8,128)(2,1)S(1)} %fusion.1), channel_id=1, source_target_pairs={{0,8},{1,9},{2,10},{3,11},{4,12},{5,13},{6,14},{7,15},{8,0},{9,1},... | collective-permute-start | bytes 294920 | tf_op jit(solution)/shard_map/ppermute | solution.py:334
  65.6 21.0 %copy-start.3 = (bf16[2,48,512]{2,1,0:T(8,128)(2,1)}, bf16[2,48,512]{2,1,0:T(8,128)(2,1)S(1)}, u32[]{:S(2)}) copy-start(bf16[2,48,512]{2,1,0:T(8,128)(2,1)S(1)} %add_convert_fusion.3) | copy-start | bytes 294916
  65.6 3.6 %collective-permute-start.5 = (bf16[96,512]{1,0:T(8,128)(2,1)S(1)}, bf16[96,512]{1,0:T(8,128)(2,1)S(1)}, u32[]{:S(2)}, u32[]{:S(2)}) collective-permute-start(bf16[96,512]{1,0:T(8,128)(2,1)S(1)} %bitcast.17), channel_id=1, source_target_pairs={{0,8},{1,9},{2,10},{3,11},{4,12},{5,13},{6,14},{7,15},{8,0},{9,1},... | collective-permute-start | bytes 294920 | tf_op jit(solution)/shard_map/ppermute | solution.py:338
  69.2 8.8 %collective-permute-start.8 = (bf16[2,96,512]{2,1,0:T(8,128)(2,1)S(1)}, bf16[2,96,512]{2,1,0:T(8,128)(2,1)S(1)}, u32[]{:S(2)}, u32[]{:S(2)}) collective-permute-start(bf16[2,96,512]{2,1,0:T(8,128)(2,1)S(1)} %pad_maximum_fusion.refs_0_), channel_id=1, source_target_pairs={{0,2},{1,3},{2,4},{3,5},{4,6},{5,7},{6,0},{7,1},{8,10},{9,11},{10,... | collective-permute-start | bytes 589832 | tf_op jit(solution)/shard_map/ppermute | solution.py:341
  70.5 10.6 %collective-permute-start.7 = (bf16[2,96,512]{2,1,0:T(8,128)(2,1)S(1)}, bf16[2,96,512]{2,1,0:T(8,128)(2,1)S(1)}, u32[]{:S(2)}, u32[]{:S(2)}) collective-permute-start(bf16[2,96,512]{2,1,0:T(8,128)(2,1)S(1)} %pad_maximum_fusion.refs_0_), channel_id=1, source_target_pairs={{0,4},{1,5},{2,6},{3,7},{4,0},{5,1},{6,2},{7,3},{8,12},{9,13},{10,... | collective-permute-start | bytes 589832 | tf_op jit(solution)/shard_map/ppermute | solution.py:341
  73.2 10.1 %collective-permute-start.6 = (bf16[2,96,512]{2,1,0:T(8,128)(2,1)S(1)}, bf16[2,96,512]{2,1,0:T(8,128)(2,1)S(1)}, u32[]{:S(2)}, u32[]{:S(2)}) collective-permute-start(bf16[2,96,512]{2,1,0:T(8,128)(2,1)S(1)} %pad_maximum_fusion.refs_0_), channel_id=1, source_target_pairs={{0,6},{1,7},{2,0},{3,1},{4,2},{5,3},{6,4},{7,5},{8,14},{9,15},{10,... | collective-permute-start | bytes 589832 | tf_op jit(solution)/shard_map/ppermute | solution.py:341
  74.2 9.0 %collective-permute-start.9 = (bf16[2,96,512]{2,1,0:T(8,128)(2,1)S(1)}, bf16[2,96,512]{2,1,0:T(8,128)(2,1)S(1)}, u32[]{:S(2)}, u32[]{:S(2)}) collective-permute-start(bf16[2,96,512]{2,1,0:T(8,128)(2,1)S(1)} %pad_maximum_fusion.refs_0_), channel_id=1, source_target_pairs={{0,1},{1,0},{2,3},{3,2},{4,5},{5,4},{6,7},{7,6},{8,9},{9,8},{10,11... | collective-permute-start | bytes 589832 | tf_op jit(solution)/shard_map/ppermute | solution.py:343
  78.0 5.3 %collective-permute-start.12 = (bf16[2,96,512]{2,1,0:T(8,128)(2,1)S(1)}, bf16[2,96,512]{2,1,0:T(8,128)(2,1)S(1)}, u32[]{:S(2)}, u32[]{:S(2)}) collective-permute-start(bf16[2,96,512]{2,1,0:T(8,128)(2,1)S(1)} %collective-permute-done.8.refs_3_), channel_id=1, source_target_pairs={{0,1},{1,0},{2,3},{3,2},{4,5},{5,4},{6,7},{7,6},{8,9},{9,8},{10,11... | collective-permute-start | bytes 589832 | tf_op jit(solution)/shard_map/ppermute | solution.py:343
  81.1 3.2 %collective-permute-start.11 = (bf16[2,96,512]{2,1,0:T(8,128)(2,1)S(1)}, bf16[2,96,512]{2,1,0:T(8,128)(2,1)S(1)}, u32[]{:S(2)}, u32[]{:S(2)}) collective-permute-start(bf16[2,96,512]{2,1,0:T(8,128)(2,1)S(1)} %collective-permute-done.7.refs_2_), channel_id=1, source_target_pairs={{0,1},{1,0},{2,3},{3,2},{4,5},{5,4},{6,7},{7,6},{8,9},{9,8},{10,11... | collective-permute-start | bytes 589832 | tf_op jit(solution)/shard_map/ppermute | solution.py:343
  83.2 1.4 %collective-permute-start.10 = (bf16[2,96,512]{2,1,0:T(8,128)(2,1)S(1)}, bf16[2,96,512]{2,1,0:T(8,128)(2,1)S(1)}, u32[]{:S(2)}, u32[]{:S(2)}) collective-permute-start(bf16[2,96,512]{2,1,0:T(8,128)(2,1)S(1)} %collective-permute-done.6.refs_1_), channel_id=1, source_target_pairs={{0,1},{1,0},{2,3},{3,2},{4,5},{5,4},{6,7},{7,6},{8,9},{9,8},{10,11... | collective-permute-start | bytes 589832 | tf_op jit(solution)/shard_map/ppermute | solution.py:343
  89.8 1.2 %copy-start.1 = (bf16[16,400,128]{2,1,0:T(8,128)(2,1)}, bf16[16,400,128]{2,1,0:T(8,128)(2,1)S(1)}, u32[]{:S(2)}) copy-start(bf16[16,400,128]{2,1,0:T(8,128)(2,1)S(1)} %collective-permute-done.13.refs_0_) | copy-start | bytes 4915204

commit v3 on v2

v3 whole, which is shorter than its diff:
```python
import functools

import jax
import jax.numpy as jnp
from jax import lax
from jax.experimental import pallas as pl
from jax.experimental.pallas import tpu as pltpu
from jax.sharding import PartitionSpec as P

F32 = jnp.float32
BF16 = jnp.bfloat16
EPSILON = 1e-05
MASKED = -1e30

SLOTS = 48
MAXB = 3
PAGE = 128
HD = 128
STEPS = 2
INST = 16
CHIPS = 8
ROWS = STEPS * SLOTS
D = 8192
SHARE = 512
PAGES = SLOTS * MAXB
TOK = MAXB * PAGE
MSG = TOK + 16
Z = 8
SHIFTS = [(dx, dy) for dy in range(4) for dx in range(2)]


def any_spec():
    return pl.BlockSpec(memory_space=pl.ANY)


def smem_spec():
    return pl.BlockSpec(memory_space=pltpu.SMEM)


def vmem_spec():
    return pl.BlockSpec(memory_space=pltpu.VMEM)


def in_hbm(x):
    return pltpu.with_memory_space_constraint(x, pltpu.HBM)


def in_vmem(x):
    return pltpu.with_memory_space_constraint(x, pltpu.VMEM)


def params(mib):
    return pltpu.CompilerParams(vmem_limit_bytes=mib << 20)


def pack_kernel(tbl, blk, mv, nkv, kv, near, far, fresh, stage, sems, fsem):
    tp = lax.axis_index("tp")
    core = lax.rem(tp, 2)
    side = lax.rem(lax.axis_index("inst"), 2)
    fcopy = pltpu.make_async_copy(
        nkv.at[:, :, :, pl.ds(pl.multiple_of(lax.div(tp, 2) * HD, HD), HD)], fresh, fsem
    )
    fcopy.start()

    def page_copy(out, i, z, b, page):
        return pltpu.make_async_copy(
            kv.at[page, core, 0], out.at[z, pl.ds(b * PAGE, PAGE)], sems.at[(i * Z + z) * MAXB + b]
        )

    groups = [
        (out, i, z, mv[0, 2 * z + (side if i == 0 else 1 - side)])
        for i, out in enumerate((near, far))
        for z in range(Z)
    ]
    for out, i, z, m in groups:
        for b in range(MAXB):
            page_copy(out, i, z, b, tbl[b, m]).start()
    stage[...] = jnp.zeros_like(stage)
    fcopy.wait()
    for out, i, z, m in groups:
        stage[i, z, 0:2] = fresh[0, m].astype(F32)
        stage[i, z, 2:4] = fresh[1, m].astype(F32)
    near[:, TOK:MSG] = stage[0].astype(BF16)
    far[:, TOK:MSG] = stage[1].astype(BF16)
    for out, i, z, m in groups:
        count = blk[m]
        for b in range(MAXB):
            page_copy(out, i, z, b, 0).wait()
            if b > 0:
                @pl.when(b >= count)
                def _():
                    out[z, b * PAGE:(b + 1) * PAGE] = jnp.zeros((PAGE, HD), BF16)


def pack(table, blocks, moves, new_kv, kv_pages):
    return pl.pallas_call(
        pack_kernel,
        out_shape=(pltpu.VMEM((Z, MSG, HD), BF16),) * 2,
        in_specs=[smem_spec()] * 3 + [any_spec()] * 2,
        out_specs=(vmem_spec(),) * 2,
        scratch_shapes=[
            pltpu.VMEM((STEPS, SLOTS, 2, HD), BF16),
            pltpu.VMEM((2, Z, 16, HD), F32),
            pltpu.SemaphoreType.DMA((2 * Z * MAXB,)),
            pltpu.SemaphoreType.DMA,
        ],
        compiler_params=params(16),
        cost_estimate=pl.CostEstimate(flops=0, bytes_accessed=4 << 20, transcendentals=0),
        name="pack",
    )(in_hbm(table), in_hbm(blocks), in_hbm(moves), in_hbm(new_kv), in_hbm(kv_pages))


def place_of(tp):
    chip = lax.div(tp, 2)
    return lax.rem(tp, 2), lax.div(chip, 4), lax.rem(chip, 4)


def block_of(x, y, k, parity):
    dx, dy = SHIFTS[k]
    return (lax.rem(x + dx, 2) * 4 + lax.rem(y + dy, 4)) * 2 + parity


def attend_kernel(tbl, blk, q_hbm, nkv, kv, w, send, heads, wb, kvb, fresh, qs, ks, sc, ob, q, kvsem, wsem, fsem, qsem):
    tp = lax.axis_index("tp")
    core, x, y = place_of(tp)
    qcopy = pltpu.make_async_copy(q_hbm, q, qsem)
    qcopy.start()
    fcopy = pltpu.make_async_copy(
        nkv.at[:, :, :, pl.ds(pl.multiple_of(lax.div(tp, 2) * HD, HD), HD)], fresh, fsem
    )
    fcopy.start()
    pools = [pltpu.make_async_copy(kv.at[:, i, 0], kvb.at[i], kvsem.at[i]) for i in range(2)]
    for copy in pools:
        copy.start()
    wcopy = pltpu.make_async_copy(w, wb, wsem)
    wcopy.start()
    qcopy.wait()
    for t in range(STEPS):
        for g in range(2):
            qs[pl.ds(t * 2 + g, SLOTS, stride=4), :] = q[t, :, g * HD:(g + 1) * HD].astype(F32)
    fcopy.wait()
    fr = fresh[...].astype(F32)
    for u in range(STEPS):
        for c in range(2):
            val = fr[u, :, c, :]
            for j in range(4):
                ks[u * 2 + c, pl.ds(j, SLOTS, stride=4), :] = val

    scaling = HD ** (-0.5)
    row_a = lax.broadcasted_iota(jnp.int32, (8, TOK), 0) < 4
    block_no = lax.div(lax.broadcasted_iota(jnp.int32, (8, TOK), 1), PAGE)

    def score_pair(p, carry):
        rows = pl.ds(pl.multiple_of(p * 8, 8), 8)
        q8 = qs[rows, :].astype(BF16)
        parts = []
        for h in range(2):
            keys = jnp.concatenate([kvb[0, tbl[b, 2 * p + h]] for b in range(MAXB)], axis=0)
            parts.append(lax.dot_general(q8, keys, (((1,), (1,)), ((), ())), preferred_element_type=F32))
        s8 = jnp.where(row_a, parts[0], parts[1]) * scaling
        count = jnp.where(row_a, blk[2 * p], blk[2 * p + 1])
        sc[rows, :] = jnp.where(block_no < count, s8, MASKED)
        return carry

    pools[0].wait()
    lax.fori_loop(0, SLOTS // 2, score_pair, 0, unroll=True)

    qa = qs[...]
    f0 = jnp.sum(qa * ks[0], axis=-1, keepdims=True) * scaling
    f1 = jnp.sum(qa * ks[2], axis=-1, keepdims=True) * scaling
    late = lax.rem(lax.broadcasted_iota(jnp.int32, (SLOTS * 4, 1), 0), 4) >= 2
    f1 = jnp.where(late, f1, MASKED)
    s = sc[...]
    top = jnp.maximum(jnp.max(s, axis=-1, keepdims=True), jnp.maximum(f0, f1))
    e = jnp.exp(s - top)
    e0 = jnp.exp(f0 - top)
    e1 = jnp.exp(f1 - top)
    total = jnp.sum(e, axis=-1, keepdims=True) + e0 + e1
    sc[...] = e / total
    w0 = (e0 / total).astype(BF16).astype(F32)
    w1 = (e1 / total).astype(BF16).astype(F32)
    ob[...] = w0 * ks[1] + w1 * ks[3]
    row_o = lax.broadcasted_iota(jnp.int32, (8, HD), 0) < 4

    def mix_pair(p, carry):
        rows = pl.ds(pl.multiple_of(p * 8, 8), 8)
        w8 = sc[rows, :].astype(BF16)
        parts = []
        for h in range(2):
            vals = jnp.concatenate([kvb[1, tbl[b, 2 * p + h]] for b in range(MAXB)], axis=0)
            parts.append(jnp.dot(w8, vals, preferred_element_type=F32))
        ob[rows, :] += jnp.where(row_o, parts[0], parts[1])
        return carry

    pools[1].wait()
    lax.fori_loop(0, SLOTS // 2, mix_pair, 0, unroll=True)

    for t in range(STEPS):
        for g in range(2):
            heads[t * SLOTS:(t + 1) * SLOTS, g * HD:(g + 1) * HD] = ob[
                pl.ds(t * 2 + g, SLOTS, stride=4), :
            ].astype(BF16)
    wcopy.wait()
    project(heads, wb, send, x, y, 1 - core)


def project(heads, wb, out, x, y, parity):
    rows = heads[...]
    for k in range(CHIPS):
        cols = pl.ds(pl.multiple_of(block_of(x, y, k, parity) * SHARE, SHARE), SHARE)
        out[k] = jnp.dot(rows, wb[:, cols], preferred_element_type=F32).astype(out.dtype)


def attend(table, blocks, query, new_kv, kv_pages, out_weight):
    return pl.pallas_call(
        attend_kernel,
        out_shape=(
            pltpu.VMEM((CHIPS, ROWS, SHARE), BF16),
            pltpu.VMEM((ROWS, 2 * HD), BF16),
            pltpu.VMEM((2 * HD, D), BF16),
        ),
        in_specs=[smem_spec()] * 2 + [any_spec()] * 4,
        out_specs=(vmem_spec(),) * 3,
        scratch_shapes=[
            pltpu.VMEM((2, PAGES, PAGE, HD), BF16),
            pltpu.VMEM((STEPS, SLOTS, 2, HD), BF16),
            pltpu.VMEM((SLOTS * 4, HD), F32),
            pltpu.VMEM((4, SLOTS * 4, HD), F32),
            pltpu.VMEM((SLOTS * 4, TOK), F32),
            pltpu.VMEM((SLOTS * 4, HD), F32),
            pltpu.VMEM((STEPS, SLOTS, 2 * HD), BF16),
            pltpu.SemaphoreType.DMA((2,)),
            pltpu.SemaphoreType.DMA,
            pltpu.SemaphoreType.DMA,
            pltpu.SemaphoreType.DMA,
        ],
        compiler_params=params(32),
        cost_estimate=pl.CostEstimate(flops=10**10, bytes_accessed=64 << 20, transcendentals=10**5),
        name="attend",
    )(in_hbm(table), in_hbm(blocks), in_hbm(query), in_hbm(new_kv), in_hbm(kv_pages), in_hbm(out_weight))


def own_kernel(heads, wb, keep):
    core, x, y = place_of(lax.axis_index("tp"))
    project(heads, wb, keep, x, y, core)


def own(heads, wb):
    return pl.pallas_call(
        own_kernel,
        out_shape=pltpu.VMEM((CHIPS, ROWS, SHARE), F32),
        in_specs=[vmem_spec()] * 2,
        out_specs=vmem_spec(),
        compiler_params=params(16),
        cost_estimate=pl.CostEstimate(flops=1, bytes_accessed=1, transcendentals=0),
        name="own",
    )(in_vmem(heads), in_vmem(wb))


def finish_kernel(gain, near, far, far_other, into, *refs):
    blocks, (normed, arrived, tail, buf, sem, nsem) = refs[:8], refs[8:]
    core, x, y = place_of(lax.axis_index("tp"))
    side = lax.rem(lax.axis_index("inst"), 2)
    copies = place_copies(far, far_other, arrived, 1 - side, sem)
    squares = jnp.zeros((ROWS, SHARE), F32)
    for ref in blocks:
        for dx in range(2):
            v = ref[dx].astype(F32)
            squares = squares + v * v
    scale = lax.rsqrt(jnp.sum(squares, axis=-1, keepdims=True) / D + EPSILON)
    for part in range(2):
        for k in range(CHIPS):
            block = block_of(x, y, k, core if part == 0 else 1 - core)
            at = pl.ds(pl.multiple_of(block * SHARE, SHARE), SHARE)
            v = blocks[part * 4 + k // 2][k % 2].astype(F32)
            buf[:, at] = (v * scale * gain[:, at].astype(F32)).astype(BF16)
            copy = pltpu.make_async_copy(buf.at[:, at], normed.at[:, at], nsem.at[part * CHIPS + k])
            copy.start()
            copies.append(copy)
    for refs, way in ((near, side), (far, 1 - side)):
        for z in range(Z):
            tail[2 * z + way] = refs[z, TOK:MSG].astype(F32)[0:4].astype(BF16)
    for copy in copies:
        copy.wait()


def finish(gain, near, far, far_other, into, mine, other):
    return pl.pallas_call(
        finish_kernel,
        out_shape=(
            pltpu.HBM((ROWS, D), BF16),
            pltpu.HBM((INST, MAXB, 2, PAGE, HD), BF16),
            jax.ShapeDtypeStruct((INST, 4, HD), BF16),
        ),
        in_specs=[vmem_spec()] * 4 + [any_spec()] + [vmem_spec()] * 8,
        out_specs=(any_spec(), any_spec(), vmem_spec()),
        scratch_shapes=[
            pltpu.VMEM((ROWS, D), BF16),
            pltpu.SemaphoreType.DMA((2 * Z * MAXB,)),
            pltpu.SemaphoreType.DMA((2 * CHIPS,)),
        ],
        input_output_aliases={4: 1},
        compiler_params=params(24),
        cost_estimate=pl.CostEstimate(flops=4 * ROWS * D, bytes_accessed=8 << 20, transcendentals=0),
        name="finish",
    )(gain.reshape(1, D), near, far, far_other, into, *mine, *other)


def place_copies(mine, other, out, way, sems):
    core = lax.rem(lax.axis_index("tp"), 2)
    copies = []
    for part, (src, half) in enumerate(((mine, core), (other, 1 - core))):
        for z in range(Z):
            for b in range(MAXB):
                copies.append(
                    pltpu.make_async_copy(
                        src.at[z, pl.ds(b * PAGE, PAGE)],
                        out.at[2 * z + way, b, half],
                        sems.at[(part * Z + z) * MAXB + b],
                    )
                )
                copies[-1].start()
    return copies


def place_kernel(mine, other, out, sems):
    side = lax.rem(lax.axis_index("inst"), 2)
    for copy in place_copies(mine, other, out, side, sems):
        copy.wait()


def place(mine, other):
    return pl.pallas_call(
        place_kernel,
        out_shape=pltpu.HBM((INST, MAXB, 2, PAGE, HD), BF16),
        in_specs=[vmem_spec()] * 2,
        out_specs=any_spec(),
        scratch_shapes=[pltpu.SemaphoreType.DMA((2 * Z * MAXB,))],
        compiler_params=params(8),
        cost_estimate=pl.CostEstimate(flops=0, bytes_accessed=3 << 20, transcendentals=0),
        name="place",
    )(mine, other)


def tp_perm(dx, dy, dc):
    return [
        (k, ((k // 8) ^ dx) * 8 + ((k // 2 % 4 + dy) % 4) * 2 + ((k % 2) ^ dc)) for k in range(16)
    ]


SWAP = tp_perm(0, 0, 1)
CROSS = tp_perm(1, 0, 0)
AROUND = (2, 1, 3)


Z_GROUPS = [[2 * z + side for z in range(Z)] for side in range(2)]
SIDES = [(k, k ^ 1) for k in range(INST)]


def along_z(x):
    return lax.all_to_all(x, "inst", 0, 0, tiled=True, axis_index_groups=Z_GROUPS)


def after(x, *values):
    return lax.optimization_barrier((x, *values))[0]


def local(query, new_kv, residual, kv_pages, block_table, blocks, moves, out_weight, norm_gain):
    table = block_table.T
    own_rows = residual.reshape(ROWS, SHARE)
    peer_rows = lax.ppermute(own_rows, "tp", CROSS)
    near, far = pack(table, blocks, moves, new_kv, kv_pages)
    far = lax.ppermute(far, "inst", SIDES)
    near = along_z(near)

    send, heads, weight = attend(table, blocks, query, new_kv, kv_pages, out_weight)
    got = after(lax.ppermute(send, "tp", SWAP), far)
    keep = own(heads, weight)
    sums = [
        keep[2 * dy:2 * dy + 2] + got[2 * dy:2 * dy + 2].astype(F32) for dy in range(4)
    ]
    terms = [lax.ppermute(sums[dy].astype(BF16), "tp", tp_perm(0, dy, 0)) for dy in AROUND]
    terms[0] = after(terms[0], near)
    far = along_z(after(far, sums[1], near))
    total = sums[0]
    for term in terms:
        total = total + term.astype(F32)
    part = total.astype(BF16)
    cross = lax.ppermute(part, "tp", CROSS)
    pair = jnp.stack(
        [
            (rows.astype(F32) + (part[dx].astype(F32) + cross[1 - dx].astype(F32))).astype(BF16)
            for dx, rows in enumerate((own_rows, peer_rows))
        ]
    )
    hidden = pair[0].reshape(STEPS, SLOTS, SHARE)
    mine = {0: pair}
    for dy in AROUND:
        mine[dy] = lax.ppermute(pair, "tp", tp_perm(0, 4 - dy, 0))
    mine = [mine[dy] for dy in range(4)]
    arrived = place(near, lax.ppermute(after(near, part), "tp", SWAP))
    mine[2], arrived = lax.optimization_barrier((mine[2], arrived))
    far = after(far, *mine)
    far_other = lax.ppermute(far, "tp", SWAP)
    other = [lax.ppermute(block, "tp", SWAP) for block in mine]
    normed, arrived, tail = finish(norm_gain, near, far, far_other, arrived, mine, other)
    return (
        hidden,
        normed.reshape(STEPS, SLOTS, D),
        arrived.reshape(INST, MAXB, 2, 1, PAGE, HD),
        tail.reshape(INST, STEPS, 2, 1, HD),
    )


def solution(mesh):
    in_specs = (
        P(None, "inst", "tp"),
        P(None, "inst", None, None),
        P(None, "inst", "tp"),
        P("inst", None, "tp", None, None),
        P("inst", None),
        P("inst"),
        P("inst", None),
        P("tp", None),
        P(),
    )
    out_specs = (
        P(None, "inst", "tp"),
        P(None, "inst", None),
        P("inst", None, None, "tp", None, None),
        P("inst", None, None, "tp", None),
    )
    return jax.shard_map(local, mesh=mesh, in_specs=in_specs, out_specs=out_specs, check_vma=False)
```

time: 94 us -> 78.8 us (0.84)
  waiting for transfers between devices: 28.3 us -> 14.4 us
  starting transfers between devices: 36.4 us -> 42.7 us
  Pallas kernels: 21.5 us -> 16.7 us
  local copies, waits for them, and re-layouts: 1.86 us -> 0.04 us
  other arithmetic: 4.75 us -> 3.77 us
    all_to_all x1 -> x2, waiting for transfers between devices: 18.4 us -> 0.01 us  [along_z(): lax.all_to_all(x, 'inst', 0, 0, tiled=True, axis_index_groups=Z_GROUPS)]
    ppermute x4, starting transfers between devices: 8.99 us -> 1.28 us  [local(): other = [lax.ppermute(block, 'tp', SWAP) for block in mine]]
    ppermute x4 -> x6, starting transfers between devices: 6.41 us -> 12.7 us  [the longest x1 3.84 us: local(): arrived = place(near, lax.ppermute(after(near, part), 'tp', SWAP))]
    pallas_call x5, Pallas kernels: 21.5 us -> 16.7 us  [the longest x1 7.85 us: attend(): pl.pallas_call(attend_kernel, out_shape=(pltpu.VMEM((CHIPS, ROWS, SHARE),...]
    ppermute x3, waiting for transfers between devices: 0.01 us -> 4.83 us  [local(): mine[dy] = lax.ppermute(pair, 'tp', tp_perm(0, 4 - dy, 0))]
    all_to_all x1 -> x2, starting transfers between devices: 11.6 us -> 15.4 us  [along_z(): lax.all_to_all(x, 'inst', 0, 0, tiled=True, axis_index_groups=Z_GROUPS)]
    ppermute x3, starting transfers between devices: 5.06 us -> 7.73 us  [local(): mine[dy] = lax.ppermute(pair, 'tp', tp_perm(0, 4 - dy, 0))]
    convert_element_type x1, other arithmetic: 2.42 us -> 0.9 us  [local(): sums[dy].astype(BF16)]
  transfers between devices with their start and end apart: 15 -> 18, of which waited for: 6 -> 8; matrix products, arithmetic and copies ran while one was open for 6% -> 5% of each run, Pallas kernels for 16% -> 13%
where the time goes in v3:
time: 78.8 us; the launch traced here: 78.4 us
  starting transfers between devices  42.7 us (54%)
  Pallas kernels  16.7 us (21%)
  waiting for transfers between devices  14.4 us (18%)
  other arithmetic  3.77 us (5%)
  between operations  0.91 us (1%)
    all_to_all x2, starting transfers between devices, along_z(): lax.all_to_all(x, 'inst', 0, 0, tiled=True, axis_index_groups=Z_GROUPS)  15.4 us
    pallas_call x1, Pallas kernels, attend(): pl.pallas_call(attend_kernel, out_shape=(pltpu.VMEM((CHIPS, ROWS, SHARE),...  7.85 us
    ppermute x3, starting transfers between devices, local(): mine[dy] = lax.ppermute(pair, 'tp', tp_perm(0, 4 - dy, 0))  7.73 us
    ppermute x1, waiting for transfers between devices, local(): far = lax.ppermute(far, 'inst', SIDES)  6.46 us
    ppermute x3, starting transfers between devices, local(): lax.ppermute(sums[dy].astype(BF16), 'tp', tp_perm(0, dy, 0))  5.59 us
    ppermute x3, waiting for transfers between devices, local(): mine[dy] = lax.ppermute(pair, 'tp', tp_perm(0, 4 - dy, 0))  4.83 us
    ppermute x1, starting transfers between devices, local(): arrived = place(near, lax.ppermute(after(near, part), 'tp', SWAP))  3.84 us
    pallas_call x1, Pallas kernels, pack(): pl.pallas_call(pack_kernel, out_shape=(pltpu.VMEM((Z, MSG, HD), BF16),) *...  3.72 us
  transfers between devices with their start and end apart: 18, of which 8 were waited for; matrix products, arithmetic and copies ran while one was open for 5% of the time, Pallas kernels for 13%

profile of v3, /device:TPU:1, one launch (start us, length us, event | category | flops | bytes accessed | tf_op | source)
XLA Modules:
  0.0 78.4 jit_solution(5050240549133784978)
XLA Ops:
  0.6 3.7 %pack.1 = (bf16[8,400,128]{2,1,0:T(8,128)(2,1)}, bf16[8,400,128]{2,1,0:T(8,128)(2,1)S(1)}) custom-call(s32[3,48]{1,0:T(4,128)} %bitcast.27, s32[48]{0:T(128)} %blk.3, s32[1,16]{1,0:T(1,128)} %mv.1, bf16[2,48,2,1024]{3,2,1,0:T(2,128)(2,1)} %nkv.3, bf16[144,2,1,128,128]{4,3,2,1,0:T(8,128)(2,1)} %kv.3), custom_call_target="tpu_custom_call" | custom-call | bytes 4194304 | tf_op jit(solution)/shard_map/pack/pallas_call | solution.py:96
  4.4 9.0 %all-to-all-start = ((bf16[8,400,128]{2,1,0:T(8,128)(2,1)}), bf16[8,400,128]{2,1,0:T(8,128)(2,1)S(1)}, u32[]{:S(2)}, u32[]{:S(2)}) async-start(bf16[8,400,128]{2,1,0:T(8,128)(2,1)} %get-tuple-element.24), calls=%async_computation | async-start | bytes 1638400 | tf_op jit(solution)/shard_map/all_to_all | solution.py:361
  13.4 2.7 %collective-permute-start.1 = (bf16[8,400,128]{2,1,0:T(8,128)(2,1)S(1)}, bf16[8,400,128]{2,1,0:T(8,128)(2,1)S(1)}, u32[]{:S(2)}, u32[]{:S(2)}) collective-permute-start(bf16[8,400,128]{2,1,0:T(8,128)(2,1)S(1)} %get-tuple-element.22), channel_id=1, source_target_pairs={{0,16},{16,0},{32,48},{48,32},{64,80},{80,64},{96,112},{112,96},{1... | collective-permute-start | bytes 2457608 | tf_op jit(solution)/shard_map/ppermute | solution.py:373
  16.1 7.8 %attend.1 = (bf16[8,96,512]{2,1,0:T(8,128)(2,1)S(1)}, bf16[96,256]{1,0:T(8,128)(2,1)S(1)}, bf16[256,8192]{1,0:T(8,128)(2,1)S(1)}) custom-call(s32[3,48]{1,0:T(4,128)} %bitcast.28, s32[48]{0:T(128)} %blk.3, bf16[2,48,256]{2,1,0:T(8,128)(2,1)} %q_hbm.1, bf16[2,48,2,1024]{3,2,1,0:T(2,128)(2,1)} %nkv.3, bf16[144,2,1,128,128]{4,3,2,1,0:T(8,128)(2,1)} %kv.3, ...), custom_call_target="tpu_custom_call" | custom-call | flops 10000000000 | bytes 67108864 | tf_op jit(solution)/shard_map/attend/pallas_call | solution.py:215
  24.0 1.3 %collective-permute-start = (bf16[8,96,512]{2,1,0:T(8,128)(2,1)S(1)}, bf16[8,96,512]{2,1,0:T(8,128)(2,1)S(1)}, u32[]{:S(2)}, u32[]{:S(2)}) collective-permute-start(bf16[8,96,512]{2,1,0:T(8,128)(2,1)S(1)} %get-tuple-element.21), channel_id=1, source_target_pairs={{0,1},{1,0},{2,3},{3,2},{4,5},{5,4},{6,7},{7,6},{8,9},{9,8},{10,11... | collective-permute-start | bytes 2359304 | tf_op jit(solution)/shard_map/ppermute | solution.py:377
  25.3 0.5 own.1
  25.8 1.4 %collective-permute-done = bf16[8,96,512]{2,1,0:T(8,128)(2,1)S(1)} collective-permute-done((bf16[8,96,512]{2,1,0:T(8,128)(2,1)S(1)}, bf16[8,96,512]{2,1,0:T(8,128)(2,1)S(1)}, u32[]{:S(2)}, u32[]{:S(2)}) %collective-permute-start) | collective-permute-done | bytes 786464 | tf_op jit(solution)/shard_map/ppermute | solution.py:377
  27.2 6.5 %collective-permute-done.1 = bf16[8,400,128]{2,1,0:T(8,128)(2,1)S(1)} collective-permute-done((bf16[8,400,128]{2,1,0:T(8,128)(2,1)S(1)}, bf16[8,400,128]{2,1,0:T(8,128)(2,1)S(1)}, u32[]{:S(2)}, u32[]{:S(2)}) %collective-permute-start.1) | collective-permute-done | bytes 819232 | tf_op jit(solution)/shard_map/ppermute | solution.py:373
  33.7 0.9 %fusion.1 = (bf16[2,96,512]{2,1,0:T(8,128)(2,1)}, bf16[2,96,512]{2,1,0:T(8,128)(2,1)S(1)}) fusion(f32[8,96,512]{2,1,0:T(8,128)S(1)} %own.1, bf16[8,96,512]{2,1,0:T(8,128)(2,1)S(1)} %collective-permute-done), kind=kLoop, calls=%fused_computation.4 | loop fusion | flops 589824 | bytes 1572864 | tf_op jit(solution)/shard_map/convert_element_type | solution.py:382
  34.6 2.9 %collective-permute-start.2 = (bf16[2,96,512]{2,1,0:T(8,128)(2,1)}, bf16[2,96,512]{2,1,0:T(8,128)(2,1)}, u32[]{:S(2)}, u32[]{:S(2)}) collective-permute-start(bf16[2,96,512]{2,1,0:T(8,128)(2,1)} %get-tuple-element.38), channel_id=1, source_target_pairs={{0,4},{1,5},{2,6},{3,7},{4,0},{5,1},{6,2},{7,3},{8,12},{9,13},{10,... | collective-permute-start | bytes 589832 | tf_op jit(solution)/shard_map/ppermute | solution.py:382
  37.5 0.7 slice_add_fusion.1
  38.2 0.4 collective-permute-start.3
  38.6 2.3 %collective-permute-start.4 = (bf16[2,96,512]{2,1,0:T(8,128)(2,1)S(1)}, bf16[2,96,512]{2,1,0:T(8,128)(2,1)}, u32[]{:S(2)}, u32[]{:S(2)}) collective-permute-start(bf16[2,96,512]{2,1,0:T(8,128)(2,1)S(1)} %get-tuple-element.39), channel_id=1, source_target_pairs={{0,6},{1,7},{2,0},{3,1},{4,2},{5,3},{6,4},{7,5},{8,14},{9,15},{10,... | collective-permute-start | bytes 589832 | tf_op jit(solution)/shard_map/ppermute | solution.py:382
  40.9 6.4 %all-to-all-start.1 = ((bf16[8,400,128]{2,1,0:T(8,128)(2,1)}), bf16[8,400,128]{2,1,0:T(8,128)(2,1)S(1)}, u32[]{:S(2)}, u32[]{:S(2)}) async-start(bf16[8,400,128]{2,1,0:T(8,128)(2,1)} %copy-done), calls=%async_computation.1 | async-start | bytes 1638400 | tf_op jit(solution)/shard_map/all_to_all | solution.py:361
  47.3 1.4 %fusion.5 = bf16[2,96,512]{2,1,0:T(8,128)(2,1)S(1)} fusion(f32[8,96,512]{2,1,0:T(8,128)S(1)} %own.1, bf16[2,96,512]{2,1,0:T(8,128)(2,1)} %collective-permute-done.4, bf16[2,96,512]{2,1,0:T(8,128)(2,1)} %collective-permute-done.3, bf16[2,96,512]{2,1,0:T(8,128)(2,1)} %collective-permute-done.2, bf16[8,96,512]{2,1,0:T(8,128)(2,1)} %copy-done.1), kind=kLoop, calls=%fused_computation.9 | loop fusion | flops 884736 | bytes 1376256 | tf_op jit(solution)/shard_map/convert_element_type | solution.py:388
  48.7 1.3 %collective-permute-start.5 = (bf16[2,96,512]{2,1,0:T(8,128)(2,1)S(1)}, bf16[2,96,512]{2,1,0:T(8,128)(2,1)S(1)}, u32[]{:S(2)}, u32[]{:S(2)}) collective-permute-start(bf16[2,96,512]{2,1,0:T(8,128)(2,1)S(1)} %fusion.5), channel_id=1, source_target_pairs={{0,8},{1,9},{2,10},{3,11},{4,12},{5,13},{6,14},{7,15},{8,0},{9,1},... | collective-permute-start | bytes 589832 | tf_op jit(solution)/shard_map/ppermute | solution.py:389
  50.2 3.8 %collective-permute-start.9 = (bf16[8,400,128]{2,1,0:T(8,128)(2,1)S(1)}, bf16[8,400,128]{2,1,0:T(8,128)(2,1)S(1)}, u32[]{:S(2)}, u32[]{:S(2)}) collective-permute-start(bf16[8,400,128]{2,1,0:T(8,128)(2,1)S(1)} %all-to-all-done.mine.near), channel_id=1, source_target_pairs={{0,1},{1,0},{2,3},{3,2},{4,5},{5,4},{6,7},{7,6},{8,9},{9,8},{10,11... | collective-permute-start | bytes 2457608 | tf_op jit(solution)/shard_map/ppermute | solution.py:401
  54.1 0.5 collective-permute-done.6
  54.7 5.1 %collective-permute-start.8 = (bf16[2,96,512]{2,1,0:T(8,128)(2,1)S(1)}, bf16[2,96,512]{2,1,0:T(8,128)(2,1)S(1)}, u32[]{:S(2)}, u32[]{:S(2)}) collective-permute-start(bf16[2,96,512]{2,1,0:T(8,128)(2,1)S(1)} %pad_maximum_fusion.refs_0_), channel_id=1, source_target_pairs={{0,4},{1,5},{2,6},{3,7},{4,0},{5,1},{6,2},{7,3},{8,12},{9,13},{10,... | collective-permute-start | bytes 589832 | tf_op jit(solution)/shard_map/ppermute | solution.py:399
  59.8 2.7 %collective-permute-start.7 = (bf16[2,96,512]{2,1,0:T(8,128)(2,1)S(1)}, bf16[2,96,512]{2,1,0:T(8,128)(2,1)S(1)}, u32[]{:S(2)}, u32[]{:S(2)}) collective-permute-start(bf16[2,96,512]{2,1,0:T(8,128)(2,1)S(1)} %pad_maximum_fusion.refs_0_), channel_id=1, source_target_pairs={{0,6},{1,7},{2,0},{3,1},{4,2},{5,3},{6,4},{7,5},{8,14},{9,15},{10,... | collective-permute-start | bytes 589832 | tf_op jit(solution)/shard_map/ppermute | solution.py:399
  62.5 1.5 %place.1.into = bf16[16,3,2,128,128]{4,3,2,1,0:T(8,128)(2,1)} custom-call(bf16[8,400,128]{2,1,0:T(8,128)(2,1)S(1)} %all-to-all-done.mine.near, bf16[8,400,128]{2,1,0:T(8,128)(2,1)S(1)} %collective-permute-done.9.other), custom_call_target="tpu_custom_call" | custom-call | bytes 3145728 | tf_op jit(solution)/shard_map/place/pallas_call | solution.py:333
  64.0 4.8 %collective-permute-done.10.refs_3_ = bf16[2,96,512]{2,1,0:T(8,128)(2,1)S(1)} collective-permute-done((bf16[2,96,512]{2,1,0:T(8,128)(2,1)S(1)}, bf16[2,96,512]{2,1,0:T(8,128)(2,1)S(1)}, u32[]{:S(2)}, u32[]{:S(2)}) %collective-permute-start.10) | collective-permute-done | bytes 196640 | tf_op jit(solution)/shard_map/ppermute | solution.py:399
  68.9 3.2 %collective-permute-start.11 = (bf16[8,400,128]{2,1,0:T(8,128)(2,1)S(1)}, bf16[8,400,128]{2,1,0:T(8,128)(2,1)S(1)}, u32[]{:S(2)}, u32[]{:S(2)}) collective-permute-start(bf16[8,400,128]{2,1,0:T(8,128)(2,1)S(1)} %all-to-all-done.1.far), channel_id=1, source_target_pairs={{0,1},{1,0},{2,3},{3,2},{4,5},{5,4},{6,7},{7,6},{8,9},{9,8},{10,11... | collective-permute-start | bytes 2457608 | tf_op jit(solution)/shard_map/ppermute | solution.py:404
  72.1 0.3 collective-permute-start.12
  72.4 0.5 collective-permute-start.15
  73.0 0.4 collective-permute-start.14
  73.4 0.7 add_convert_fusion
  74.1 0.3 collective-permute-done.12.refs_4_
  74.3 0.3 collective-permute-done.15.refs_7_
  74.6 0.3 collective-permute-done.13.refs_5_
  74.9 0.3 collective-permute-done.14.refs_6_
  75.2 3.1 %finish.1 = (bf16[96,8192]{1,0:T(8,128)(2,1)}, bf16[16,3,2,128,128]{4,3,2,1,0:T(8,128)(2,1)}, bf16[16,4,128]{2,1,0:T(4,128)(2,1)}) custom-call(bf16[1,8192]{1,0:T(2,128)(2,1)S(1)} %reshape.43.gain, bf16[8,400,128]{2,1,0:T(8,128)(2,1)S(1)} %all-to-all-done.mine.near, bf16[8,400,128]{2,1,0:T(8,128)(2,1)S(1)} %all-to-all-done.1.far, ...), custom_call_target="tpu_custom_call", output_to_operand_aliasing={{1}: (4, {})} | custom-call | flops 3145728 | bytes 8388608 | tf_op jit(solution)/shard_map/finish/pallas_call | solution.py:288
  (26 shorter events, 0.5 us)
Async XLA Ops:
  4.4 36.6 %all-to-all-start = ((bf16[8,400,128]{2,1,0:T(8,128)(2,1)}), bf16[8,400,128]{2,1,0:T(8,128)(2,1)S(1)}, u32[]{:S(2)}, u32[]{:S(2)}) async-start(bf16[8,400,128]{2,1,0:T(8,128)(2,1)} %get-tuple-element.24), calls=%async_computation | async-start | bytes 1638400 | tf_op jit(solution)/shard_map/all_to_all | solution.py:361
  13.4 20.3 %collective-permute-start.1 = (bf16[8,400,128]{2,1,0:T(8,128)(2,1)S(1)}, bf16[8,400,128]{2,1,0:T(8,128)(2,1)S(1)}, u32[]{:S(2)}, u32[]{:S(2)}) collective-permute-start(bf16[8,400,128]{2,1,0:T(8,128)(2,1)S(1)} %get-tuple-element.22), channel_id=1, source_target_pairs={{0,16},{16,0},{32,48},{48,32},{64,80},{80,64},{96,112},{112,96},{1... | collective-permute-start | bytes 2457608 | tf_op jit(solution)/shard_map/ppermute | solution.py:373
  24.0 3.2 %collective-permute-start = (bf16[8,96,512]{2,1,0:T(8,128)(2,1)S(1)}, bf16[8,96,512]{2,1,0:T(8,128)(2,1)S(1)}, u32[]{:S(2)}, u32[]{:S(2)}) collective-permute-start(bf16[8,96,512]{2,1,0:T(8,128)(2,1)S(1)} %get-tuple-element.21), channel_id=1, source_target_pairs={{0,1},{1,0},{2,3},{3,2},{4,5},{5,4},{6,7},{7,6},{8,9},{9,8},{10,11... | collective-permute-start | bytes 2359304 | tf_op jit(solution)/shard_map/ppermute | solution.py:377
  25.8 24.2 %copy-start.2 = (bf16[2,48,512]{2,1,0:T(8,128)(2,1)S(1)}, bf16[2,48,512]{2,1,0:T(8,128)(2,1)}, u32[]{:S(2)}) copy-start(bf16[2,48,512]{2,1,0:T(8,128)(2,1)} %param.11) | copy-start | bytes 294916
  27.2 11.4 %copy-start.1 = (bf16[8,96,512]{2,1,0:T(8,128)(2,1)}, bf16[8,96,512]{2,1,0:T(8,128)(2,1)S(1)}, u32[]{:S(2)}) copy-start(bf16[8,96,512]{2,1,0:T(8,128)(2,1)S(1)} %collective-permute-done) | copy-start | bytes 2359300
  33.7 5.0 %copy-start = (bf16[8,400,128]{2,1,0:T(8,128)(2,1)}, bf16[8,400,128]{2,1,0:T(8,128)(2,1)S(1)}, u32[]{:S(2)}) copy-start(bf16[8,400,128]{2,1,0:T(8,128)(2,1)S(1)} %collective-permute-done.1) | copy-start | bytes 2457604
  34.6 12.7 %collective-permute-start.2 = (bf16[2,96,512]{2,1,0:T(8,128)(2,1)}, bf16[2,96,512]{2,1,0:T(8,128)(2,1)}, u32[]{:S(2)}, u32[]{:S(2)}) collective-permute-start(bf16[2,96,512]{2,1,0:T(8,128)(2,1)} %get-tuple-element.38), channel_id=1, source_target_pairs={{0,4},{1,5},{2,6},{3,7},{4,0},{5,1},{6,2},{7,3},{8,12},{9,13},{10,... | collective-permute-start | bytes 589832 | tf_op jit(solution)/shard_map/ppermute | solution.py:382
  38.2 9.0 %collective-permute-start.3 = (bf16[2,96,512]{2,1,0:T(8,128)(2,1)}, bf16[2,96,512]{2,1,0:T(8,128)(2,1)}, u32[]{:S(2)}, u32[]{:S(2)}) collective-permute-start(bf16[2,96,512]{2,1,0:T(8,128)(2,1)} %slice_add_fusion.1), channel_id=1, source_target_pairs={{0,2},{1,3},{2,4},{3,5},{4,6},{5,7},{6,0},{7,1},{8,10},{9,11},{10,... | collective-permute-start | bytes 589832 | tf_op jit(solution)/shard_map/ppermute | solution.py:382
  38.6 8.7 %collective-permute-start.4 = (bf16[2,96,512]{2,1,0:T(8,128)(2,1)S(1)}, bf16[2,96,512]{2,1,0:T(8,128)(2,1)}, u32[]{:S(2)}, u32[]{:S(2)}) collective-permute-start(bf16[2,96,512]{2,1,0:T(8,128)(2,1)S(1)} %get-tuple-element.39), channel_id=1, source_target_pairs={{0,6},{1,7},{2,0},{3,1},{4,2},{5,3},{6,4},{7,5},{8,14},{9,15},{10,... | collective-permute-start | bytes 589832 | tf_op jit(solution)/shard_map/ppermute | solution.py:382
  40.9 27.9 %all-to-all-start.1 = ((bf16[8,400,128]{2,1,0:T(8,128)(2,1)}), bf16[8,400,128]{2,1,0:T(8,128)(2,1)S(1)}, u32[]{:S(2)}, u32[]{:S(2)}) async-start(bf16[8,400,128]{2,1,0:T(8,128)(2,1)} %copy-done), calls=%async_computation.1 | async-start | bytes 1638400 | tf_op jit(solution)/shard_map/all_to_all | solution.py:361
  48.7 6.0 %collective-permute-start.5 = (bf16[2,96,512]{2,1,0:T(8,128)(2,1)S(1)}, bf16[2,96,512]{2,1,0:T(8,128)(2,1)S(1)}, u32[]{:S(2)}, u32[]{:S(2)}) collective-permute-start(bf16[2,96,512]{2,1,0:T(8,128)(2,1)S(1)} %fusion.5), channel_id=1, source_target_pairs={{0,8},{1,9},{2,10},{3,11},{4,12},{5,13},{6,14},{7,15},{8,0},{9,1},... | collective-permute-start | bytes 589832 | tf_op jit(solution)/shard_map/ppermute | solution.py:389
  50.0 4.7 %collective-permute-start.6 = (bf16[96,512]{1,0:T(8,128)(2,1)S(1)}, bf16[96,512]{1,0:T(8,128)(2,1)S(1)}, u32[]{:S(2)}, u32[]{:S(2)}) collective-permute-start(bf16[96,512]{1,0:T(8,128)(2,1)S(1)} %bitcast.26), channel_id=1, source_target_pairs={{0,8},{1,9},{2,10},{3,11},{4,12},{5,13},{6,14},{7,15},{8,0},{9,1},... | collective-permute-start | bytes 294920 | tf_op jit(solution)/shard_map/ppermute | solution.py:371
  50.2 12.3 %collective-permute-start.9 = (bf16[8,400,128]{2,1,0:T(8,128)(2,1)S(1)}, bf16[8,400,128]{2,1,0:T(8,128)(2,1)S(1)}, u32[]{:S(2)}, u32[]{:S(2)}) collective-permute-start(bf16[8,400,128]{2,1,0:T(8,128)(2,1)S(1)} %all-to-all-done.mine.near), channel_id=1, source_target_pairs={{0,1},{1,0},{2,3},{3,2},{4,5},{5,4},{6,7},{7,6},{8,9},{9,8},{10,11... | collective-permute-start | bytes 2457608 | tf_op jit(solution)/shard_map/ppermute | solution.py:401
  54.1 18.0 %copy-start.3 = (bf16[8192]{0:T(1024)(128)(2,1)S(1)}, bf16[8192]{0:T(1024)(128)(2,1)}, u32[]{:S(2)}) copy-start(bf16[8192]{0:T(1024)(128)(2,1)} %param.17) | copy-start | bytes 49156
  54.7 9.3 %collective-permute-start.8 = (bf16[2,96,512]{2,1,0:T(8,128)(2,1)S(1)}, bf16[2,96,512]{2,1,0:T(8,128)(2,1)S(1)}, u32[]{:S(2)}, u32[]{:S(2)}) collective-permute-start(bf16[2,96,512]{2,1,0:T(8,128)(2,1)S(1)} %pad_maximum_fusion.refs_0_), channel_id=1, source_target_pairs={{0,4},{1,5},{2,6},{3,7},{4,0},{5,1},{6,2},{7,3},{8,12},{9,13},{10,... | collective-permute-start | bytes 589832 | tf_op jit(solution)/shard_map/ppermute | solution.py:399
  59.8 9.1 %collective-permute-start.10 = (bf16[2,96,512]{2,1,0:T(8,128)(2,1)S(1)}, bf16[2,96,512]{2,1,0:T(8,128)(2,1)S(1)}, u32[]{:S(2)}, u32[]{:S(2)}) collective-permute-start(bf16[2,96,512]{2,1,0:T(8,128)(2,1)S(1)} %pad_maximum_fusion.refs_0_), channel_id=1, source_target_pairs={{0,2},{1,3},{2,4},{3,5},{4,6},{5,7},{6,0},{7,1},{8,10},{9,11},{10,... | collective-permute-start | bytes 589832 | tf_op jit(solution)/shard_map/ppermute | solution.py:399
  59.8 9.1 %collective-permute-start.7 = (bf16[2,96,512]{2,1,0:T(8,128)(2,1)S(1)}, bf16[2,96,512]{2,1,0:T(8,128)(2,1)S(1)}, u32[]{:S(2)}, u32[]{:S(2)}) collective-permute-start(bf16[2,96,512]{2,1,0:T(8,128)(2,1)S(1)} %pad_maximum_fusion.refs_0_), channel_id=1, source_target_pairs={{0,6},{1,7},{2,0},{3,1},{4,2},{5,3},{6,4},{7,5},{8,14},{9,15},{10,... | collective-permute-start | bytes 589832 | tf_op jit(solution)/shard_map/ppermute | solution.py:399
  68.9 6.3 %collective-permute-start.11 = (bf16[8,400,128]{2,1,0:T(8,128)(2,1)S(1)}, bf16[8,400,128]{2,1,0:T(8,128)(2,1)S(1)}, u32[]{:S(2)}, u32[]{:S(2)}) collective-permute-start(bf16[8,400,128]{2,1,0:T(8,128)(2,1)S(1)} %all-to-all-done.1.far), channel_id=1, source_target_pairs={{0,1},{1,0},{2,3},{3,2},{4,5},{5,4},{6,7},{7,6},{8,9},{9,8},{10,11... | collective-permute-start | bytes 2457608 | tf_op jit(solution)/shard_map/ppermute | solution.py:404
  72.1 2.2 %collective-permute-start.12 = (bf16[2,96,512]{2,1,0:T(8,128)(2,1)S(1)}, bf16[2,96,512]{2,1,0:T(8,128)(2,1)S(1)}, u32[]{:S(2)}, u32[]{:S(2)}) collective-permute-start(bf16[2,96,512]{2,1,0:T(8,128)(2,1)S(1)} %pad_maximum_fusion.refs_0_), channel_id=1, source_target_pairs={{0,1},{1,0},{2,3},{3,2},{4,5},{5,4},{6,7},{7,6},{8,9},{9,8},{10,11... | collective-permute-start | bytes 589832 | tf_op jit(solution)/shard_map/ppermute | solution.py:405
  72.4 2.2 %collective-permute-start.15 = (bf16[2,96,512]{2,1,0:T(8,128)(2,1)S(1)}, bf16[2,96,512]{2,1,0:T(8,128)(2,1)S(1)}, u32[]{:S(2)}, u32[]{:S(2)}) collective-permute-start(bf16[2,96,512]{2,1,0:T(8,128)(2,1)S(1)} %collective-permute-done.10.refs_3_), channel_id=1, source_target_pairs={{0,1},{1,0},{2,3},{3,2},{4,5},{5,4},{6,7},{7,6},{8,9},{9,8},{10,11... | collective-permute-start | bytes 589832 | tf_op jit(solution)/shard_map/ppermute | solution.py:405
  72.9 2.0 %collective-permute-start.13 = (bf16[2,96,512]{2,1,0:T(8,128)(2,1)S(1)}, bf16[2,96,512]{2,1,0:T(8,128)(2,1)S(1)}, u32[]{:S(2)}, u32[]{:S(2)}) collective-permute-start(bf16[2,96,512]{2,1,0:T(8,128)(2,1)S(1)} %collective-permute-done.7.refs_1_), channel_id=1, source_target_pairs={{0,1},{1,0},{2,3},{3,2},{4,5},{5,4},{6,7},{7,6},{8,9},{9,8},{10,11... | collective-permute-start | bytes 589832 | tf_op jit(solution)/shard_map/ppermute | solution.py:405
  73.0 2.2 %collective-permute-start.14 = (bf16[2,96,512]{2,1,0:T(8,128)(2,1)S(1)}, bf16[2,96,512]{2,1,0:T(8,128)(2,1)S(1)}, u32[]{:S(2)}, u32[]{:S(2)}) collective-permute-start(bf16[2,96,512]{2,1,0:T(8,128)(2,1)S(1)} %collective-permute-done.8.refs_2_), channel_id=1, source_target_pairs={{0,1},{1,0},{2,3},{3,2},{4,5},{5,4},{6,7},{7,6},{8,9},{9,8},{10,11... | collective-permute-start | bytes 589832 | tf_op jit(solution)/shard_map/ppermute | solution.py:405

commit v4 on v3

--- a/solution.py
+++ b/solution.py
@@ -53,7 +53,7 @@
     return pltpu.CompilerParams(vmem_limit_bytes=mib << 20)
 
 
-def pack_kernel(tbl, blk, mv, nkv, kv, near, far, fresh, stage, sems, fsem):
+def pack_kernel(tbl, blk, mv, nkv, kv, near_out, far, near, fresh, stage, sems, fsem, osem):
     tp = lax.axis_index("tp")
     core = lax.rem(tp, 2)
     side = lax.rem(lax.axis_index("inst"), 2)
@@ -82,32 +82,54 @@
         stage[i, z, 2:4] = fresh[1, m].astype(F32)
     near[:, TOK:MSG] = stage[0].astype(BF16)
     far[:, TOK:MSG] = stage[1].astype(BF16)
-    for out, i, z, m in groups:
+    for n, (out, i, z, m) in enumerate(groups):
         count = blk[m]
+        if n == Z:
+            ocopy = pltpu.make_async_copy(near, near_out, osem)
+            ocopy.start()
         for b in range(MAXB):
             page_copy(out, i, z, b, 0).wait()
             if b > 0:
                 @pl.when(b >= count)
                 def _():
                     out[z, b * PAGE:(b + 1) * PAGE] = jnp.zeros((PAGE, HD), BF16)
+    ocopy.wait()
 
 
 def pack(table, blocks, moves, new_kv, kv_pages):
     return pl.pallas_call(
         pack_kernel,
-        out_shape=(pltpu.VMEM((Z, MSG, HD), BF16),) * 2,
+        out_shape=(pltpu.HBM((Z, MSG, HD), BF16), pltpu.VMEM((Z, MSG, HD), BF16)),
         in_specs=[smem_spec()] * 3 + [any_spec()] * 2,
-        out_specs=(vmem_spec(),) * 2,
+        out_specs=(any_spec(), vmem_spec()),
         scratch_shapes=[
+            pltpu.VMEM((Z, MSG, HD), BF16),
             pltpu.VMEM((STEPS, SLOTS, 2, HD), BF16),
             pltpu.VMEM((2, Z, 16, HD), F32),
             pltpu.SemaphoreType.DMA((2 * Z * MAXB,)),
+            pltpu.SemaphoreType.DMA,
             pltpu.SemaphoreType.DMA,
         ],
         compiler_params=params(16),
         cost_estimate=pl.CostEstimate(flops=0, bytes_accessed=4 << 20, transcendentals=0),
         name="pack",
     )(in_hbm(table), in_hbm(blocks), in_hbm(moves), in_hbm(new_kv), in_hbm(kv_pages))
+
+
+def touch_kernel(x, out):
+    del x, out
+
+
+def touch(x):
+    return pl.pallas_call(
+        touch_kernel,
+        out_shape=pltpu.HBM(x.shape, x.dtype),
+        in_specs=[any_spec()],
+        out_specs=any_spec(),
+        input_output_aliases={0: 0},
+        cost_estimate=pl.CostEstimate(flops=0, bytes_accessed=128 << 20, transcendentals=0),
+        name="touch",
+    )(in_hbm(x))
 
 
 def place_of(tp):
@@ -240,34 +262,37 @@
     )(in_hbm(table), in_hbm(blocks), in_hbm(query), in_hbm(new_kv), in_hbm(kv_pages), in_hbm(out_weight))
 
 
-def own_kernel(heads, wb, keep):
+def own_kernel(heads, wb, got, *outs):
     core, x, y = place_of(lax.axis_index("tp"))
-    project(heads, wb, keep, x, y, core)
-
-
-def own(heads, wb):
+    rows = heads[...]
+    for k in range(CHIPS):
+        cols = pl.ds(pl.multiple_of(block_of(x, y, k, core) * SHARE, SHARE), SHARE)
+        part = jnp.dot(rows, wb[:, cols], preferred_element_type=F32) + got[k].astype(F32)
+        outs[k // 2][k % 2] = part.astype(outs[k // 2].dtype)
+
+
+def own(heads, wb, got):
     return pl.pallas_call(
         own_kernel,
-        out_shape=pltpu.VMEM((CHIPS, ROWS, SHARE), F32),
-        in_specs=[vmem_spec()] * 2,
-        out_specs=vmem_spec(),
+        out_shape=tuple(pltpu.VMEM((2, ROWS, SHARE), F32 if dy == 0 else BF16) for dy in range(4)),
+        in_specs=[vmem_spec()] * 3,
+        out_specs=(vmem_spec(),) * 4,
         compiler_params=params(16),
         cost_estimate=pl.CostEstimate(flops=1, bytes_accessed=1, transcendentals=0),
         name="own",
-    )(in_vmem(heads), in_vmem(wb))
-
-
-def finish_kernel(gain, near, far, far_other, into, *refs):
-    blocks, (normed, arrived, tail, buf, sem, nsem) = refs[:8], refs[8:]
+    )(in_vmem(heads), in_vmem(wb), in_vmem(got))
+
+
+def norm_kernel(gain, *refs):
+    blocks, (normed, buf, nsem) = refs[:8], refs[8:]
     core, x, y = place_of(lax.axis_index("tp"))
-    side = lax.rem(lax.axis_index("inst"), 2)
-    copies = place_copies(far, far_other, arrived, 1 - side, sem)
     squares = jnp.zeros((ROWS, SHARE), F32)
     for ref in blocks:
         for dx in range(2):
             v = ref[dx].astype(F32)
             squares = squares + v * v
     scale = lax.rsqrt(jnp.sum(squares, axis=-1, keepdims=True) / D + EPSILON)
+    copies = []
     for part in range(2):
         for k in range(CHIPS):
             block = block_of(x, y, k, core if part == 0 else 1 - core)
@@ -277,69 +302,96 @@
             copy = pltpu.make_async_copy(buf.at[:, at], normed.at[:, at], nsem.at[part * CHIPS + k])
             copy.start()
             copies.append(copy)
-    for refs, way in ((near, side), (far, 1 - side)):
-        for z in range(Z):
-            tail[2 * z + way] = refs[z, TOK:MSG].astype(F32)[0:4].astype(BF16)
     for copy in copies:
         copy.wait()
 
 
-def finish(gain, near, far, far_other, into, mine, other):
-    return pl.pallas_call(
-        finish_kernel,
-        out_shape=(
-            pltpu.HBM((ROWS, D), BF16),
-            pltpu.HBM((INST, MAXB, 2, PAGE, HD), BF16),
-            jax.ShapeDtypeStruct((INST, 4, HD), BF16),
-        ),
-        in_specs=[vmem_spec()] * 4 + [any_spec()] + [vmem_spec()] * 8,
-        out_specs=(any_spec(), any_spec(), vmem_spec()),
+def norm(gain, mine, other):
+    return pl.pallas_call(
+        norm_kernel,
+        out_shape=pltpu.HBM((ROWS, D), BF16),
+        in_specs=[vmem_spec()] * 9,
+        out_specs=any_spec(),
         scratch_shapes=[
             pltpu.VMEM((ROWS, D), BF16),
-            pltpu.SemaphoreType.DMA((2 * Z * MAXB,)),
             pltpu.SemaphoreType.DMA((2 * CHIPS,)),
         ],
-        input_output_aliases={4: 1},
         compiler_params=params(24),
         cost_estimate=pl.CostEstimate(flops=4 * ROWS * D, bytes_accessed=8 << 20, transcendentals=0),
-        name="finish",
-    )(gain.reshape(1, D), near, far, far_other, into, *mine, *other)
-
-
-def place_copies(mine, other, out, way, sems):
+        name="norm",
+    )(gain.reshape(1, D), *mine, *other)
+
+
+def half_copies(src, out, way, half, sems, first):
+    copies = []
+    for z in range(Z):
+        for b in range(MAXB):
+            copies.append(
+                pltpu.make_async_copy(
+                    src.at[z, pl.ds(b * PAGE, PAGE)],
+                    out.at[2 * z + way, b, half],
+                    sems.at[first + z * MAXB + b],
+                )
+            )
+            copies[-1].start()
+    return copies
+
+
+def place_near_kernel(mine, other, out, rows, sems):
     core = lax.rem(lax.axis_index("tp"), 2)
-    copies = []
-    for part, (src, half) in enumerate(((mine, core), (other, 1 - core))):
-        for z in range(Z):
-            for b in range(MAXB):
-                copies.append(
-                    pltpu.make_async_copy(
-                        src.at[z, pl.ds(b * PAGE, PAGE)],
-                        out.at[2 * z + way, b, half],
-                        sems.at[(part * Z + z) * MAXB + b],
-                    )
-                )
-                copies[-1].start()
-    return copies
-
-
-def place_kernel(mine, other, out, sems):
     side = lax.rem(lax.axis_index("inst"), 2)
-    for copy in place_copies(mine, other, out, side, sems):
+    copies = half_copies(mine, out, side, core, sems, 0)
+    copies += half_copies(other, out, side, 1 - core, sems, Z * MAXB)
+    for z in range(Z):
+        rows[z] = mine[z, TOK:MSG].astype(F32)[0:4]
+    for copy in copies:
         copy.wait()
 
 
-def place(mine, other):
-    return pl.pallas_call(
-        place_kernel,
-        out_shape=pltpu.HBM((INST, MAXB, 2, PAGE, HD), BF16),
+def place_near(mine, other):
+    return pl.pallas_call(
+        place_near_kernel,
+        out_shape=(
+            pltpu.HBM((INST, MAXB, 2, PAGE, HD), BF16),
+            jax.ShapeDtypeStruct((Z, 4, HD), F32),
+        ),
         in_specs=[vmem_spec()] * 2,
-        out_specs=any_spec(),
+        out_specs=(any_spec(), vmem_spec()),
         scratch_shapes=[pltpu.SemaphoreType.DMA((2 * Z * MAXB,))],
         compiler_params=params(8),
         cost_estimate=pl.CostEstimate(flops=0, bytes_accessed=3 << 20, transcendentals=0),
-        name="place",
+        name="place_near",
     )(mine, other)
+
+
+def place_far_kernel(other, src, *refs):
+    out, sems = refs[-2:] if other else (refs[-3], refs[-1])
+    core = lax.rem(lax.axis_index("tp"), 2)
+    side = lax.rem(lax.axis_index("inst"), 2)
+    copies = half_copies(src, out, 1 - side, 1 - core if other else core, sems, 0)
+    if not other:
+        rows, tail = refs[0], refs[-2]
+        for z in range(Z):
+            tail[2 * z + side] = rows[z].astype(BF16)
+            tail[2 * z + 1 - side] = src[z, TOK:MSG].astype(F32)[0:4].astype(BF16)
+    for copy in copies:
+        copy.wait()
+
+
+def place_far(src, into, rows=None):
+    whole = pltpu.HBM((INST, MAXB, 2, PAGE, HD), BF16)
+    own_half = rows is not None
+    return pl.pallas_call(
+        functools.partial(place_far_kernel, not own_half),
+        out_shape=(whole, jax.ShapeDtypeStruct((INST, 4, HD), BF16)) if own_half else whole,
+        in_specs=[vmem_spec()] * (2 if own_half else 1) + [any_spec()],
+        out_specs=(any_spec(), vmem_spec()) if own_half else any_spec(),
+        scratch_shapes=[pltpu.SemaphoreType.DMA((Z * MAXB,))],
+        input_output_aliases={2 if own_half else 1: 0},
+        compiler_params=params(8),
+        cost_estimate=pl.CostEstimate(flops=0, bytes_accessed=3 << 20, transcendentals=0),
+        name="place_far",
+    )(src, *((rows,) if own_half else ()), into)
 
 
 def tp_perm(dx, dy, dc):
@@ -367,43 +419,39 @@
 
 def local(query, new_kv, residual, kv_pages, block_table, blocks, moves, out_weight, norm_gain):
     table = block_table.T
-    own_rows = residual.reshape(ROWS, SHARE)
-    peer_rows = lax.ppermute(own_rows, "tp", CROSS)
     near, far = pack(table, blocks, moves, new_kv, kv_pages)
     far = lax.ppermute(far, "inst", SIDES)
-    near = along_z(near)
+    near = along_z(touch(near))
 
     send, heads, weight = attend(table, blocks, query, new_kv, kv_pages, out_weight)
-    got = after(lax.ppermute(send, "tp", SWAP), far)
-    keep = own(heads, weight)
-    sums = [
-        keep[2 * dy:2 * dy + 2] + got[2 * dy:2 * dy + 2].astype(F32) for dy in range(4)
-    ]
-    terms = [lax.ppermute(sums[dy].astype(BF16), "tp", tp_perm(0, dy, 0)) for dy in AROUND]
+    got = lax.ppermute(send, "tp", SWAP)
+    sums = own(after(heads, far), weight, got)
+    terms = [lax.ppermute(sums[dy], "tp", tp_perm(0, dy, 0)) for dy in AROUND]
     terms[0] = after(terms[0], near)
-    far = along_z(after(far, sums[1], near))
+    far = along_z(after(far, sums[1]))
     total = sums[0]
     for term in terms:
         total = total + term.astype(F32)
-    part = total.astype(BF16)
+    own_rows = residual.reshape(ROWS, SHARE).astype(F32)
+    part = jnp.stack([own_rows + total[0], total[1]]).astype(BF16)
     cross = lax.ppermute(part, "tp", CROSS)
     pair = jnp.stack(
-        [
-            (rows.astype(F32) + (part[dx].astype(F32) + cross[1 - dx].astype(F32))).astype(BF16)
-            for dx, rows in enumerate((own_rows, peer_rows))
-        ]
+        [(part[dx].astype(F32) + cross[1 - dx].astype(F32)).astype(BF16) for dx in range(2)]
     )
     hidden = pair[0].reshape(STEPS, SLOTS, SHARE)
     mine = {0: pair}
     for dy in AROUND:
         mine[dy] = lax.ppermute(pair, "tp", tp_perm(0, 4 - dy, 0))
     mine = [mine[dy] for dy in range(4)]
-    arrived = place(near, lax.ppermute(after(near, part), "tp", SWAP))
-    mine[2], arrived = lax.optimization_barrier((mine[2], arrived))
+    near = after(near, pair)
+    arrived, rows = place_near(near, lax.ppermute(near, "tp", SWAP))
+    mine[2], arrived, hidden = lax.optimization_barrier((mine[2], arrived, hidden))
+    other = [lax.ppermute(block, "tp", SWAP) for block in mine]
+    normed = norm(norm_gain, mine, other)
     far = after(far, *mine)
     far_other = lax.ppermute(far, "tp", SWAP)
-    other = [lax.ppermute(block, "tp", SWAP) for block in mine]
-    normed, arrived, tail = finish(norm_gain, near, far, far_other, arrived, mine, other)
+    arrived, tail = place_far(far, arrived, rows)
+    arrived = place_far(far_other, arrived)
     return (
         hidden,
         normed.reshape(STEPS, SLOTS, D),

time: 78.8 us -> 75.2 us (0.954)
  starting transfers between devices: 42.7 us -> 30.1 us
  waiting for transfers between devices: 14.4 us -> 25.4 us
  other arithmetic: 3.77 us -> 0.21 us
  Pallas kernels: 16.7 us -> 18.2 us
    all_to_all x2, waiting for transfers between devices: 0.01 us -> 10.9 us  [along_z(): lax.all_to_all(x, 'inst', 0, 0, tiled=True, axis_index_groups=Z_GROUPS)]
    ppermute x1, waiting for transfers between devices: 6.46 us -> 0.01 us  [local(): far = lax.ppermute(far, 'inst', SIDES)]
    ppermute x1, waiting for transfers between devices: 0.01 us -> 5.67 us  [local(): cross = lax.ppermute(part, 'tp', CROSS)]
    all_to_all x2, starting transfers between devices: 15.4 us -> 11.7 us  [along_z(): lax.all_to_all(x, 'inst', 0, 0, tiled=True, axis_index_groups=Z_GROUPS)]
    ppermute x3, starting transfers between devices: 7.73 us -> 4.4 us  [local(): mine[dy] = lax.ppermute(pair, 'tp', tp_perm(0, 4 - dy, 0))]
    convert_element_type x5 -> x1, other arithmetic: 2.96 us -> 0.05 us  [local(): (part[dx].astype(F32) + cross[1 - dx].astype(F32)).astype(BF16)]
    ppermute x1, starting transfers between devices: 3.24 us -> 0.49 us  [local(): far_other = lax.ppermute(far, 'tp', SWAP)]
    ppermute x6 -> x5, starting transfers between devices: 11 us -> 8.39 us  [the longest x3 5.64 us: local(): terms = [lax.ppermute(sums[dy], 'tp', tp_perm(0, dy, 0)) for dy in AROUND]]
  transfers between devices with their start and end apart: 18 -> 17, of which waited for: 8 -> 7; matrix products, arithmetic and copies ran while one was open for 5% -> 0% of each run, Pallas kernels for 13% -> 18%
where the time goes in v4:
time: 75.2 us; the launch traced here: 74.8 us
  starting transfers between devices  30.1 us (40%)
  waiting for transfers between devices  25.4 us (34%)
  Pallas kernels  18.2 us (24%)
  between operations  0.81 us (1%)
    all_to_all x2, starting transfers between devices, along_z(): lax.all_to_all(x, 'inst', 0, 0, tiled=True, axis_index_groups=Z_GROUPS)  11.7 us
    all_to_all x2, waiting for transfers between devices, along_z(): lax.all_to_all(x, 'inst', 0, 0, tiled=True, axis_index_groups=Z_GROUPS)  10.9 us
    pallas_call x1, Pallas kernels, attend(): pl.pallas_call(attend_kernel, out_shape=(pltpu.VMEM((CHIPS, ROWS, SHARE),...  7.85 us
    ppermute x3, waiting for transfers between devices, local(): mine[dy] = lax.ppermute(pair, 'tp', tp_perm(0, 4 - dy, 0))  6.61 us
    ppermute x1, waiting for transfers between devices, local(): cross = lax.ppermute(part, 'tp', CROSS)  5.67 us
    ppermute x3, starting transfers between devices, local(): terms = [lax.ppermute(sums[dy], 'tp', tp_perm(0, dy, 0)) for dy in AROUND]  5.64 us
    ppermute x3, starting transfers between devices, local(): mine[dy] = lax.ppermute(pair, 'tp', tp_perm(0, 4 - dy, 0))  4.4 us
    ppermute x1, starting transfers between devices, local(): far = lax.ppermute(far, 'inst', SIDES)  3.66 us
  transfers between devices with their start and end apart: 17, of which 7 were waited for; matrix products, arithmetic and copies ran while one was open for 0% of the time, Pallas kernels for 18%

profile of v4, /device:TPU:1, one launch (start us, length us, event | category | flops | bytes accessed | tf_op | source)
XLA Modules:
  0.0 74.8 jit_solution(10192841079598025987)
XLA Ops:
  0.6 3.6 %pack.1 = (bf16[8,400,128]{2,1,0:T(8,128)(2,1)}, bf16[8,400,128]{2,1,0:T(8,128)(2,1)S(1)}) custom-call(s32[3,48]{1,0:T(4,128)} %bitcast.17, s32[48]{0:T(128)} %blk.3, s32[1,16]{1,0:T(1,128)} %mv.1, bf16[2,48,2,1024]{3,2,1,0:T(2,128)(2,1)} %nkv.3, bf16[144,2,1,128,128]{4,3,2,1,0:T(8,128)(2,1)} %kv.3), custom_call_target="tpu_custom_call" | custom-call | bytes 4194304 | tf_op jit(solution)/shard_map/pack/pallas_call | solution.py:100
  4.2 3.7 %collective-permute-start = (bf16[8,400,128]{2,1,0:T(8,128)(2,1)S(1)}, bf16[8,400,128]{2,1,0:T(8,128)(2,1)}, u32[]{:S(2)}, u32[]{:S(2)}) collective-permute-start(bf16[8,400,128]{2,1,0:T(8,128)(2,1)S(1)} %get-tuple-element.26), channel_id=1, source_target_pairs={{0,16},{16,0},{32,48},{48,32},{64,80},{80,64},{96,112},{112,96},{1... | collective-permute-start | bytes 2457608 | tf_op jit(solution)/shard_map/ppermute | solution.py:423
  7.9 8.2 %all-to-all-start = ((bf16[8,400,128]{2,1,0:T(8,128)(2,1)}), bf16[8,400,128]{2,1,0:T(8,128)(2,1)S(1)}, u32[]{:S(2)}, u32[]{:S(2)}) async-start(bf16[8,400,128]{2,1,0:T(8,128)(2,1)} %touch.1), calls=%async_computation | async-start | bytes 1638400 | tf_op jit(solution)/shard_map/all_to_all | solution.py:413
  16.1 7.9 %attend.1 = (bf16[8,96,512]{2,1,0:T(8,128)(2,1)S(1)}, bf16[96,256]{1,0:T(8,128)(2,1)S(1)}, bf16[256,8192]{1,0:T(8,128)(2,1)S(1)}) custom-call(s32[3,48]{1,0:T(4,128)} %bitcast.18, s32[48]{0:T(128)} %blk.3, bf16[2,48,256]{2,1,0:T(8,128)(2,1)} %q_hbm.1, bf16[2,48,2,1024]{3,2,1,0:T(2,128)(2,1)} %nkv.3, bf16[144,2,1,128,128]{4,3,2,1,0:T(8,128)(2,1)} %kv.3, ...), custom_call_target="tpu_custom_call" | custom-call | flops 10000000000 | bytes 67108864 | tf_op jit(solution)/shard_map/attend/pallas_call | solution.py:237
  23.9 1.3 %collective-permute-start.1 = (bf16[8,96,512]{2,1,0:T(8,128)(2,1)S(1)}, bf16[8,96,512]{2,1,0:T(8,128)(2,1)S(1)}, u32[]{:S(2)}, u32[]{:S(2)}) collective-permute-start(bf16[8,96,512]{2,1,0:T(8,128)(2,1)S(1)} %get-tuple-element.29), channel_id=1, source_target_pairs={{0,1},{1,0},{2,3},{3,2},{4,5},{5,4},{6,7},{7,6},{8,9},{9,8},{10,11... | collective-permute-start | bytes 2359304 | tf_op jit(solution)/shard_map/ppermute | solution.py:427
  25.3 1.9 %collective-permute-done.1.got = bf16[8,96,512]{2,1,0:T(8,128)(2,1)S(1)} collective-permute-done((bf16[8,96,512]{2,1,0:T(8,128)(2,1)S(1)}, bf16[8,96,512]{2,1,0:T(8,128)(2,1)S(1)}, u32[]{:S(2)}, u32[]{:S(2)}) %collective-permute-start.1) | collective-permute-done | bytes 786464 | tf_op jit(solution)/shard_map/ppermute | solution.py:427
  27.2 0.5 own.1
  27.7 3.0 %collective-permute-start.2 = (bf16[2,96,512]{2,1,0:T(8,128)(2,1)S(1)}, bf16[2,96,512]{2,1,0:T(8,128)(2,1)S(1)}, u32[]{:S(2)}, u32[]{:S(2)}) collective-permute-start(bf16[2,96,512]{2,1,0:T(8,128)(2,1)S(1)} %get-tuple-element.31), channel_id=1, source_target_pairs={{0,4},{1,5},{2,6},{3,7},{4,0},{5,1},{6,2},{7,3},{8,12},{9,13},{10,... | collective-permute-start | bytes 589832 | tf_op jit(solution)/shard_map/ppermute | solution.py:429
  30.6 0.4 collective-permute-start.3
  31.0 2.3 %collective-permute-start.4 = (bf16[2,96,512]{2,1,0:T(8,128)(2,1)S(1)}, bf16[2,96,512]{2,1,0:T(8,128)(2,1)S(1)}, u32[]{:S(2)}, u32[]{:S(2)}) collective-permute-start(bf16[2,96,512]{2,1,0:T(8,128)(2,1)S(1)} %get-tuple-element.35), channel_id=1, source_target_pairs={{0,6},{1,7},{2,0},{3,1},{4,2},{5,3},{6,4},{7,5},{8,14},{9,15},{10,... | collective-permute-start | bytes 589832 | tf_op jit(solution)/shard_map/ppermute | solution.py:429
  33.3 7.0 %all-to-all-done.mine = bf16[8,400,128]{2,1,0:T(8,128)(2,1)S(1)} async-done(((bf16[8,400,128]{2,1,0:T(8,128)(2,1)}), bf16[8,400,128]{2,1,0:T(8,128)(2,1)S(1)}, u32[]{:S(2)}, u32[]{:S(2)}) %all-to-all-start) | async-done | bytes 819232 | tf_op jit(solution)/shard_map/all_to_all | solution.py:413
  40.4 3.5 %all-to-all-start.1 = ((bf16[8,400,128]{2,1,0:T(8,128)(2,1)}), bf16[8,400,128]{2,1,0:T(8,128)(2,1)S(1)}, u32[]{:S(2)}, u32[]{:S(2)}) async-start(bf16[8,400,128]{2,1,0:T(8,128)(2,1)} %collective-permute-done), calls=%async_computation.1 | async-start | bytes 1638400 | tf_op jit(solution)/shard_map/all_to_all | solution.py:413
  43.9 0.1 convert_add_fusion
  44.1 0.4 collective-permute-start.5
  44.5 5.7 %collective-permute-done.5 = bf16[2,96,512]{2,1,0:T(8,128)(2,1)S(1)} collective-permute-done((bf16[2,96,512]{2,1,0:T(8,128)(2,1)S(1)}, bf16[2,96,512]{2,1,0:T(8,128)(2,1)S(1)}, u32[]{:S(2)}, u32[]{:S(2)}) %collective-permute-start.5) | collective-permute-done | bytes 196640 | tf_op jit(solution)/shard_map/ppermute | solution.py:437
  50.3 1.4 %collective-permute-start.7 = (bf16[8,400,128]{2,1,0:T(8,128)(2,1)S(1)}, bf16[8,400,128]{2,1,0:T(8,128)(2,1)S(1)}, u32[]{:S(2)}, u32[]{:S(2)}) collective-permute-start(bf16[8,400,128]{2,1,0:T(8,128)(2,1)S(1)} %all-to-all-done.mine), channel_id=1, source_target_pairs={{0,1},{1,0},{2,3},{3,2},{4,5},{5,4},{6,7},{7,6},{8,9},{9,8},{10,11... | collective-permute-start | bytes 2457608 | tf_op jit(solution)/shard_map/ppermute | solution.py:447
  51.7 2.9 %collective-permute-start.6 = (bf16[2,96,512]{2,1,0:T(8,128)(2,1)S(1)}, bf16[2,96,512]{2,1,0:T(8,128)(2,1)S(1)}, u32[]{:S(2)}, u32[]{:S(2)}) collective-permute-start(bf16[2,96,512]{2,1,0:T(8,128)(2,1)S(1)} %pad_maximum_fusion.1.refs_0_), channel_id=1, source_target_pairs={{0,4},{1,5},{2,6},{3,7},{4,0},{5,1},{6,2},{7,3},{8,12},{9,13},{10,... | collective-permute-start | bytes 589832 | tf_op jit(solution)/shard_map/ppermute | solution.py:444
  54.7 0.8 %collective-permute-start.8 = (bf16[2,96,512]{2,1,0:T(8,128)(2,1)S(1)}, bf16[2,96,512]{2,1,0:T(8,128)(2,1)S(1)}, u32[]{:S(2)}, u32[]{:S(2)}) collective-permute-start(bf16[2,96,512]{2,1,0:T(8,128)(2,1)S(1)} %pad_maximum_fusion.1.refs_0_), channel_id=1, source_target_pairs={{0,6},{1,7},{2,0},{3,1},{4,2},{5,3},{6,4},{7,5},{8,14},{9,15},{10,... | collective-permute-start | bytes 589832 | tf_op jit(solution)/shard_map/ppermute | solution.py:444
  55.4 0.7 collective-permute-start.9
  56.1 1.5 %place_near.1 = (bf16[16,3,2,128,128]{4,3,2,1,0:T(8,128)(2,1)}, f32[8,4,128]{2,1,0:T(4,128)S(1)}) custom-call(bf16[8,400,128]{2,1,0:T(8,128)(2,1)S(1)} %all-to-all-done.mine, bf16[8,400,128]{2,1,0:T(8,128)(2,1)S(1)} %collective-permute-done.7.other), custom_call_target="tpu_custom_call" | custom-call | bytes 3145728 | tf_op jit(solution)/shard_map/place_near/pallas_call | solution.py:352
  57.7 2.0 %collective-permute-done.6.refs_2_ = bf16[2,96,512]{2,1,0:T(8,128)(2,1)S(1)} collective-permute-done((bf16[2,96,512]{2,1,0:T(8,128)(2,1)S(1)}, bf16[2,96,512]{2,1,0:T(8,128)(2,1)S(1)}, u32[]{:S(2)}, u32[]{:S(2)}) %collective-permute-start.6) | collective-permute-done | bytes 196640 | tf_op jit(solution)/shard_map/ppermute | solution.py:444
  59.7 4.6 %collective-permute-done.8.refs_1_ = bf16[2,96,512]{2,1,0:T(8,128)(2,1)S(1)} collective-permute-done((bf16[2,96,512]{2,1,0:T(8,128)(2,1)S(1)}, bf16[2,96,512]{2,1,0:T(8,128)(2,1)S(1)}, u32[]{:S(2)}, u32[]{:S(2)}) %collective-permute-start.8) | collective-permute-done | bytes 196640 | tf_op jit(solution)/shard_map/ppermute | solution.py:444
  64.3 3.9 %all-to-all-done.1.src = bf16[8,400,128]{2,1,0:T(8,128)(2,1)S(1)} async-done(((bf16[8,400,128]{2,1,0:T(8,128)(2,1)}), bf16[8,400,128]{2,1,0:T(8,128)(2,1)S(1)}, u32[]{:S(2)}, u32[]{:S(2)}) %all-to-all-start.1) | async-done | bytes 819232 | tf_op jit(solution)/shard_map/all_to_all | solution.py:413
  68.2 0.5 collective-permute-start.14
  68.6 0.0 collective-permute-start.10
  68.7 0.5 collective-permute-start.11
  69.2 0.5 collective-permute-start.12
  69.7 1.7 %place_far.2 = (bf16[16,3,2,128,128]{4,3,2,1,0:T(8,128)(2,1)}, bf16[16,4,128]{2,1,0:T(4,128)(2,1)}) custom-call(bf16[8,400,128]{2,1,0:T(8,128)(2,1)S(1)} %all-to-all-done.1.src, f32[8,4,128]{2,1,0:T(4,128)S(1)} %get-tuple-element.42.refs_0_, bf16[16,3,2,128,128]{4,3,2,1,0:T(8,128)(2,1)} %get-tuple-element.43.refs_1_), custom_call_target="tpu_custom_call", output_to_operand_aliasing={{0}: (2, {})} | custom-call | bytes 3145728 | tf_op jit(solution)/shard_map/place_far/pallas_call | solution.py:384
  71.4 0.0 collective-permute-done.13.refs_7_
  71.4 0.3 collective-permute-done.12.refs_6_
  71.7 2.0 %norm.1 = bf16[96,8192]{1,0:T(8,128)(2,1)} custom-call(bf16[1,8192]{1,0:T(2,128)(2,1)S(1)} %reshape.39.gain, bf16[2,96,512]{2,1,0:T(8,128)(2,1)S(1)} %pad_maximum_fusion.1.refs_0_, bf16[2,96,512]{2,1,0:T(8,128)(2,1)S(1)} %collective-permute-done.8.refs_1_, bf16[2,96,512]{2,1,0:T(8,128)(2,1)S(1)} %collective-permute-done.6.refs_2_, ...), custom_call_target="tpu_custom_call" | custom-call | flops 3145728 | bytes 8388608 | tf_op jit(solution)/shard_map/norm/pallas_call | solution.py:310
  73.7 1.1 %place_far.3 = bf16[16,3,2,128,128]{4,3,2,1,0:T(8,128)(2,1)} custom-call(bf16[8,400,128]{2,1,0:T(8,128)(2,1)S(1)} %collective-permute-done.14.src, bf16[16,3,2,128,128]{4,3,2,1,0:T(8,128)(2,1)} %get-tuple-element.44.refs_0_), custom_call_target="tpu_custom_call", output_to_operand_aliasing={{}: (1, {})} | custom-call | bytes 3145728 | tf_op jit(solution)/shard_map/place_far/pallas_call | solution.py:384
  (23 shorter events, 0.2 us)
Async XLA Ops:
  4.2 21.0 %collective-permute-start = (bf16[8,400,128]{2,1,0:T(8,128)(2,1)S(1)}, bf16[8,400,128]{2,1,0:T(8,128)(2,1)}, u32[]{:S(2)}, u32[]{:S(2)}) collective-permute-start(bf16[8,400,128]{2,1,0:T(8,128)(2,1)S(1)} %get-tuple-element.26), channel_id=1, source_target_pairs={{0,16},{16,0},{32,48},{48,32},{64,80},{80,64},{96,112},{112,96},{1... | collective-permute-start | bytes 2457608 | tf_op jit(solution)/shard_map/ppermute | solution.py:423
  7.9 32.5 %all-to-all-start = ((bf16[8,400,128]{2,1,0:T(8,128)(2,1)}), bf16[8,400,128]{2,1,0:T(8,128)(2,1)S(1)}, u32[]{:S(2)}, u32[]{:S(2)}) async-start(bf16[8,400,128]{2,1,0:T(8,128)(2,1)} %touch.1), calls=%async_computation | async-start | bytes 1638400 | tf_op jit(solution)/shard_map/all_to_all | solution.py:413
  23.9 3.2 %collective-permute-start.1 = (bf16[8,96,512]{2,1,0:T(8,128)(2,1)S(1)}, bf16[8,96,512]{2,1,0:T(8,128)(2,1)S(1)}, u32[]{:S(2)}, u32[]{:S(2)}) collective-permute-start(bf16[8,96,512]{2,1,0:T(8,128)(2,1)S(1)} %get-tuple-element.29), channel_id=1, source_target_pairs={{0,1},{1,0},{2,3},{3,2},{4,5},{5,4},{6,7},{7,6},{8,9},{9,8},{10,11... | collective-permute-start | bytes 2359304 | tf_op jit(solution)/shard_map/ppermute | solution.py:427
  27.2 16.9 %copy-start.1 = (bf16[2,48,512]{2,1,0:T(8,128)(2,1)S(1)}, bf16[2,48,512]{2,1,0:T(8,128)(2,1)}, u32[]{:S(2)}) copy-start(bf16[2,48,512]{2,1,0:T(8,128)(2,1)} %param.11) | copy-start | bytes 294916
  27.7 16.2 %collective-permute-start.2 = (bf16[2,96,512]{2,1,0:T(8,128)(2,1)S(1)}, bf16[2,96,512]{2,1,0:T(8,128)(2,1)S(1)}, u32[]{:S(2)}, u32[]{:S(2)}) collective-permute-start(bf16[2,96,512]{2,1,0:T(8,128)(2,1)S(1)} %get-tuple-element.31), channel_id=1, source_target_pairs={{0,4},{1,5},{2,6},{3,7},{4,0},{5,1},{6,2},{7,3},{8,12},{9,13},{10,... | collective-permute-start | bytes 589832 | tf_op jit(solution)/shard_map/ppermute | solution.py:429
  30.6 13.3 %collective-permute-start.3 = (bf16[2,96,512]{2,1,0:T(8,128)(2,1)S(1)}, bf16[2,96,512]{2,1,0:T(8,128)(2,1)S(1)}, u32[]{:S(2)}, u32[]{:S(2)}) collective-permute-start(bf16[2,96,512]{2,1,0:T(8,128)(2,1)S(1)} %get-tuple-element.34), channel_id=1, source_target_pairs={{0,2},{1,3},{2,4},{3,5},{4,6},{5,7},{6,0},{7,1},{8,10},{9,11},{10,... | collective-permute-start | bytes 589832 | tf_op jit(solution)/shard_map/ppermute | solution.py:429
  31.0 38.6 %copy-start.2 = (bf16[8192]{0:T(1024)(128)(2,1)S(1)}, bf16[8192]{0:T(1024)(128)(2,1)}, u32[]{:S(2)}) copy-start(bf16[8192]{0:T(1024)(128)(2,1)} %param.17) | copy-start | bytes 49156
  31.0 12.9 %collective-permute-start.4 = (bf16[2,96,512]{2,1,0:T(8,128)(2,1)S(1)}, bf16[2,96,512]{2,1,0:T(8,128)(2,1)S(1)}, u32[]{:S(2)}, u32[]{:S(2)}) collective-permute-start(bf16[2,96,512]{2,1,0:T(8,128)(2,1)S(1)} %get-tuple-element.35), channel_id=1, source_target_pairs={{0,6},{1,7},{2,0},{3,1},{4,2},{5,3},{6,4},{7,5},{8,14},{9,15},{10,... | collective-permute-start | bytes 589832 | tf_op jit(solution)/shard_map/ppermute | solution.py:429
  40.4 27.8 %all-to-all-start.1 = ((bf16[8,400,128]{2,1,0:T(8,128)(2,1)}), bf16[8,400,128]{2,1,0:T(8,128)(2,1)S(1)}, u32[]{:S(2)}, u32[]{:S(2)}) async-start(bf16[8,400,128]{2,1,0:T(8,128)(2,1)} %collective-permute-done), calls=%async_computation.1 | async-start | bytes 1638400 | tf_op jit(solution)/shard_map/all_to_all | solution.py:413
  44.1 6.1 %collective-permute-start.5 = (bf16[2,96,512]{2,1,0:T(8,128)(2,1)S(1)}, bf16[2,96,512]{2,1,0:T(8,128)(2,1)S(1)}, u32[]{:S(2)}, u32[]{:S(2)}) collective-permute-start(bf16[2,96,512]{2,1,0:T(8,128)(2,1)S(1)} %pad_maximum_fusion), channel_id=1, source_target_pairs={{0,8},{1,9},{2,10},{3,11},{4,12},{5,13},{6,14},{7,15},{8,0},{9,1},... | collective-permute-start | bytes 589832 | tf_op jit(solution)/shard_map/ppermute | solution.py:437
  50.3 23.5 %copy-start = (bf16[1,96,512]{2,1,0:T(8,128)(2,1)}, bf16[1,96,512]{2,1,0:T(8,128)(2,1)S(1)}, u32[]{:S(2)}) copy-start(bf16[1,96,512]{2,1,0:T(8,128)(2,1)S(1)} %get-tuple-element.50) | copy-start | bytes 294916
  50.3 5.8 %collective-permute-start.7 = (bf16[8,400,128]{2,1,0:T(8,128)(2,1)S(1)}, bf16[8,400,128]{2,1,0:T(8,128)(2,1)S(1)}, u32[]{:S(2)}, u32[]{:S(2)}) collective-permute-start(bf16[8,400,128]{2,1,0:T(8,128)(2,1)S(1)} %all-to-all-done.mine), channel_id=1, source_target_pairs={{0,1},{1,0},{2,3},{3,2},{4,5},{5,4},{6,7},{7,6},{8,9},{9,8},{10,11... | collective-permute-start | bytes 2457608 | tf_op jit(solution)/shard_map/ppermute | solution.py:447
  51.7 8.0 %collective-permute-start.6 = (bf16[2,96,512]{2,1,0:T(8,128)(2,1)S(1)}, bf16[2,96,512]{2,1,0:T(8,128)(2,1)S(1)}, u32[]{:S(2)}, u32[]{:S(2)}) collective-permute-start(bf16[2,96,512]{2,1,0:T(8,128)(2,1)S(1)} %pad_maximum_fusion.1.refs_0_), channel_id=1, source_target_pairs={{0,4},{1,5},{2,6},{3,7},{4,0},{5,1},{6,2},{7,3},{8,12},{9,13},{10,... | collective-permute-start | bytes 589832 | tf_op jit(solution)/shard_map/ppermute | solution.py:444
  54.7 9.6 %collective-permute-start.8 = (bf16[2,96,512]{2,1,0:T(8,128)(2,1)S(1)}, bf16[2,96,512]{2,1,0:T(8,128)(2,1)S(1)}, u32[]{:S(2)}, u32[]{:S(2)}) collective-permute-start(bf16[2,96,512]{2,1,0:T(8,128)(2,1)S(1)} %pad_maximum_fusion.1.refs_0_), channel_id=1, source_target_pairs={{0,6},{1,7},{2,0},{3,1},{4,2},{5,3},{6,4},{7,5},{8,14},{9,15},{10,... | collective-permute-start | bytes 589832 | tf_op jit(solution)/shard_map/ppermute | solution.py:444
  55.4 8.9 %collective-permute-start.9 = (bf16[2,96,512]{2,1,0:T(8,128)(2,1)S(1)}, bf16[2,96,512]{2,1,0:T(8,128)(2,1)S(1)}, u32[]{:S(2)}, u32[]{:S(2)}) collective-permute-start(bf16[2,96,512]{2,1,0:T(8,128)(2,1)S(1)} %pad_maximum_fusion.1.refs_0_), channel_id=1, source_target_pairs={{0,2},{1,3},{2,4},{3,5},{4,6},{5,7},{6,0},{7,1},{8,10},{9,11},{10,... | collective-permute-start | bytes 589832 | tf_op jit(solution)/shard_map/ppermute | solution.py:444
  68.2 5.6 %collective-permute-start.14 = (bf16[8,400,128]{2,1,0:T(8,128)(2,1)S(1)}, bf16[8,400,128]{2,1,0:T(8,128)(2,1)S(1)}, u32[]{:S(2)}, u32[]{:S(2)}) collective-permute-start(bf16[8,400,128]{2,1,0:T(8,128)(2,1)S(1)} %all-to-all-done.1.src), channel_id=1, source_target_pairs={{0,1},{1,0},{2,3},{3,2},{4,5},{5,4},{6,7},{7,6},{8,9},{9,8},{10,11... | collective-permute-start | bytes 2457608 | tf_op jit(solution)/shard_map/ppermute | solution.py:452
  68.6 2.8 %collective-permute-start.10 = (bf16[2,96,512]{2,1,0:T(8,128)(2,1)S(1)}, bf16[2,96,512]{2,1,0:T(8,128)(2,1)S(1)}, u32[]{:S(2)}, u32[]{:S(2)}) collective-permute-start(bf16[2,96,512]{2,1,0:T(8,128)(2,1)S(1)} %pad_maximum_fusion.1.refs_0_), channel_id=1, source_target_pairs={{0,1},{1,0},{2,3},{3,2},{4,5},{5,4},{6,7},{7,6},{8,9},{9,8},{10,11... | collective-permute-start | bytes 589832 | tf_op jit(solution)/shard_map/ppermute | solution.py:449
  68.7 2.7 %collective-permute-start.11 = (bf16[2,96,512]{2,1,0:T(8,128)(2,1)S(1)}, bf16[2,96,512]{2,1,0:T(8,128)(2,1)S(1)}, u32[]{:S(2)}, u32[]{:S(2)}) collective-permute-start(bf16[2,96,512]{2,1,0:T(8,128)(2,1)S(1)} %collective-permute-done.8.refs_1_), channel_id=1, source_target_pairs={{0,1},{1,0},{2,3},{3,2},{4,5},{5,4},{6,7},{7,6},{8,9},{9,8},{10,11... | collective-permute-start | bytes 589832 | tf_op jit(solution)/shard_map/ppermute | solution.py:449
  69.2 2.3 %collective-permute-start.13 = (bf16[2,96,512]{2,1,0:T(8,128)(2,1)S(1)}, bf16[2,96,512]{2,1,0:T(8,128)(2,1)S(1)}, u32[]{:S(2)}, u32[]{:S(2)}) collective-permute-start(bf16[2,96,512]{2,1,0:T(8,128)(2,1)S(1)} %collective-permute-done.9.refs_3_), channel_id=1, source_target_pairs={{0,1},{1,0},{2,3},{3,2},{4,5},{5,4},{6,7},{7,6},{8,9},{9,8},{10,11... | collective-permute-start | bytes 589832 | tf_op jit(solution)/shard_map/ppermute | solution.py:449
  69.2 2.5 %collective-permute-start.12 = (bf16[2,96,512]{2,1,0:T(8,128)(2,1)S(1)}, bf16[2,96,512]{2,1,0:T(8,128)(2,1)S(1)}, u32[]{:S(2)}, u32[]{:S(2)}) collective-permute-start(bf16[2,96,512]{2,1,0:T(8,128)(2,1)S(1)} %collective-permute-done.6.refs_2_), channel_id=1, source_target_pairs={{0,1},{1,0},{2,3},{3,2},{4,5},{5,4},{6,7},{7,6},{8,9},{9,8},{10,11... | collective-permute-start | bytes 589832 | tf_op jit(solution)/shard_map/ppermute | solution.py:449

commit v5 on v4

--- a/solution.py
+++ b/solution.py
@@ -53,83 +53,69 @@
     return pltpu.CompilerParams(vmem_limit_bytes=mib << 20)
 
 
-def pack_kernel(tbl, blk, mv, nkv, kv, near_out, far, near, fresh, stage, sems, fsem, osem):
+def pack_kernel(far, tbl, blk, mv, nkv, kv, *refs):
+    if far:
+        buf, fresh, stage, sems, fsem = refs[-5:]
+    else:
+        out, buf, fresh, stage, sems, fsem, osems = refs
     tp = lax.axis_index("tp")
     core = lax.rem(tp, 2)
     side = lax.rem(lax.axis_index("inst"), 2)
+    slots = [mv[0, 2 * z + (1 - side if far else side)] for z in range(Z)]
+
+    def page_copy(z, b, page):
+        return pltpu.make_async_copy(
+            kv.at[page, core, 0], buf.at[z, pl.ds(b * PAGE, PAGE)], sems.at[z * MAXB + b]
+        )
+
     fcopy = pltpu.make_async_copy(
         nkv.at[:, :, :, pl.ds(pl.multiple_of(lax.div(tp, 2) * HD, HD), HD)], fresh, fsem
     )
     fcopy.start()
-
-    def page_copy(out, i, z, b, page):
-        return pltpu.make_async_copy(
-            kv.at[page, core, 0], out.at[z, pl.ds(b * PAGE, PAGE)], sems.at[(i * Z + z) * MAXB + b]
-        )
-
-    groups = [
-        (out, i, z, mv[0, 2 * z + (side if i == 0 else 1 - side)])
-        for i, out in enumerate((near, far))
-        for z in range(Z)
-    ]
-    for out, i, z, m in groups:
+    for z, m in enumerate(slots):
         for b in range(MAXB):
-            page_copy(out, i, z, b, tbl[b, m]).start()
+            page_copy(z, b, tbl[b, m]).start()
     stage[...] = jnp.zeros_like(stage)
     fcopy.wait()
-    for out, i, z, m in groups:
-        stage[i, z, 0:2] = fresh[0, m].astype(F32)
-        stage[i, z, 2:4] = fresh[1, m].astype(F32)
-    near[:, TOK:MSG] = stage[0].astype(BF16)
-    far[:, TOK:MSG] = stage[1].astype(BF16)
-    for n, (out, i, z, m) in enumerate(groups):
+    for z, m in enumerate(slots):
+        stage[z, 0:2] = fresh[0, m].astype(F32)
+        stage[z, 2:4] = fresh[1, m].astype(F32)
+    buf[:, TOK:MSG] = stage[...].astype(BF16)
+    copies = []
+    for z, m in enumerate(slots):
         count = blk[m]
-        if n == Z:
-            ocopy = pltpu.make_async_copy(near, near_out, osem)
-            ocopy.start()
         for b in range(MAXB):
-            page_copy(out, i, z, b, 0).wait()
+            page_copy(z, b, 0).wait()
             if b > 0:
                 @pl.when(b >= count)
                 def _():
-                    out[z, b * PAGE:(b + 1) * PAGE] = jnp.zeros((PAGE, HD), BF16)
-    ocopy.wait()
-
-
-def pack(table, blocks, moves, new_kv, kv_pages):
-    return pl.pallas_call(
-        pack_kernel,
-        out_shape=(pltpu.HBM((Z, MSG, HD), BF16), pltpu.VMEM((Z, MSG, HD), BF16)),
-        in_specs=[smem_spec()] * 3 + [any_spec()] * 2,
-        out_specs=(any_spec(), vmem_spec()),
-        scratch_shapes=[
-            pltpu.VMEM((Z, MSG, HD), BF16),
+                    buf[z, b * PAGE:(b + 1) * PAGE] = jnp.zeros((PAGE, HD), BF16)
+        if not far:
+            copies.append(pltpu.make_async_copy(buf.at[z], out.at[z], osems.at[z]))
+            copies[-1].start()
+    for copy in copies:
+        copy.wait()
+
+
+def pack(far, table, blocks, moves, new_kv, kv_pages, *first):
+    shape = (Z, MSG, HD)
+    return pl.pallas_call(
+        functools.partial(pack_kernel, far),
+        out_shape=pltpu.VMEM(shape, BF16) if far else pltpu.HBM(shape, BF16),
+        in_specs=[smem_spec()] * 3 + [any_spec()] * (2 + len(first)),
+        out_specs=vmem_spec() if far else any_spec(),
+        scratch_shapes=([] if far else [pltpu.VMEM(shape, BF16)])
+        + [
             pltpu.VMEM((STEPS, SLOTS, 2, HD), BF16),
-            pltpu.VMEM((2, Z, 16, HD), F32),
-            pltpu.SemaphoreType.DMA((2 * Z * MAXB,)),
+            pltpu.VMEM((Z, 16, HD), F32),
+            pltpu.SemaphoreType.DMA((Z * MAXB,)),
             pltpu.SemaphoreType.DMA,
-            pltpu.SemaphoreType.DMA,
-        ],
+        ]
+        + ([] if far else [pltpu.SemaphoreType.DMA((Z,))]),
         compiler_params=params(16),
-        cost_estimate=pl.CostEstimate(flops=0, bytes_accessed=4 << 20, transcendentals=0),
-        name="pack",
-    )(in_hbm(table), in_hbm(blocks), in_hbm(moves), in_hbm(new_kv), in_hbm(kv_pages))
-
-
-def touch_kernel(x, out):
-    del x, out
-
-
-def touch(x):
-    return pl.pallas_call(
-        touch_kernel,
-        out_shape=pltpu.HBM(x.shape, x.dtype),
-        in_specs=[any_spec()],
-        out_specs=any_spec(),
-        input_output_aliases={0: 0},
-        cost_estimate=pl.CostEstimate(flops=0, bytes_accessed=128 << 20, transcendentals=0),
-        name="touch",
-    )(in_hbm(x))
+        cost_estimate=pl.CostEstimate(flops=0, bytes_accessed=(128 if far else 1) << 20, transcendentals=0),
+        name="pack_far" if far else "pack_near",
+    )(in_hbm(table), in_hbm(blocks), in_hbm(moves), in_hbm(new_kv), in_hbm(kv_pages), *map(in_hbm, first))
 
 
 def place_of(tp):
@@ -142,7 +128,7 @@
     return (lax.rem(x + dx, 2) * 4 + lax.rem(y + dy, 4)) * 2 + parity
 
 
-def attend_kernel(tbl, blk, q_hbm, nkv, kv, w, send, heads, wb, kvb, fresh, qs, ks, sc, ob, q, kvsem, wsem, fsem, qsem):
+def attend_kernel(tbl, blk, q_hbm, nkv, kv, w, send_a, send_b, heads, wb, kvb, fresh, qs, ks, sc, ob, q, kvsem, wsem, fsem, qsem):
     tp = lax.axis_index("tp")
     core, x, y = place_of(tp)
     qcopy = pltpu.make_async_copy(q_hbm, q, qsem)
@@ -223,26 +209,28 @@
                 pl.ds(t * 2 + g, SLOTS, stride=4), :
             ].astype(BF16)
     wcopy.wait()
-    project(heads, wb, send, x, y, 1 - core)
-
-
-def project(heads, wb, out, x, y, parity):
+    sends = [ref.at[k] for ref in (send_a, send_b) for k in range(4)]
+    project(heads, wb, sends, x, y, 1 - core)
+
+
+def project(heads, wb, outs, x, y, parity):
     rows = heads[...]
     for k in range(CHIPS):
         cols = pl.ds(pl.multiple_of(block_of(x, y, k, parity) * SHARE, SHARE), SHARE)
-        out[k] = jnp.dot(rows, wb[:, cols], preferred_element_type=F32).astype(out.dtype)
+        outs[k][...] = jnp.dot(rows, wb[:, cols], preferred_element_type=F32).astype(outs[k].dtype)
 
 
 def attend(table, blocks, query, new_kv, kv_pages, out_weight):
     return pl.pallas_call(
         attend_kernel,
         out_shape=(
-            pltpu.VMEM((CHIPS, ROWS, SHARE), BF16),
+            pltpu.VMEM((4, ROWS, SHARE), BF16),
+            pltpu.VMEM((4, ROWS, SHARE), BF16),
             pltpu.VMEM((ROWS, 2 * HD), BF16),
             pltpu.VMEM((2 * HD, D), BF16),
         ),
         in_specs=[smem_spec()] * 2 + [any_spec()] * 4,
-        out_specs=(vmem_spec(),) * 3,
+        out_specs=(vmem_spec(),) * 4,
         scratch_shapes=[
             pltpu.VMEM((2, PAGES, PAGE, HD), BF16),
             pltpu.VMEM((STEPS, SLOTS, 2, HD), BF16),
@@ -262,37 +250,39 @@
     )(in_hbm(table), in_hbm(blocks), in_hbm(query), in_hbm(new_kv), in_hbm(kv_pages), in_hbm(out_weight))
 
 
-def own_kernel(heads, wb, got, *outs):
+def own_kernel(heads, wb, got_a, got_b, *outs):
     core, x, y = place_of(lax.axis_index("tp"))
     rows = heads[...]
     for k in range(CHIPS):
         cols = pl.ds(pl.multiple_of(block_of(x, y, k, core) * SHARE, SHARE), SHARE)
-        part = jnp.dot(rows, wb[:, cols], preferred_element_type=F32) + got[k].astype(F32)
+        part = jnp.dot(rows, wb[:, cols], preferred_element_type=F32)
+        part = part + (got_a, got_b)[k // 4][k % 4].astype(F32)
         outs[k // 2][k % 2] = part.astype(outs[k // 2].dtype)
 
 
-def own(heads, wb, got):
+def own(heads, wb, got_a, got_b):
     return pl.pallas_call(
         own_kernel,
         out_shape=tuple(pltpu.VMEM((2, ROWS, SHARE), F32 if dy == 0 else BF16) for dy in range(4)),
-        in_specs=[vmem_spec()] * 3,
+        in_specs=[vmem_spec()] * 4,
         out_specs=(vmem_spec(),) * 4,
         compiler_params=params(16),
         cost_estimate=pl.CostEstimate(flops=1, bytes_accessed=1, transcendentals=0),
         name="own",
-    )(in_vmem(heads), in_vmem(wb), in_vmem(got))
-
-
-def norm_kernel(gain, *refs):
-    blocks, (normed, buf, nsem) = refs[:8], refs[8:]
+    )(in_vmem(heads), in_vmem(wb), in_vmem(got_a), in_vmem(got_b))
+
+
+def finish_kernel(gain, near_rows, far, far_other, into, *refs):
+    blocks, (normed, arrived, tail, buf, sems, nsem) = refs[:8], refs[8:]
     core, x, y = place_of(lax.axis_index("tp"))
+    side = lax.rem(lax.axis_index("inst"), 2)
+    copies = half_copies(far_other, arrived, 1 - side, 1 - core, sems, 0)
     squares = jnp.zeros((ROWS, SHARE), F32)
     for ref in blocks:
         for dx in range(2):
             v = ref[dx].astype(F32)
             squares = squares + v * v
     scale = lax.rsqrt(jnp.sum(squares, axis=-1, keepdims=True) / D + EPSILON)
-    copies = []
     for part in range(2):
         for k in range(CHIPS):
             block = block_of(x, y, k, core if part == 0 else 1 - core)
@@ -302,24 +292,33 @@
             copy = pltpu.make_async_copy(buf.at[:, at], normed.at[:, at], nsem.at[part * CHIPS + k])
             copy.start()
             copies.append(copy)
+    for z in range(Z):
+        tail[2 * z + side] = near_rows[z].astype(BF16)
+        tail[2 * z + 1 - side] = far[z, TOK:MSG].astype(F32)[0:4].astype(BF16)
     for copy in copies:
         copy.wait()
 
 
-def norm(gain, mine, other):
-    return pl.pallas_call(
-        norm_kernel,
-        out_shape=pltpu.HBM((ROWS, D), BF16),
-        in_specs=[vmem_spec()] * 9,
-        out_specs=any_spec(),
+def finish(gain, near_rows, far, far_other, into, mine, other):
+    return pl.pallas_call(
+        finish_kernel,
+        out_shape=(
+            pltpu.HBM((ROWS, D), BF16),
+            pltpu.HBM((INST, MAXB, 2, PAGE, HD), BF16),
+            jax.ShapeDtypeStruct((INST, 4, HD), BF16),
+        ),
+        in_specs=[vmem_spec()] * 4 + [any_spec()] + [vmem_spec()] * 8,
+        out_specs=(any_spec(), any_spec(), vmem_spec()),
         scratch_shapes=[
             pltpu.VMEM((ROWS, D), BF16),
+            pltpu.SemaphoreType.DMA((Z * MAXB,)),
             pltpu.SemaphoreType.DMA((2 * CHIPS,)),
         ],
+        input_output_aliases={4: 1},
         compiler_params=params(24),
         cost_estimate=pl.CostEstimate(flops=4 * ROWS * D, bytes_accessed=8 << 20, transcendentals=0),
-        name="norm",
-    )(gain.reshape(1, D), *mine, *other)
+        name="finish",
+    )(gain.reshape(1, D), near_rows, far, far_other, into, *mine, *other)
 
 
 def half_copies(src, out, way, half, sems, first):
@@ -364,34 +363,25 @@
     )(mine, other)
 
 
-def place_far_kernel(other, src, *refs):
-    out, sems = refs[-2:] if other else (refs[-3], refs[-1])
+def place_far_kernel(src, into, out, sems):
     core = lax.rem(lax.axis_index("tp"), 2)
     side = lax.rem(lax.axis_index("inst"), 2)
-    copies = half_copies(src, out, 1 - side, 1 - core if other else core, sems, 0)
-    if not other:
-        rows, tail = refs[0], refs[-2]
-        for z in range(Z):
-            tail[2 * z + side] = rows[z].astype(BF16)
-            tail[2 * z + 1 - side] = src[z, TOK:MSG].astype(F32)[0:4].astype(BF16)
-    for copy in copies:
+    for copy in half_copies(src, out, 1 - side, core, sems, 0):
         copy.wait()
 
 
-def place_far(src, into, rows=None):
-    whole = pltpu.HBM((INST, MAXB, 2, PAGE, HD), BF16)
-    own_half = rows is not None
-    return pl.pallas_call(
-        functools.partial(place_far_kernel, not own_half),
-        out_shape=(whole, jax.ShapeDtypeStruct((INST, 4, HD), BF16)) if own_half else whole,
-        in_specs=[vmem_spec()] * (2 if own_half else 1) + [any_spec()],
-        out_specs=(any_spec(), vmem_spec()) if own_half else any_spec(),
+def place_far(src, into):
+    return pl.pallas_call(
+        place_far_kernel,
+        out_shape=pltpu.HBM((INST, MAXB, 2, PAGE, HD), BF16),
+        in_specs=[vmem_spec(), any_spec()],
+        out_specs=any_spec(),
         scratch_shapes=[pltpu.SemaphoreType.DMA((Z * MAXB,))],
-        input_output_aliases={2 if own_half else 1: 0},
+        input_output_aliases={1: 0},
         compiler_params=params(8),
         cost_estimate=pl.CostEstimate(flops=0, bytes_accessed=3 << 20, transcendentals=0),
         name="place_far",
-    )(src, *((rows,) if own_half else ()), into)
+    )(src, into)
 
 
 def tp_perm(dx, dy, dc):
@@ -419,15 +409,15 @@
 
 def local(query, new_kv, residual, kv_pages, block_table, blocks, moves, out_weight, norm_gain):
     table = block_table.T
-    near, far = pack(table, blocks, moves, new_kv, kv_pages)
-    far = lax.ppermute(far, "inst", SIDES)
-    near = along_z(touch(near))
-
-    send, heads, weight = attend(table, blocks, query, new_kv, kv_pages, out_weight)
-    got = lax.ppermute(send, "tp", SWAP)
-    sums = own(after(heads, far), weight, got)
+    near = pack(False, table, blocks, moves, new_kv, kv_pages)
+    far = lax.ppermute(pack(True, table, blocks, moves, new_kv, kv_pages, near), "inst", SIDES)
+    near = along_z(near)
+
+    *sends, heads, weight = attend(table, blocks, query, new_kv, kv_pages, out_weight)
+    got = [lax.ppermute(send, "tp", SWAP) for send in sends]
+    sums = own(heads, weight, *got)
     terms = [lax.ppermute(sums[dy], "tp", tp_perm(0, dy, 0)) for dy in AROUND]
-    terms[0] = after(terms[0], near)
+    terms[0] = after(terms[0], near, far)
     far = along_z(after(far, sums[1]))
     total = sums[0]
     for term in terms:
@@ -447,11 +437,10 @@
     arrived, rows = place_near(near, lax.ppermute(near, "tp", SWAP))
     mine[2], arrived, hidden = lax.optimization_barrier((mine[2], arrived, hidden))
     other = [lax.ppermute(block, "tp", SWAP) for block in mine]
-    normed = norm(norm_gain, mine, other)
-    far = after(far, *mine)
+    far = after(far, *mine, other[3], other[0])
     far_other = lax.ppermute(far, "tp", SWAP)
-    arrived, tail = place_far(far, arrived, rows)
-    arrived = place_far(far_other, arrived)
+    arrived = place_far(far, arrived)
+    normed, arrived, tail = finish(norm_gain, rows, far, far_other, arrived, mine, other)
     return (
         hidden,
         normed.reshape(STEPS, SLOTS, D),

time: 75.2 us -> 72.4 us (0.963)
  waiting for transfers between devices: 25.4 us -> 14.8 us
  starting transfers between devices: 30.1 us -> 37 us
  Pallas kernels: 18.2 us -> 19 us
    all_to_all x2, waiting for transfers between devices: 10.9 us -> 2.05 us  [along_z(): lax.all_to_all(x, 'inst', 0, 0, tiled=True, axis_index_groups=Z_GROUPS)]
    ppermute x1, waiting for transfers between devices: 5.67 us -> 3.31 us  [local(): cross = lax.ppermute(part, 'tp', CROSS)]
    ppermute x1, starting transfers between devices: 1.43 us -> 3.68 us  [local(): arrived, rows = place_near(near, lax.ppermute(near, 'tp', SWAP))]
    all_to_all x2, starting transfers between devices: 11.7 us -> 13.8 us  [along_z(): lax.all_to_all(x, 'inst', 0, 0, tiled=True, axis_index_groups=Z_GROUPS)]
    ppermute x1, starting transfers between devices: 0.49 us -> 2.54 us  [local(): far_other = lax.ppermute(far, 'tp', SWAP)]
    ppermute x2 -> x3, waiting for transfers between devices: 1.91 us -> 3.45 us  [the longest x2 1.81 us: local(): got = [lax.ppermute(send, 'tp', SWAP) for send in sends]]
    ppermute x3, waiting for transfers between devices: 6.61 us -> 5.12 us  [local(): mine[dy] = lax.ppermute(pair, 'tp', tp_perm(0, 4 - dy, 0))]
    ppermute x3, starting transfers between devices: 5.64 us -> 4.43 us  [local(): terms = [lax.ppermute(sums[dy], 'tp', tp_perm(0, dy, 0)) for dy in AROUND]]
  transfers between devices with their start and end apart: 17 -> 18, of which waited for: 7 -> 10; matrix products, arithmetic and copies ran while one was open for 0% -> 0% of each run, Pallas kernels for 18% -> 18%
where the time goes in v5:
time: 72.4 us; the launch traced here: 72 us
  starting transfers between devices  37 us (51%)
  Pallas kernels  19 us (26%)
  waiting for transfers between devices  14.8 us (20%)
  between operations  0.94 us (1%)
    all_to_all x2, starting transfers between devices, along_z(): lax.all_to_all(x, 'inst', 0, 0, tiled=True, axis_index_groups=Z_GROUPS)  13.8 us
    pallas_call x1, Pallas kernels, attend(): pl.pallas_call(attend_kernel, out_shape=(pltpu.VMEM((4, ROWS, SHARE), BF1...  7.85 us
    pallas_call x2, Pallas kernels, pack(): pl.pallas_call(functools.partial(pack_kernel, far), out_shape=pltpu.VMEM(...  5.3 us
    ppermute x3, waiting for transfers between devices, local(): mine[dy] = lax.ppermute(pair, 'tp', tp_perm(0, 4 - dy, 0))  5.12 us
    ppermute x3, starting transfers between devices, local(): mine[dy] = lax.ppermute(pair, 'tp', tp_perm(0, 4 - dy, 0))  5 us
    ppermute x3, starting transfers between devices, local(): terms = [lax.ppermute(sums[dy], 'tp', tp_perm(0, dy, 0)) for dy in AROUND]  4.43 us
    ppermute x1, starting transfers between devices, local(): arrived, rows = place_near(near, lax.ppermute(near, 'tp', SWAP))  3.68 us
    ppermute x1, waiting for transfers between devices, local(): cross = lax.ppermute(part, 'tp', CROSS)  3.31 us
  transfers between devices with their start and end apart: 18, of which 10 were waited for; matrix products, arithmetic and copies ran while one was open for 0% of the time, Pallas kernels for 18%

profile of v5, /device:TPU:1, one launch (start us, length us, event | category | flops | bytes accessed | tf_op | source)
XLA Modules:
  0.0 72.0 jit_solution(15432328737365584839)
XLA Ops:
  0.6 3.1 %pack_near.1.refs_0_ = bf16[8,400,128]{2,1,0:T(8,128)(2,1)} custom-call(s32[3,48]{1,0:T(4,128)} %bitcast.16, s32[48]{0:T(128)} %blk.5, s32[1,16]{1,0:T(1,128)} %mv.3, bf16[2,48,2,1024]{3,2,1,0:T(2,128)(2,1)} %nkv.5, bf16[144,2,1,128,128]{4,3,2,1,0:T(8,128)(2,1)} %kv.5), custom_call_target="tpu_custom_call" | custom-call | bytes 1048576 | tf_op jit(solution)/shard_map/pack_near/pallas_call | solution.py:102
  3.7 9.0 %all-to-all-start = ((bf16[8,400,128]{2,1,0:T(8,128)(2,1)}), bf16[8,400,128]{2,1,0:T(8,128)(2,1)S(1)}, u32[]{:S(2)}, u32[]{:S(2)}) async-start(bf16[8,400,128]{2,1,0:T(8,128)(2,1)} %pack_near.1.refs_0_), calls=%async_computation | async-start | bytes 1638400 | tf_op jit(solution)/shard_map/all_to_all | solution.py:403
  12.7 2.2 %pack_far.1 = bf16[8,400,128]{2,1,0:T(8,128)(2,1)S(1)} custom-call(s32[3,48]{1,0:T(4,128)} %bitcast.17, s32[48]{0:T(128)} %blk.5, s32[1,16]{1,0:T(1,128)} %mv.3, bf16[2,48,2,1024]{3,2,1,0:T(2,128)(2,1)} %nkv.5, bf16[144,2,1,128,128]{4,3,2,1,0:T(8,128)(2,1)} %kv.5, bf16[8,400,128]{2,1,0:T(8,128)(2,1)} %pack_near.1.refs_0_), custom_call_target="tpu_custom_call" | custom-call | bytes 134217728 | tf_op jit(solution)/shard_map/pack_far/pallas_call | solution.py:102
  15.0 2.8 %collective-permute-start.3 = (bf16[8,400,128]{2,1,0:T(8,128)(2,1)S(1)}, bf16[8,400,128]{2,1,0:T(8,128)(2,1)}, u32[]{:S(2)}, u32[]{:S(2)}) collective-permute-start(bf16[8,400,128]{2,1,0:T(8,128)(2,1)S(1)} %pack_far.1), channel_id=1, source_target_pairs={{0,16},{16,0},{32,48},{48,32},{64,80},{80,64},{96,112},{112,96},{1... | collective-permute-start | bytes 2457608 | tf_op jit(solution)/shard_map/ppermute | solution.py:413
  17.8 7.9 %attend.1 = (bf16[4,96,512]{2,1,0:T(8,128)(2,1)S(1)}, bf16[4,96,512]{2,1,0:T(8,128)(2,1)S(1)}, bf16[96,256]{1,0:T(8,128)(2,1)S(1)}, bf16[256,8192]{1,0:T(8,128)(2,1)S(1)}) custom-call(s32[3,48]{1,0:T(4,128)} %bitcast.18, s32[48]{0:T(128)} %blk.5, bf16[2,48,256]{2,1,0:T(8,128)(2,1)} %q_hbm.1, bf16[2,48,2,1024]{3,2,1,0:T(2,128)(2,1)} %nkv.5, ...), custom_call_target="tpu_custom_call" | custom-call | flops 10000000000 | bytes 67108864 | tf_op jit(solution)/shard_map/attend/pallas_call | solution.py:224
  25.7 1.3 %collective-permute-start = (bf16[4,96,512]{2,1,0:T(8,128)(2,1)S(1)}, bf16[4,96,512]{2,1,0:T(8,128)(2,1)S(1)}, u32[]{:S(2)}, u32[]{:S(2)}) collective-permute-start(bf16[4,96,512]{2,1,0:T(8,128)(2,1)S(1)} %get-tuple-element.26), channel_id=1, source_target_pairs={{0,1},{1,0},{2,3},{3,2},{4,5},{5,4},{6,7},{7,6},{8,9},{9,8},{10,11... | collective-permute-start | bytes 1179656 | tf_op jit(solution)/shard_map/ppermute | solution.py:417
  27.1 1.2 %collective-permute-done.got_a = bf16[4,96,512]{2,1,0:T(8,128)(2,1)S(1)} collective-permute-done((bf16[4,96,512]{2,1,0:T(8,128)(2,1)S(1)}, bf16[4,96,512]{2,1,0:T(8,128)(2,1)S(1)}, u32[]{:S(2)}, u32[]{:S(2)}) %collective-permute-start) | collective-permute-done | bytes 393248 | tf_op jit(solution)/shard_map/ppermute | solution.py:417
  28.3 0.6 collective-permute-done.1.got_b
  28.9 0.5 own.1
  29.4 3.0 %collective-permute-start.2 = (bf16[2,96,512]{2,1,0:T(8,128)(2,1)S(1)}, bf16[2,96,512]{2,1,0:T(8,128)(2,1)S(1)}, u32[]{:S(2)}, u32[]{:S(2)}) collective-permute-start(bf16[2,96,512]{2,1,0:T(8,128)(2,1)S(1)} %get-tuple-element.29), channel_id=1, source_target_pairs={{0,4},{1,5},{2,6},{3,7},{4,0},{5,1},{6,2},{7,3},{8,12},{9,13},{10,... | collective-permute-start | bytes 589832 | tf_op jit(solution)/shard_map/ppermute | solution.py:419
  32.3 0.8 %collective-permute-start.5 = (bf16[2,96,512]{2,1,0:T(8,128)(2,1)S(1)}, bf16[2,96,512]{2,1,0:T(8,128)(2,1)S(1)}, u32[]{:S(2)}, u32[]{:S(2)}) collective-permute-start(bf16[2,96,512]{2,1,0:T(8,128)(2,1)S(1)} %get-tuple-element.32), channel_id=1, source_target_pairs={{0,6},{1,7},{2,0},{3,1},{4,2},{5,3},{6,4},{7,5},{8,14},{9,15},{10,... | collective-permute-start | bytes 589832 | tf_op jit(solution)/shard_map/ppermute | solution.py:419
  33.1 0.7 collective-permute-start.4
  33.8 1.6 %collective-permute-done.3 = bf16[8,400,128]{2,1,0:T(8,128)(2,1)} collective-permute-done((bf16[8,400,128]{2,1,0:T(8,128)(2,1)S(1)}, bf16[8,400,128]{2,1,0:T(8,128)(2,1)}, u32[]{:S(2)}, u32[]{:S(2)}) %collective-permute-start.3) | collective-permute-done | bytes 819232 | tf_op jit(solution)/shard_map/ppermute | solution.py:413
  35.5 1.6 %all-to-all-done.mine = bf16[8,400,128]{2,1,0:T(8,128)(2,1)S(1)} async-done(((bf16[8,400,128]{2,1,0:T(8,128)(2,1)}), bf16[8,400,128]{2,1,0:T(8,128)(2,1)S(1)}, u32[]{:S(2)}, u32[]{:S(2)}) %all-to-all-start) | async-done | bytes 819232 | tf_op jit(solution)/shard_map/all_to_all | solution.py:403
  37.0 4.8 %all-to-all-start.1 = ((bf16[8,400,128]{2,1,0:T(8,128)(2,1)}), bf16[8,400,128]{2,1,0:T(8,128)(2,1)S(1)}, u32[]{:S(2)}, u32[]{:S(2)}) async-start(bf16[8,400,128]{2,1,0:T(8,128)(2,1)} %collective-permute-done.3), calls=%async_computation.1 | async-start | bytes 1638400 | tf_op jit(solution)/shard_map/all_to_all | solution.py:403
  42.0 1.3 %collective-permute-start.6 = (bf16[2,96,512]{2,1,0:T(8,128)(2,1)S(1)}, bf16[2,96,512]{2,1,0:T(8,128)(2,1)S(1)}, u32[]{:S(2)}, u32[]{:S(2)}) collective-permute-start(bf16[2,96,512]{2,1,0:T(8,128)(2,1)S(1)} %pad_maximum_fusion), channel_id=1, source_target_pairs={{0,8},{1,9},{2,10},{3,11},{4,12},{5,13},{6,14},{7,15},{8,0},{9,1},... | collective-permute-start | bytes 589832 | tf_op jit(solution)/shard_map/ppermute | solution.py:427
  43.3 3.3 %collective-permute-done.6 = bf16[2,96,512]{2,1,0:T(8,128)(2,1)S(1)} collective-permute-done((bf16[2,96,512]{2,1,0:T(8,128)(2,1)S(1)}, bf16[2,96,512]{2,1,0:T(8,128)(2,1)S(1)}, u32[]{:S(2)}, u32[]{:S(2)}) %collective-permute-start.6) | collective-permute-done | bytes 196640 | tf_op jit(solution)/shard_map/ppermute | solution.py:427
  46.7 3.7 %collective-permute-start.8 = (bf16[8,400,128]{2,1,0:T(8,128)(2,1)S(1)}, bf16[8,400,128]{2,1,0:T(8,128)(2,1)S(1)}, u32[]{:S(2)}, u32[]{:S(2)}) collective-permute-start(bf16[8,400,128]{2,1,0:T(8,128)(2,1)S(1)} %all-to-all-done.mine), channel_id=1, source_target_pairs={{0,1},{1,0},{2,3},{3,2},{4,5},{5,4},{6,7},{7,6},{8,9},{9,8},{10,11... | collective-permute-start | bytes 2457608 | tf_op jit(solution)/shard_map/ppermute | solution.py:437
  50.4 1.3 %collective-permute-start.10 = (bf16[2,96,512]{2,1,0:T(8,128)(2,1)S(1)}, bf16[2,96,512]{2,1,0:T(8,128)(2,1)S(1)}, u32[]{:S(2)}, u32[]{:S(2)}) collective-permute-start(bf16[2,96,512]{2,1,0:T(8,128)(2,1)S(1)} %pad_maximum_fusion.1.refs_0_), channel_id=1, source_target_pairs={{0,2},{1,3},{2,4},{3,5},{4,6},{5,7},{6,0},{7,1},{8,10},{9,11},{10,... | collective-permute-start | bytes 589832 | tf_op jit(solution)/shard_map/ppermute | solution.py:434
  51.7 2.6 %collective-permute-start.7 = (bf16[2,96,512]{2,1,0:T(8,128)(2,1)S(1)}, bf16[2,96,512]{2,1,0:T(8,128)(2,1)S(1)}, u32[]{:S(2)}, u32[]{:S(2)}) collective-permute-start(bf16[2,96,512]{2,1,0:T(8,128)(2,1)S(1)} %pad_maximum_fusion.1.refs_0_), channel_id=1, source_target_pairs={{0,4},{1,5},{2,6},{3,7},{4,0},{5,1},{6,2},{7,3},{8,12},{9,13},{10,... | collective-permute-start | bytes 589832 | tf_op jit(solution)/shard_map/ppermute | solution.py:434
  54.3 0.6 collective-permute-start.12
  55.0 1.1 %collective-permute-start.9 = (bf16[2,96,512]{2,1,0:T(8,128)(2,1)S(1)}, bf16[2,96,512]{2,1,0:T(8,128)(2,1)S(1)}, u32[]{:S(2)}, u32[]{:S(2)}) collective-permute-start(bf16[2,96,512]{2,1,0:T(8,128)(2,1)S(1)} %pad_maximum_fusion.1.refs_0_), channel_id=1, source_target_pairs={{0,6},{1,7},{2,0},{3,1},{4,2},{5,3},{6,4},{7,5},{8,14},{9,15},{10,... | collective-permute-start | bytes 589832 | tf_op jit(solution)/shard_map/ppermute | solution.py:434
  56.0 2.1 %collective-permute-done.10.refs_3_ = bf16[2,96,512]{2,1,0:T(8,128)(2,1)S(1)} collective-permute-done((bf16[2,96,512]{2,1,0:T(8,128)(2,1)S(1)}, bf16[2,96,512]{2,1,0:T(8,128)(2,1)S(1)}, u32[]{:S(2)}, u32[]{:S(2)}) %collective-permute-start.10) | collective-permute-done | bytes 196640 | tf_op jit(solution)/shard_map/ppermute | solution.py:434
  58.2 0.8 %collective-permute-start.11 = (bf16[2,96,512]{2,1,0:T(8,128)(2,1)S(1)}, bf16[2,96,512]{2,1,0:T(8,128)(2,1)S(1)}, u32[]{:S(2)}, u32[]{:S(2)}) collective-permute-start(bf16[2,96,512]{2,1,0:T(8,128)(2,1)S(1)} %collective-permute-done.10.refs_3_), channel_id=1, source_target_pairs={{0,1},{1,0},{2,3},{3,2},{4,5},{5,4},{6,7},{7,6},{8,9},{9,8},{10,11... | collective-permute-start | bytes 589832 | tf_op jit(solution)/shard_map/ppermute | solution.py:439
  59.0 1.5 %place_near.1 = (bf16[16,3,2,128,128]{4,3,2,1,0:T(8,128)(2,1)}, f32[8,4,128]{2,1,0:T(4,128)S(1)}) custom-call(bf16[8,400,128]{2,1,0:T(8,128)(2,1)S(1)} %all-to-all-done.mine, bf16[8,400,128]{2,1,0:T(8,128)(2,1)S(1)} %collective-permute-done.8.other), custom_call_target="tpu_custom_call" | custom-call | bytes 3145728 | tf_op jit(solution)/shard_map/place_near/pallas_call | solution.py:351
  60.6 3.0 %collective-permute-done.7.refs_2_ = bf16[2,96,512]{2,1,0:T(8,128)(2,1)S(1)} collective-permute-done((bf16[2,96,512]{2,1,0:T(8,128)(2,1)S(1)}, bf16[2,96,512]{2,1,0:T(8,128)(2,1)S(1)}, u32[]{:S(2)}, u32[]{:S(2)}) %collective-permute-start.7) | collective-permute-done | bytes 196640 | tf_op jit(solution)/shard_map/ppermute | solution.py:434
  63.6 0.5 all-to-all-done.1.src.far
  64.1 2.5 %collective-permute-start.13 = (bf16[8,400,128]{2,1,0:T(8,128)(2,1)S(1)}, bf16[8,400,128]{2,1,0:T(8,128)(2,1)S(1)}, u32[]{:S(2)}, u32[]{:S(2)}) collective-permute-start(bf16[8,400,128]{2,1,0:T(8,128)(2,1)S(1)} %all-to-all-done.1.src.far), channel_id=1, source_target_pairs={{0,1},{1,0},{2,3},{3,2},{4,5},{5,4},{6,7},{7,6},{8,9},{9,8},{10,11... | collective-permute-start | bytes 2457608 | tf_op jit(solution)/shard_map/ppermute | solution.py:441
  66.6 0.5 collective-permute-start.15
  67.1 1.1 %place_far.1.into = bf16[16,3,2,128,128]{4,3,2,1,0:T(8,128)(2,1)} custom-call(bf16[8,400,128]{2,1,0:T(8,128)(2,1)S(1)} %all-to-all-done.1.src.far, bf16[16,3,2,128,128]{4,3,2,1,0:T(8,128)(2,1)} %get-tuple-element.40.into), custom_call_target="tpu_custom_call", output_to_operand_aliasing={{}: (1, {})} | custom-call | bytes 3145728 | tf_op jit(solution)/shard_map/place_far/pallas_call | solution.py:374
  68.2 0.6 collective-permute-done.14.refs_5_
  69.1 2.7 %finish.1 = (bf16[96,8192]{1,0:T(8,128)(2,1)}, bf16[16,3,2,128,128]{4,3,2,1,0:T(8,128)(2,1)}, bf16[16,4,128]{2,1,0:T(4,128)(2,1)}) custom-call(bf16[1,8192]{1,0:T(2,128)(2,1)S(1)} %reshape.39.gain, f32[8,4,128]{2,1,0:T(4,128)S(1)} %get-tuple-element.36.near_rows, bf16[8,400,128]{2,1,0:T(8,128)(2,1)S(1)} %all-to-all-done.1.src.far, ...), custom_call_target="tpu_custom_call", output_to_operand_aliasing={{1}: (4, {})} | custom-call | flops 3145728 | bytes 8388608 | tf_op jit(solution)/shard_map/finish/pallas_call | solution.py:303
  (24 shorter events, 0.7 us)
Async XLA Ops:
  3.7 33.3 %all-to-all-start = ((bf16[8,400,128]{2,1,0:T(8,128)(2,1)}), bf16[8,400,128]{2,1,0:T(8,128)(2,1)S(1)}, u32[]{:S(2)}, u32[]{:S(2)}) async-start(bf16[8,400,128]{2,1,0:T(8,128)(2,1)} %pack_near.1.refs_0_), calls=%async_computation | async-start | bytes 1638400 | tf_op jit(solution)/shard_map/all_to_all | solution.py:403
  15.0 20.5 %collective-permute-start.3 = (bf16[8,400,128]{2,1,0:T(8,128)(2,1)S(1)}, bf16[8,400,128]{2,1,0:T(8,128)(2,1)}, u32[]{:S(2)}, u32[]{:S(2)}) collective-permute-start(bf16[8,400,128]{2,1,0:T(8,128)(2,1)S(1)} %pack_far.1), channel_id=1, source_target_pairs={{0,16},{16,0},{32,48},{48,32},{64,80},{80,64},{96,112},{112,96},{1... | collective-permute-start | bytes 2457608 | tf_op jit(solution)/shard_map/ppermute | solution.py:413
  25.7 2.7 %collective-permute-start = (bf16[4,96,512]{2,1,0:T(8,128)(2,1)S(1)}, bf16[4,96,512]{2,1,0:T(8,128)(2,1)S(1)}, u32[]{:S(2)}, u32[]{:S(2)}) collective-permute-start(bf16[4,96,512]{2,1,0:T(8,128)(2,1)S(1)} %get-tuple-element.26), channel_id=1, source_target_pairs={{0,1},{1,0},{2,3},{3,2},{4,5},{5,4},{6,7},{7,6},{8,9},{9,8},{10,11... | collective-permute-start | bytes 1179656 | tf_op jit(solution)/shard_map/ppermute | solution.py:417
  27.0 1.9 %collective-permute-start.1 = (bf16[4,96,512]{2,1,0:T(8,128)(2,1)S(1)}, bf16[4,96,512]{2,1,0:T(8,128)(2,1)S(1)}, u32[]{:S(2)}, u32[]{:S(2)}) collective-permute-start(bf16[4,96,512]{2,1,0:T(8,128)(2,1)S(1)} %get-tuple-element.27), channel_id=1, source_target_pairs={{0,1},{1,0},{2,3},{3,2},{4,5},{5,4},{6,7},{7,6},{8,9},{9,8},{10,11... | collective-permute-start | bytes 1179656 | tf_op jit(solution)/shard_map/ppermute | solution.py:417
  28.9 13.1 %copy-start.1 = (bf16[2,48,512]{2,1,0:T(8,128)(2,1)S(1)}, bf16[2,48,512]{2,1,0:T(8,128)(2,1)}, u32[]{:S(2)}) copy-start(bf16[2,48,512]{2,1,0:T(8,128)(2,1)} %param.11) | copy-start | bytes 294916
  29.4 12.4 %collective-permute-start.2 = (bf16[2,96,512]{2,1,0:T(8,128)(2,1)S(1)}, bf16[2,96,512]{2,1,0:T(8,128)(2,1)S(1)}, u32[]{:S(2)}, u32[]{:S(2)}) collective-permute-start(bf16[2,96,512]{2,1,0:T(8,128)(2,1)S(1)} %get-tuple-element.29), channel_id=1, source_target_pairs={{0,4},{1,5},{2,6},{3,7},{4,0},{5,1},{6,2},{7,3},{8,12},{9,13},{10,... | collective-permute-start | bytes 589832 | tf_op jit(solution)/shard_map/ppermute | solution.py:419
  32.3 9.5 %collective-permute-start.5 = (bf16[2,96,512]{2,1,0:T(8,128)(2,1)S(1)}, bf16[2,96,512]{2,1,0:T(8,128)(2,1)S(1)}, u32[]{:S(2)}, u32[]{:S(2)}) collective-permute-start(bf16[2,96,512]{2,1,0:T(8,128)(2,1)S(1)} %get-tuple-element.32), channel_id=1, source_target_pairs={{0,6},{1,7},{2,0},{3,1},{4,2},{5,3},{6,4},{7,5},{8,14},{9,15},{10,... | collective-permute-start | bytes 589832 | tf_op jit(solution)/shard_map/ppermute | solution.py:419
  33.1 34.0 %copy-start.2 = (bf16[8192]{0:T(1024)(128)(2,1)S(1)}, bf16[8192]{0:T(1024)(128)(2,1)}, u32[]{:S(2)}) copy-start(bf16[8192]{0:T(1024)(128)(2,1)} %param.17) | copy-start | bytes 49156
  33.1 8.7 %collective-permute-start.4 = (bf16[2,96,512]{2,1,0:T(8,128)(2,1)S(1)}, bf16[2,96,512]{2,1,0:T(8,128)(2,1)S(1)}, u32[]{:S(2)}, u32[]{:S(2)}) collective-permute-start(bf16[2,96,512]{2,1,0:T(8,128)(2,1)S(1)} %get-tuple-element.31), channel_id=1, source_target_pairs={{0,2},{1,3},{2,4},{3,5},{4,6},{5,7},{6,0},{7,1},{8,10},{9,11},{10,... | collective-permute-start | bytes 589832 | tf_op jit(solution)/shard_map/ppermute | solution.py:419
  37.0 27.0 %all-to-all-start.1 = ((bf16[8,400,128]{2,1,0:T(8,128)(2,1)}), bf16[8,400,128]{2,1,0:T(8,128)(2,1)S(1)}, u32[]{:S(2)}, u32[]{:S(2)}) async-start(bf16[8,400,128]{2,1,0:T(8,128)(2,1)} %collective-permute-done.3), calls=%async_computation.1 | async-start | bytes 1638400 | tf_op jit(solution)/shard_map/all_to_all | solution.py:403
  42.0 4.6 %collective-permute-start.6 = (bf16[2,96,512]{2,1,0:T(8,128)(2,1)S(1)}, bf16[2,96,512]{2,1,0:T(8,128)(2,1)S(1)}, u32[]{:S(2)}, u32[]{:S(2)}) collective-permute-start(bf16[2,96,512]{2,1,0:T(8,128)(2,1)S(1)} %pad_maximum_fusion), channel_id=1, source_target_pairs={{0,8},{1,9},{2,10},{3,11},{4,12},{5,13},{6,14},{7,15},{8,0},{9,1},... | collective-permute-start | bytes 589832 | tf_op jit(solution)/shard_map/ppermute | solution.py:427
  46.7 21.5 %copy-start = (bf16[1,96,512]{2,1,0:T(8,128)(2,1)}, bf16[1,96,512]{2,1,0:T(8,128)(2,1)S(1)}, u32[]{:S(2)}) copy-start(bf16[1,96,512]{2,1,0:T(8,128)(2,1)S(1)} %get-tuple-element.48) | copy-start | bytes 294916
  46.7 12.3 %collective-permute-start.8 = (bf16[8,400,128]{2,1,0:T(8,128)(2,1)S(1)}, bf16[8,400,128]{2,1,0:T(8,128)(2,1)S(1)}, u32[]{:S(2)}, u32[]{:S(2)}) collective-permute-start(bf16[8,400,128]{2,1,0:T(8,128)(2,1)S(1)} %all-to-all-done.mine), channel_id=1, source_target_pairs={{0,1},{1,0},{2,3},{3,2},{4,5},{5,4},{6,7},{7,6},{8,9},{9,8},{10,11... | collective-permute-start | bytes 2457608 | tf_op jit(solution)/shard_map/ppermute | solution.py:437
  50.4 7.8 %collective-permute-start.10 = (bf16[2,96,512]{2,1,0:T(8,128)(2,1)S(1)}, bf16[2,96,512]{2,1,0:T(8,128)(2,1)S(1)}, u32[]{:S(2)}, u32[]{:S(2)}) collective-permute-start(bf16[2,96,512]{2,1,0:T(8,128)(2,1)S(1)} %pad_maximum_fusion.1.refs_0_), channel_id=1, source_target_pairs={{0,2},{1,3},{2,4},{3,5},{4,6},{5,7},{6,0},{7,1},{8,10},{9,11},{10,... | collective-permute-start | bytes 589832 | tf_op jit(solution)/shard_map/ppermute | solution.py:434
  51.7 11.8 %collective-permute-start.7 = (bf16[2,96,512]{2,1,0:T(8,128)(2,1)S(1)}, bf16[2,96,512]{2,1,0:T(8,128)(2,1)S(1)}, u32[]{:S(2)}, u32[]{:S(2)}) collective-permute-start(bf16[2,96,512]{2,1,0:T(8,128)(2,1)S(1)} %pad_maximum_fusion.1.refs_0_), channel_id=1, source_target_pairs={{0,4},{1,5},{2,6},{3,7},{4,0},{5,1},{6,2},{7,3},{8,12},{9,13},{10,... | collective-permute-start | bytes 589832 | tf_op jit(solution)/shard_map/ppermute | solution.py:434
  54.3 9.2 %collective-permute-start.12 = (bf16[2,96,512]{2,1,0:T(8,128)(2,1)S(1)}, bf16[2,96,512]{2,1,0:T(8,128)(2,1)S(1)}, u32[]{:S(2)}, u32[]{:S(2)}) collective-permute-start(bf16[2,96,512]{2,1,0:T(8,128)(2,1)S(1)} %pad_maximum_fusion.1.refs_0_), channel_id=1, source_target_pairs={{0,1},{1,0},{2,3},{3,2},{4,5},{5,4},{6,7},{7,6},{8,9},{9,8},{10,11... | collective-permute-start | bytes 589832 | tf_op jit(solution)/shard_map/ppermute | solution.py:439
  55.0 8.6 %collective-permute-start.9 = (bf16[2,96,512]{2,1,0:T(8,128)(2,1)S(1)}, bf16[2,96,512]{2,1,0:T(8,128)(2,1)S(1)}, u32[]{:S(2)}, u32[]{:S(2)}) collective-permute-start(bf16[2,96,512]{2,1,0:T(8,128)(2,1)S(1)} %pad_maximum_fusion.1.refs_0_), channel_id=1, source_target_pairs={{0,6},{1,7},{2,0},{3,1},{4,2},{5,3},{6,4},{7,5},{8,14},{9,15},{10,... | collective-permute-start | bytes 589832 | tf_op jit(solution)/shard_map/ppermute | solution.py:434
  58.2 5.4 %collective-permute-start.11 = (bf16[2,96,512]{2,1,0:T(8,128)(2,1)S(1)}, bf16[2,96,512]{2,1,0:T(8,128)(2,1)S(1)}, u32[]{:S(2)}, u32[]{:S(2)}) collective-permute-start(bf16[2,96,512]{2,1,0:T(8,128)(2,1)S(1)} %collective-permute-done.10.refs_3_), channel_id=1, source_target_pairs={{0,1},{1,0},{2,3},{3,2},{4,5},{5,4},{6,7},{7,6},{8,9},{9,8},{10,11... | collective-permute-start | bytes 589832 | tf_op jit(solution)/shard_map/ppermute | solution.py:439
  64.1 5.1 %collective-permute-start.13 = (bf16[8,400,128]{2,1,0:T(8,128)(2,1)S(1)}, bf16[8,400,128]{2,1,0:T(8,128)(2,1)S(1)}, u32[]{:S(2)}, u32[]{:S(2)}) collective-permute-start(bf16[8,400,128]{2,1,0:T(8,128)(2,1)S(1)} %all-to-all-done.1.src.far), channel_id=1, source_target_pairs={{0,1},{1,0},{2,3},{3,2},{4,5},{5,4},{6,7},{7,6},{8,9},{9,8},{10,11... | collective-permute-start | bytes 2457608 | tf_op jit(solution)/shard_map/ppermute | solution.py:441
  66.6 2.2 %collective-permute-start.14 = (bf16[2,96,512]{2,1,0:T(8,128)(2,1)S(1)}, bf16[2,96,512]{2,1,0:T(8,128)(2,1)S(1)}, u32[]{:S(2)}, u32[]{:S(2)}) collective-permute-start(bf16[2,96,512]{2,1,0:T(8,128)(2,1)S(1)} %collective-permute-done.9.refs_1_), channel_id=1, source_target_pairs={{0,1},{1,0},{2,3},{3,2},{4,5},{5,4},{6,7},{7,6},{8,9},{9,8},{10,11... | collective-permute-start | bytes 589832 | tf_op jit(solution)/shard_map/ppermute | solution.py:439
  66.6 2.5 %collective-permute-start.15 = (bf16[2,96,512]{2,1,0:T(8,128)(2,1)S(1)}, bf16[2,96,512]{2,1,0:T(8,128)(2,1)S(1)}, u32[]{:S(2)}, u32[]{:S(2)}) collective-permute-start(bf16[2,96,512]{2,1,0:T(8,128)(2,1)S(1)} %collective-permute-done.7.refs_2_), channel_id=1, source_target_pairs={{0,1},{1,0},{2,3},{3,2},{4,5},{5,4},{6,7},{7,6},{8,9},{9,8},{10,11... | collective-permute-start | bytes 589832 | tf_op jit(solution)/shard_map/ppermute | solution.py:439

commit v6 on v5

--- a/solution.py
+++ b/solution.py
@@ -272,16 +272,24 @@
     )(in_vmem(heads), in_vmem(wb), in_vmem(got_a), in_vmem(got_b))
 
 
-def finish_kernel(gain, near_rows, far, far_other, into, *refs):
+EARLY = (0, 1, 2, 3, 4, 7)
+
+
+def block_squares(refs):
+    squares = jnp.zeros((ROWS, SHARE), F32)
+    for ref in refs:
+        for dx in range(2):
+            v = ref[dx].astype(F32)
+            squares = squares + v * v
+    return squares
+
+
+def finish_kernel(gain, early, near_rows, far, far_other, into, *refs):
     blocks, (normed, arrived, tail, buf, sems, nsem) = refs[:8], refs[8:]
     core, x, y = place_of(lax.axis_index("tp"))
     side = lax.rem(lax.axis_index("inst"), 2)
     copies = half_copies(far_other, arrived, 1 - side, 1 - core, sems, 0)
-    squares = jnp.zeros((ROWS, SHARE), F32)
-    for ref in blocks:
-        for dx in range(2):
-            v = ref[dx].astype(F32)
-            squares = squares + v * v
+    squares = early[...] + block_squares([blocks[k] for k in range(8) if k not in EARLY])
     scale = lax.rsqrt(jnp.sum(squares, axis=-1, keepdims=True) / D + EPSILON)
     for part in range(2):
         for k in range(CHIPS):
@@ -299,7 +307,7 @@
         copy.wait()
 
 
-def finish(gain, near_rows, far, far_other, into, mine, other):
+def finish(gain, early, near_rows, far, far_other, into, mine, other):
     return pl.pallas_call(
         finish_kernel,
         out_shape=(
@@ -307,18 +315,18 @@
             pltpu.HBM((INST, MAXB, 2, PAGE, HD), BF16),
             jax.ShapeDtypeStruct((INST, 4, HD), BF16),
         ),
-        in_specs=[vmem_spec()] * 4 + [any_spec()] + [vmem_spec()] * 8,
+        in_specs=[vmem_spec()] * 5 + [any_spec()] + [vmem_spec()] * 8,
         out_specs=(any_spec(), any_spec(), vmem_spec()),
         scratch_shapes=[
             pltpu.VMEM((ROWS, D), BF16),
             pltpu.SemaphoreType.DMA((Z * MAXB,)),
             pltpu.SemaphoreType.DMA((2 * CHIPS,)),
         ],
-        input_output_aliases={4: 1},
+        input_output_aliases={5: 1},
         compiler_params=params(24),
         cost_estimate=pl.CostEstimate(flops=4 * ROWS * D, bytes_accessed=8 << 20, transcendentals=0),
         name="finish",
-    )(gain.reshape(1, D), near_rows, far, far_other, into, *mine, *other)
+    )(gain.reshape(1, D), early, near_rows, far, far_other, into, *mine, *other)
 
 
 def half_copies(src, out, way, half, sems, first):
@@ -363,25 +371,31 @@
     )(mine, other)
 
 
-def place_far_kernel(src, into, out, sems):
+def place_far_kernel(src, into, *refs):
+    blocks, (out, early, sems) = refs[:-3], refs[-3:]
     core = lax.rem(lax.axis_index("tp"), 2)
     side = lax.rem(lax.axis_index("inst"), 2)
-    for copy in half_copies(src, out, 1 - side, core, sems, 0):
+    copies = half_copies(src, out, 1 - side, core, sems, 0)
+    early[...] = block_squares(blocks)
+    for copy in copies:
         copy.wait()
 
 
-def place_far(src, into):
+def place_far(src, into, blocks):
     return pl.pallas_call(
         place_far_kernel,
-        out_shape=pltpu.HBM((INST, MAXB, 2, PAGE, HD), BF16),
-        in_specs=[vmem_spec(), any_spec()],
-        out_specs=any_spec(),
+        out_shape=(
+            pltpu.HBM((INST, MAXB, 2, PAGE, HD), BF16),
+            pltpu.VMEM((ROWS, SHARE), F32),
+        ),
+        in_specs=[vmem_spec(), any_spec()] + [vmem_spec()] * len(blocks),
+        out_specs=(any_spec(), vmem_spec()),
         scratch_shapes=[pltpu.SemaphoreType.DMA((Z * MAXB,))],
         input_output_aliases={1: 0},
         compiler_params=params(8),
         cost_estimate=pl.CostEstimate(flops=0, bytes_accessed=3 << 20, transcendentals=0),
         name="place_far",
-    )(src, into)
+    )(src, into, *blocks)
 
 
 def tp_perm(dx, dy, dc):
@@ -433,14 +447,15 @@
     for dy in AROUND:
         mine[dy] = lax.ppermute(pair, "tp", tp_perm(0, 4 - dy, 0))
     mine = [mine[dy] for dy in range(4)]
-    near = after(near, pair)
+    near = after(near, part)
     arrived, rows = place_near(near, lax.ppermute(near, "tp", SWAP))
     mine[2], arrived, hidden = lax.optimization_barrier((mine[2], arrived, hidden))
     other = [lax.ppermute(block, "tp", SWAP) for block in mine]
     far = after(far, *mine, other[3], other[0])
     far_other = lax.ppermute(far, "tp", SWAP)
-    arrived = place_far(far, arrived)
-    normed, arrived, tail = finish(norm_gain, rows, far, far_other, arrived, mine, other)
+    blocks = [*mine, *other]
+    arrived, early = place_far(far, arrived, [blocks[k] for k in EARLY])
+    normed, arrived, tail = finish(norm_gain, early, rows, far, far_other, arrived, mine, other)
     return (
         hidden,
         normed.reshape(STEPS, SLOTS, D),

time: 72.4 us -> 72.2 us (level)
  starting transfers between devices: 37 us -> 41.7 us
  waiting for transfers between devices: 14.8 us -> 10.1 us
    ppermute x4, starting transfers between devices: 1.96 us -> 7.39 us  [local(): other = [lax.ppermute(block, 'tp', SWAP) for block in mine]]
    ppermute x3, waiting for transfers between devices: 5.12 us -> 1.26 us  [local(): mine[dy] = lax.ppermute(pair, 'tp', tp_perm(0, 4 - dy, 0))]
    ppermute x1, waiting for transfers between devices: 3.31 us -> 0.59 us  [local(): cross = lax.ppermute(part, 'tp', CROSS)]
    all_to_all x2, waiting for transfers between devices: 2.05 us -> 3.96 us  [along_z(): lax.all_to_all(x, 'inst', 0, 0, tiled=True, axis_index_groups=Z_GROUPS)]
    ppermute x1, starting transfers between devices: 3.68 us -> 2.72 us  [local(): arrived, rows = place_near(near, lax.ppermute(near, 'tp', SWAP))]
  transfers between devices with their start and end apart: 18 -> 18, of which waited for: 10 -> 9; matrix products, arithmetic and copies ran while one was open for 0% -> 0% of each run, Pallas kernels for 18% -> 18%
where the time goes in v6:
time: 72.2 us; the launch traced here: 71.8 us
  starting transfers between devices  41.7 us (58%)
  Pallas kernels  18.8 us (26%)
  waiting for transfers between devices  10.1 us (14%)
  between operations  0.95 us (1%)
    all_to_all x2, starting transfers between devices, along_z(): lax.all_to_all(x, 'inst', 0, 0, tiled=True, axis_index_groups=Z_GROUPS)  13.8 us
    pallas_call x1, Pallas kernels, attend(): pl.pallas_call(attend_kernel, out_shape=(pltpu.VMEM((4, ROWS, SHARE), BF1...  7.85 us
    ppermute x4, starting transfers between devices, local(): other = [lax.ppermute(block, 'tp', SWAP) for block in mine]  7.39 us
    pallas_call x2, Pallas kernels, pack(): pl.pallas_call(functools.partial(pack_kernel, far), out_shape=pltpu.VMEM(...  5.29 us
    ppermute x3, starting transfers between devices, local(): mine[dy] = lax.ppermute(pair, 'tp', tp_perm(0, 4 - dy, 0))  5.2 us
    ppermute x3, starting transfers between devices, local(): terms = [lax.ppermute(sums[dy], 'tp', tp_perm(0, dy, 0)) for dy in AROUND]  4.43 us
    all_to_all x2, waiting for transfers between devices, along_z(): lax.all_to_all(x, 'inst', 0, 0, tiled=True, axis_index_groups=Z_GROUPS)  3.96 us
    ppermute x1, starting transfers between devices, local(): lax.ppermute(pack(True, table, blocks, moves, new_kv, kv_pages, near), 'i...  2.83 us
  transfers between devices with their start and end apart: 18, of which 9 were waited for; matrix products, arithmetic and copies ran while one was open for 0% of the time, Pallas kernels for 18%

profile of v6, /device:TPU:1, one launch (start us, length us, event | category | flops | bytes accessed | tf_op | source)
XLA Modules:
  0.0 71.8 jit_solution(7435310440742900059)
XLA Ops:
  0.6 3.1 %pack_near.1.refs_0_ = bf16[8,400,128]{2,1,0:T(8,128)(2,1)} custom-call(s32[3,48]{1,0:T(4,128)} %bitcast.16, s32[48]{0:T(128)} %blk.5, s32[1,16]{1,0:T(1,128)} %mv.3, bf16[2,48,2,1024]{3,2,1,0:T(2,128)(2,1)} %nkv.5, bf16[144,2,1,128,128]{4,3,2,1,0:T(8,128)(2,1)} %kv.5), custom_call_target="tpu_custom_call" | custom-call | bytes 1048576 | tf_op jit(solution)/shard_map/pack_near/pallas_call | solution.py:102
  3.7 9.0 %all-to-all-start = ((bf16[8,400,128]{2,1,0:T(8,128)(2,1)}), bf16[8,400,128]{2,1,0:T(8,128)(2,1)S(1)}, u32[]{:S(2)}, u32[]{:S(2)}) async-start(bf16[8,400,128]{2,1,0:T(8,128)(2,1)} %pack_near.1.refs_0_), calls=%async_computation | async-start | bytes 1638400 | tf_op jit(solution)/shard_map/all_to_all | solution.py:417
  12.7 2.2 %pack_far.1 = bf16[8,400,128]{2,1,0:T(8,128)(2,1)S(1)} custom-call(s32[3,48]{1,0:T(4,128)} %bitcast.17, s32[48]{0:T(128)} %blk.5, s32[1,16]{1,0:T(1,128)} %mv.3, bf16[2,48,2,1024]{3,2,1,0:T(2,128)(2,1)} %nkv.5, bf16[144,2,1,128,128]{4,3,2,1,0:T(8,128)(2,1)} %kv.5, bf16[8,400,128]{2,1,0:T(8,128)(2,1)} %pack_near.1.refs_0_), custom_call_target="tpu_custom_call" | custom-call | bytes 134217728 | tf_op jit(solution)/shard_map/pack_far/pallas_call | solution.py:102
  15.0 2.8 %collective-permute-start.3 = (bf16[8,400,128]{2,1,0:T(8,128)(2,1)S(1)}, bf16[8,400,128]{2,1,0:T(8,128)(2,1)}, u32[]{:S(2)}, u32[]{:S(2)}) collective-permute-start(bf16[8,400,128]{2,1,0:T(8,128)(2,1)S(1)} %pack_far.1), channel_id=1, source_target_pairs={{0,16},{16,0},{32,48},{48,32},{64,80},{80,64},{96,112},{112,96},{1... | collective-permute-start | bytes 2457608 | tf_op jit(solution)/shard_map/ppermute | solution.py:427
  17.8 7.9 %attend.1 = (bf16[4,96,512]{2,1,0:T(8,128)(2,1)S(1)}, bf16[4,96,512]{2,1,0:T(8,128)(2,1)S(1)}, bf16[96,256]{1,0:T(8,128)(2,1)S(1)}, bf16[256,8192]{1,0:T(8,128)(2,1)S(1)}) custom-call(s32[3,48]{1,0:T(4,128)} %bitcast.18, s32[48]{0:T(128)} %blk.5, bf16[2,48,256]{2,1,0:T(8,128)(2,1)} %q_hbm.1, bf16[2,48,2,1024]{3,2,1,0:T(2,128)(2,1)} %nkv.5, ...), custom_call_target="tpu_custom_call" | custom-call | flops 10000000000 | bytes 67108864 | tf_op jit(solution)/shard_map/attend/pallas_call | solution.py:224
  25.7 1.3 %collective-permute-start = (bf16[4,96,512]{2,1,0:T(8,128)(2,1)S(1)}, bf16[4,96,512]{2,1,0:T(8,128)(2,1)S(1)}, u32[]{:S(2)}, u32[]{:S(2)}) collective-permute-start(bf16[4,96,512]{2,1,0:T(8,128)(2,1)S(1)} %get-tuple-element.28), channel_id=1, source_target_pairs={{0,1},{1,0},{2,3},{3,2},{4,5},{5,4},{6,7},{7,6},{8,9},{9,8},{10,11... | collective-permute-start | bytes 1179656 | tf_op jit(solution)/shard_map/ppermute | solution.py:431
  27.1 1.2 %collective-permute-done.got_a = bf16[4,96,512]{2,1,0:T(8,128)(2,1)S(1)} collective-permute-done((bf16[4,96,512]{2,1,0:T(8,128)(2,1)S(1)}, bf16[4,96,512]{2,1,0:T(8,128)(2,1)S(1)}, u32[]{:S(2)}, u32[]{:S(2)}) %collective-permute-start) | collective-permute-done | bytes 393248 | tf_op jit(solution)/shard_map/ppermute | solution.py:431
  28.3 0.6 collective-permute-done.1.got_b
  28.9 0.5 own.1
  29.4 3.0 %collective-permute-start.2 = (bf16[2,96,512]{2,1,0:T(8,128)(2,1)S(1)}, bf16[2,96,512]{2,1,0:T(8,128)(2,1)S(1)}, u32[]{:S(2)}, u32[]{:S(2)}) collective-permute-start(bf16[2,96,512]{2,1,0:T(8,128)(2,1)S(1)} %get-tuple-element.31), channel_id=1, source_target_pairs={{0,4},{1,5},{2,6},{3,7},{4,0},{5,1},{6,2},{7,3},{8,12},{9,13},{10,... | collective-permute-start | bytes 589832 | tf_op jit(solution)/shard_map/ppermute | solution.py:433
  32.3 0.8 %collective-permute-start.5 = (bf16[2,96,512]{2,1,0:T(8,128)(2,1)S(1)}, bf16[2,96,512]{2,1,0:T(8,128)(2,1)S(1)}, u32[]{:S(2)}, u32[]{:S(2)}) collective-permute-start(bf16[2,96,512]{2,1,0:T(8,128)(2,1)S(1)} %get-tuple-element.34), channel_id=1, source_target_pairs={{0,6},{1,7},{2,0},{3,1},{4,2},{5,3},{6,4},{7,5},{8,14},{9,15},{10,... | collective-permute-start | bytes 589832 | tf_op jit(solution)/shard_map/ppermute | solution.py:433
  33.1 0.7 collective-permute-start.4
  33.8 1.6 %collective-permute-done.3 = bf16[8,400,128]{2,1,0:T(8,128)(2,1)} collective-permute-done((bf16[8,400,128]{2,1,0:T(8,128)(2,1)S(1)}, bf16[8,400,128]{2,1,0:T(8,128)(2,1)}, u32[]{:S(2)}, u32[]{:S(2)}) %collective-permute-start.3) | collective-permute-done | bytes 819232 | tf_op jit(solution)/shard_map/ppermute | solution.py:427
  35.5 1.6 %all-to-all-done.mine = bf16[8,400,128]{2,1,0:T(8,128)(2,1)S(1)} async-done(((bf16[8,400,128]{2,1,0:T(8,128)(2,1)}), bf16[8,400,128]{2,1,0:T(8,128)(2,1)S(1)}, u32[]{:S(2)}, u32[]{:S(2)}) %all-to-all-start) | async-done | bytes 819232 | tf_op jit(solution)/shard_map/all_to_all | solution.py:417
  37.0 4.8 %all-to-all-start.1 = ((bf16[8,400,128]{2,1,0:T(8,128)(2,1)}), bf16[8,400,128]{2,1,0:T(8,128)(2,1)S(1)}, u32[]{:S(2)}, u32[]{:S(2)}) async-start(bf16[8,400,128]{2,1,0:T(8,128)(2,1)} %collective-permute-done.3), calls=%async_computation.1 | async-start | bytes 1638400 | tf_op jit(solution)/shard_map/all_to_all | solution.py:417
  42.0 1.3 %collective-permute-start.6 = (bf16[2,96,512]{2,1,0:T(8,128)(2,1)S(1)}, bf16[2,96,512]{2,1,0:T(8,128)(2,1)S(1)}, u32[]{:S(2)}, u32[]{:S(2)}) collective-permute-start(bf16[2,96,512]{2,1,0:T(8,128)(2,1)S(1)} %pad_maximum_fusion), channel_id=1, source_target_pairs={{0,8},{1,9},{2,10},{3,11},{4,12},{5,13},{6,14},{7,15},{8,0},{9,1},... | collective-permute-start | bytes 589832 | tf_op jit(solution)/shard_map/ppermute | solution.py:441
  43.3 2.7 %collective-permute-start.8 = (bf16[8,400,128]{2,1,0:T(8,128)(2,1)S(1)}, bf16[8,400,128]{2,1,0:T(8,128)(2,1)S(1)}, u32[]{:S(2)}, u32[]{:S(2)}) collective-permute-start(bf16[8,400,128]{2,1,0:T(8,128)(2,1)S(1)} %all-to-all-done.mine), channel_id=1, source_target_pairs={{0,1},{1,0},{2,3},{3,2},{4,5},{5,4},{6,7},{7,6},{8,9},{9,8},{10,11... | collective-permute-start | bytes 2457608 | tf_op jit(solution)/shard_map/ppermute | solution.py:451
  46.1 0.6 collective-permute-done.6
  46.7 1.5 %collective-permute-start.10 = (bf16[2,96,512]{2,1,0:T(8,128)(2,1)S(1)}, bf16[2,96,512]{2,1,0:T(8,128)(2,1)S(1)}, u32[]{:S(2)}, u32[]{:S(2)}) collective-permute-start(bf16[2,96,512]{2,1,0:T(8,128)(2,1)S(1)} %pad_maximum_fusion.1.refs_0_), channel_id=1, source_target_pairs={{0,2},{1,3},{2,4},{3,5},{4,6},{5,7},{6,0},{7,1},{8,10},{9,11},{10,... | collective-permute-start | bytes 589832 | tf_op jit(solution)/shard_map/ppermute | solution.py:448
  48.3 2.6 %collective-permute-start.7 = (bf16[2,96,512]{2,1,0:T(8,128)(2,1)S(1)}, bf16[2,96,512]{2,1,0:T(8,128)(2,1)S(1)}, u32[]{:S(2)}, u32[]{:S(2)}) collective-permute-start(bf16[2,96,512]{2,1,0:T(8,128)(2,1)S(1)} %pad_maximum_fusion.1.refs_0_), channel_id=1, source_target_pairs={{0,4},{1,5},{2,6},{3,7},{4,0},{5,1},{6,2},{7,3},{8,12},{9,13},{10,... | collective-permute-start | bytes 589832 | tf_op jit(solution)/shard_map/ppermute | solution.py:448
  50.9 4.0 %collective-permute-start.12 = (bf16[2,96,512]{2,1,0:T(8,128)(2,1)S(1)}, bf16[2,96,512]{2,1,0:T(8,128)(2,1)S(1)}, u32[]{:S(2)}, u32[]{:S(2)}) collective-permute-start(bf16[2,96,512]{2,1,0:T(8,128)(2,1)S(1)} %pad_maximum_fusion.1.refs_0_), channel_id=1, source_target_pairs={{0,1},{1,0},{2,3},{3,2},{4,5},{5,4},{6,7},{7,6},{8,9},{9,8},{10,11... | collective-permute-start | bytes 589832 | tf_op jit(solution)/shard_map/ppermute | solution.py:453
  54.9 1.1 %collective-permute-start.9 = (bf16[2,96,512]{2,1,0:T(8,128)(2,1)S(1)}, bf16[2,96,512]{2,1,0:T(8,128)(2,1)S(1)}, u32[]{:S(2)}, u32[]{:S(2)}) collective-permute-start(bf16[2,96,512]{2,1,0:T(8,128)(2,1)S(1)} %pad_maximum_fusion.1.refs_0_), channel_id=1, source_target_pairs={{0,6},{1,7},{2,0},{3,1},{4,2},{5,3},{6,4},{7,5},{8,14},{9,15},{10,... | collective-permute-start | bytes 589832 | tf_op jit(solution)/shard_map/ppermute | solution.py:448
  56.0 2.9 %collective-permute-start.11 = (bf16[2,96,512]{2,1,0:T(8,128)(2,1)S(1)}, bf16[2,96,512]{2,1,0:T(8,128)(2,1)S(1)}, u32[]{:S(2)}, u32[]{:S(2)}) collective-permute-start(bf16[2,96,512]{2,1,0:T(8,128)(2,1)S(1)} %collective-permute-done.10.refs_3_), channel_id=1, source_target_pairs={{0,1},{1,0},{2,3},{3,2},{4,5},{5,4},{6,7},{7,6},{8,9},{9,8},{10,11... | collective-permute-start | bytes 589832 | tf_op jit(solution)/shard_map/ppermute | solution.py:453
  58.8 1.5 %place_near.1 = (bf16[16,3,2,128,128]{4,3,2,1,0:T(8,128)(2,1)}, f32[8,4,128]{2,1,0:T(4,128)S(1)}) custom-call(bf16[8,400,128]{2,1,0:T(8,128)(2,1)S(1)} %all-to-all-done.mine, bf16[8,400,128]{2,1,0:T(8,128)(2,1)S(1)} %collective-permute-done.8.other), custom_call_target="tpu_custom_call" | custom-call | bytes 3145728 | tf_op jit(solution)/shard_map/place_near/pallas_call | solution.py:359
  60.4 1.3 %collective-permute-done.9.refs_1_ = bf16[2,96,512]{2,1,0:T(8,128)(2,1)S(1)} collective-permute-done((bf16[2,96,512]{2,1,0:T(8,128)(2,1)S(1)}, bf16[2,96,512]{2,1,0:T(8,128)(2,1)S(1)}, u32[]{:S(2)}, u32[]{:S(2)}) %collective-permute-start.9) | collective-permute-done | bytes 196640 | tf_op jit(solution)/shard_map/ppermute | solution.py:448
  61.7 2.4 %all-to-all-done.1.src.far = bf16[8,400,128]{2,1,0:T(8,128)(2,1)S(1)} async-done(((bf16[8,400,128]{2,1,0:T(8,128)(2,1)}), bf16[8,400,128]{2,1,0:T(8,128)(2,1)S(1)}, u32[]{:S(2)}, u32[]{:S(2)}) %all-to-all-start.1) | async-done | bytes 819232 | tf_op jit(solution)/shard_map/all_to_all | solution.py:417
  64.1 2.5 %collective-permute-start.13 = (bf16[8,400,128]{2,1,0:T(8,128)(2,1)S(1)}, bf16[8,400,128]{2,1,0:T(8,128)(2,1)S(1)}, u32[]{:S(2)}, u32[]{:S(2)}) collective-permute-start(bf16[8,400,128]{2,1,0:T(8,128)(2,1)S(1)} %all-to-all-done.1.src.far), channel_id=1, source_target_pairs={{0,1},{1,0},{2,3},{3,2},{4,5},{5,4},{6,7},{7,6},{8,9},{9,8},{10,11... | collective-permute-start | bytes 2457608 | tf_op jit(solution)/shard_map/ppermute | solution.py:455
  66.6 0.5 collective-permute-start.15
  67.1 1.1 %place_far.1 = (bf16[16,3,2,128,128]{4,3,2,1,0:T(8,128)(2,1)}, f32[96,512]{1,0:T(8,128)S(1)}) custom-call(bf16[8,400,128]{2,1,0:T(8,128)(2,1)S(1)} %all-to-all-done.1.src.far, bf16[16,3,2,128,128]{4,3,2,1,0:T(8,128)(2,1)} %get-tuple-element.41.into, bf16[2,96,512]{2,1,0:T(8,128)(2,1)S(1)} %pad_maximum_fusion.1.refs_0_, ...), custom_call_target="tpu_custom_call", output_to_operand_aliasing={{0}: (1, {})} | custom-call | bytes 3145728 | tf_op jit(solution)/shard_map/place_far/pallas_call | solution.py:385
  68.2 0.6 collective-permute-done.14.refs_5_
  68.8 0.3 collective-permute-done.15.refs_6_
  69.1 2.5 %finish.1 = (bf16[96,8192]{1,0:T(8,128)(2,1)}, bf16[16,3,2,128,128]{4,3,2,1,0:T(8,128)(2,1)}, bf16[16,4,128]{2,1,0:T(4,128)(2,1)}) custom-call(bf16[1,8192]{1,0:T(2,128)(2,1)S(1)} %reshape.39.gain, f32[96,512]{1,0:T(8,128)S(1)} %get-tuple-element.42.early, f32[8,4,128]{2,1,0:T(4,128)S(1)} %get-tuple-element.43.near_rows, ...), custom_call_target="tpu_custom_call", output_to_operand_aliasing={{1}: (5, {})} | custom-call | flops 3145728 | bytes 8388608 | tf_op jit(solution)/shard_map/finish/pallas_call | solution.py:311
  (24 shorter events, 0.4 us)
Async XLA Ops:
  3.7 33.3 %all-to-all-start = ((bf16[8,400,128]{2,1,0:T(8,128)(2,1)}), bf16[8,400,128]{2,1,0:T(8,128)(2,1)S(1)}, u32[]{:S(2)}, u32[]{:S(2)}) async-start(bf16[8,400,128]{2,1,0:T(8,128)(2,1)} %pack_near.1.refs_0_), calls=%async_computation | async-start | bytes 1638400 | tf_op jit(solution)/shard_map/all_to_all | solution.py:417
  15.0 20.5 %collective-permute-start.3 = (bf16[8,400,128]{2,1,0:T(8,128)(2,1)S(1)}, bf16[8,400,128]{2,1,0:T(8,128)(2,1)}, u32[]{:S(2)}, u32[]{:S(2)}) collective-permute-start(bf16[8,400,128]{2,1,0:T(8,128)(2,1)S(1)} %pack_far.1), channel_id=1, source_target_pairs={{0,16},{16,0},{32,48},{48,32},{64,80},{80,64},{96,112},{112,96},{1... | collective-permute-start | bytes 2457608 | tf_op jit(solution)/shard_map/ppermute | solution.py:427
  25.7 2.7 %collective-permute-start = (bf16[4,96,512]{2,1,0:T(8,128)(2,1)S(1)}, bf16[4,96,512]{2,1,0:T(8,128)(2,1)S(1)}, u32[]{:S(2)}, u32[]{:S(2)}) collective-permute-start(bf16[4,96,512]{2,1,0:T(8,128)(2,1)S(1)} %get-tuple-element.28), channel_id=1, source_target_pairs={{0,1},{1,0},{2,3},{3,2},{4,5},{5,4},{6,7},{7,6},{8,9},{9,8},{10,11... | collective-permute-start | bytes 1179656 | tf_op jit(solution)/shard_map/ppermute | solution.py:431
  27.0 1.9 %collective-permute-start.1 = (bf16[4,96,512]{2,1,0:T(8,128)(2,1)S(1)}, bf16[4,96,512]{2,1,0:T(8,128)(2,1)S(1)}, u32[]{:S(2)}, u32[]{:S(2)}) collective-permute-start(bf16[4,96,512]{2,1,0:T(8,128)(2,1)S(1)} %get-tuple-element.29), channel_id=1, source_target_pairs={{0,1},{1,0},{2,3},{3,2},{4,5},{5,4},{6,7},{7,6},{8,9},{9,8},{10,11... | collective-permute-start | bytes 1179656 | tf_op jit(solution)/shard_map/ppermute | solution.py:431
  28.9 13.1 %copy-start.1 = (bf16[2,48,512]{2,1,0:T(8,128)(2,1)S(1)}, bf16[2,48,512]{2,1,0:T(8,128)(2,1)}, u32[]{:S(2)}) copy-start(bf16[2,48,512]{2,1,0:T(8,128)(2,1)} %param.11) | copy-start | bytes 294916
  29.4 12.4 %collective-permute-start.2 = (bf16[2,96,512]{2,1,0:T(8,128)(2,1)S(1)}, bf16[2,96,512]{2,1,0:T(8,128)(2,1)S(1)}, u32[]{:S(2)}, u32[]{:S(2)}) collective-permute-start(bf16[2,96,512]{2,1,0:T(8,128)(2,1)S(1)} %get-tuple-element.31), channel_id=1, source_target_pairs={{0,4},{1,5},{2,6},{3,7},{4,0},{5,1},{6,2},{7,3},{8,12},{9,13},{10,... | collective-permute-start | bytes 589832 | tf_op jit(solution)/shard_map/ppermute | solution.py:433
  32.3 9.5 %collective-permute-start.5 = (bf16[2,96,512]{2,1,0:T(8,128)(2,1)S(1)}, bf16[2,96,512]{2,1,0:T(8,128)(2,1)S(1)}, u32[]{:S(2)}, u32[]{:S(2)}) collective-permute-start(bf16[2,96,512]{2,1,0:T(8,128)(2,1)S(1)} %get-tuple-element.34), channel_id=1, source_target_pairs={{0,6},{1,7},{2,0},{3,1},{4,2},{5,3},{6,4},{7,5},{8,14},{9,15},{10,... | collective-permute-start | bytes 589832 | tf_op jit(solution)/shard_map/ppermute | solution.py:433
  33.1 34.0 %copy-start.2 = (bf16[8192]{0:T(1024)(128)(2,1)S(1)}, bf16[8192]{0:T(1024)(128)(2,1)}, u32[]{:S(2)}) copy-start(bf16[8192]{0:T(1024)(128)(2,1)} %param.17) | copy-start | bytes 49156
  33.1 8.7 %collective-permute-start.4 = (bf16[2,96,512]{2,1,0:T(8,128)(2,1)S(1)}, bf16[2,96,512]{2,1,0:T(8,128)(2,1)S(1)}, u32[]{:S(2)}, u32[]{:S(2)}) collective-permute-start(bf16[2,96,512]{2,1,0:T(8,128)(2,1)S(1)} %get-tuple-element.33), channel_id=1, source_target_pairs={{0,2},{1,3},{2,4},{3,5},{4,6},{5,7},{6,0},{7,1},{8,10},{9,11},{10,... | collective-permute-start | bytes 589832 | tf_op jit(solution)/shard_map/ppermute | solution.py:433
  37.0 27.0 %all-to-all-start.1 = ((bf16[8,400,128]{2,1,0:T(8,128)(2,1)}), bf16[8,400,128]{2,1,0:T(8,128)(2,1)S(1)}, u32[]{:S(2)}, u32[]{:S(2)}) async-start(bf16[8,400,128]{2,1,0:T(8,128)(2,1)} %collective-permute-done.3), calls=%async_computation.1 | async-start | bytes 1638400 | tf_op jit(solution)/shard_map/all_to_all | solution.py:417
  42.0 4.6 %collective-permute-start.6 = (bf16[2,96,512]{2,1,0:T(8,128)(2,1)S(1)}, bf16[2,96,512]{2,1,0:T(8,128)(2,1)S(1)}, u32[]{:S(2)}, u32[]{:S(2)}) collective-permute-start(bf16[2,96,512]{2,1,0:T(8,128)(2,1)S(1)} %pad_maximum_fusion), channel_id=1, source_target_pairs={{0,8},{1,9},{2,10},{3,11},{4,12},{5,13},{6,14},{7,15},{8,0},{9,1},... | collective-permute-start | bytes 589832 | tf_op jit(solution)/shard_map/ppermute | solution.py:441
  43.3 15.5 %collective-permute-start.8 = (bf16[8,400,128]{2,1,0:T(8,128)(2,1)S(1)}, bf16[8,400,128]{2,1,0:T(8,128)(2,1)S(1)}, u32[]{:S(2)}, u32[]{:S(2)}) collective-permute-start(bf16[8,400,128]{2,1,0:T(8,128)(2,1)S(1)} %all-to-all-done.mine), channel_id=1, source_target_pairs={{0,1},{1,0},{2,3},{3,2},{4,5},{5,4},{6,7},{7,6},{8,9},{9,8},{10,11... | collective-permute-start | bytes 2457608 | tf_op jit(solution)/shard_map/ppermute | solution.py:451
  46.7 21.5 %copy-start = (bf16[1,96,512]{2,1,0:T(8,128)(2,1)}, bf16[1,96,512]{2,1,0:T(8,128)(2,1)S(1)}, u32[]{:S(2)}) copy-start(bf16[1,96,512]{2,1,0:T(8,128)(2,1)S(1)} %get-tuple-element.52) | copy-start | bytes 294916
  46.7 9.2 %collective-permute-start.10 = (bf16[2,96,512]{2,1,0:T(8,128)(2,1)S(1)}, bf16[2,96,512]{2,1,0:T(8,128)(2,1)S(1)}, u32[]{:S(2)}, u32[]{:S(2)}) collective-permute-start(bf16[2,96,512]{2,1,0:T(8,128)(2,1)S(1)} %pad_maximum_fusion.1.refs_0_), channel_id=1, source_target_pairs={{0,2},{1,3},{2,4},{3,5},{4,6},{5,7},{6,0},{7,1},{8,10},{9,11},{10,... | collective-permute-start | bytes 589832 | tf_op jit(solution)/shard_map/ppermute | solution.py:448
  48.3 12.1 %collective-permute-start.7 = (bf16[2,96,512]{2,1,0:T(8,128)(2,1)S(1)}, bf16[2,96,512]{2,1,0:T(8,128)(2,1)S(1)}, u32[]{:S(2)}, u32[]{:S(2)}) collective-permute-start(bf16[2,96,512]{2,1,0:T(8,128)(2,1)S(1)} %pad_maximum_fusion.1.refs_0_), channel_id=1, source_target_pairs={{0,4},{1,5},{2,6},{3,7},{4,0},{5,1},{6,2},{7,3},{8,12},{9,13},{10,... | collective-permute-start | bytes 589832 | tf_op jit(solution)/shard_map/ppermute | solution.py:448
  50.9 9.5 %collective-permute-start.12 = (bf16[2,96,512]{2,1,0:T(8,128)(2,1)S(1)}, bf16[2,96,512]{2,1,0:T(8,128)(2,1)S(1)}, u32[]{:S(2)}, u32[]{:S(2)}) collective-permute-start(bf16[2,96,512]{2,1,0:T(8,128)(2,1)S(1)} %pad_maximum_fusion.1.refs_0_), channel_id=1, source_target_pairs={{0,1},{1,0},{2,3},{3,2},{4,5},{5,4},{6,7},{7,6},{8,9},{9,8},{10,11... | collective-permute-start | bytes 589832 | tf_op jit(solution)/shard_map/ppermute | solution.py:453
  54.9 6.8 %collective-permute-start.9 = (bf16[2,96,512]{2,1,0:T(8,128)(2,1)S(1)}, bf16[2,96,512]{2,1,0:T(8,128)(2,1)S(1)}, u32[]{:S(2)}, u32[]{:S(2)}) collective-permute-start(bf16[2,96,512]{2,1,0:T(8,128)(2,1)S(1)} %pad_maximum_fusion.1.refs_0_), channel_id=1, source_target_pairs={{0,6},{1,7},{2,0},{3,1},{4,2},{5,3},{6,4},{7,5},{8,14},{9,15},{10,... | collective-permute-start | bytes 589832 | tf_op jit(solution)/shard_map/ppermute | solution.py:448
  56.0 5.7 %collective-permute-start.11 = (bf16[2,96,512]{2,1,0:T(8,128)(2,1)S(1)}, bf16[2,96,512]{2,1,0:T(8,128)(2,1)S(1)}, u32[]{:S(2)}, u32[]{:S(2)}) collective-permute-start(bf16[2,96,512]{2,1,0:T(8,128)(2,1)S(1)} %collective-permute-done.10.refs_3_), channel_id=1, source_target_pairs={{0,1},{1,0},{2,3},{3,2},{4,5},{5,4},{6,7},{7,6},{8,9},{9,8},{10,11... | collective-permute-start | bytes 589832 | tf_op jit(solution)/shard_map/ppermute | solution.py:453
  64.1 5.1 %collective-permute-start.13 = (bf16[8,400,128]{2,1,0:T(8,128)(2,1)S(1)}, bf16[8,400,128]{2,1,0:T(8,128)(2,1)S(1)}, u32[]{:S(2)}, u32[]{:S(2)}) collective-permute-start(bf16[8,400,128]{2,1,0:T(8,128)(2,1)S(1)} %all-to-all-done.1.src.far), channel_id=1, source_target_pairs={{0,1},{1,0},{2,3},{3,2},{4,5},{5,4},{6,7},{7,6},{8,9},{9,8},{10,11... | collective-permute-start | bytes 2457608 | tf_op jit(solution)/shard_map/ppermute | solution.py:455
  66.6 2.2 %collective-permute-start.14 = (bf16[2,96,512]{2,1,0:T(8,128)(2,1)S(1)}, bf16[2,96,512]{2,1,0:T(8,128)(2,1)S(1)}, u32[]{:S(2)}, u32[]{:S(2)}) collective-permute-start(bf16[2,96,512]{2,1,0:T(8,128)(2,1)S(1)} %collective-permute-done.9.refs_1_), channel_id=1, source_target_pairs={{0,1},{1,0},{2,3},{3,2},{4,5},{5,4},{6,7},{7,6},{8,9},{9,8},{10,11... | collective-permute-start | bytes 589832 | tf_op jit(solution)/shard_map/ppermute | solution.py:453
  66.6 2.5 %collective-permute-start.15 = (bf16[2,96,512]{2,1,0:T(8,128)(2,1)S(1)}, bf16[2,96,512]{2,1,0:T(8,128)(2,1)S(1)}, u32[]{:S(2)}, u32[]{:S(2)}) collective-permute-start(bf16[2,96,512]{2,1,0:T(8,128)(2,1)S(1)} %collective-permute-done.7.refs_2_), channel_id=1, source_target_pairs={{0,1},{1,0},{2,3},{3,2},{4,5},{5,4},{6,7},{7,6},{8,9},{9,8},{10,11... | collective-permute-start | bytes 589832 | tf_op jit(solution)/shard_map/ppermute | solution.py:453
